TPU v7x, 256 devices: a whole 4x4x8 slice. The times are simulated.
256 devices in a mesh: ctx: 32 (over z, x), tp: 8 (over y, core).
Axes of the slice: x: 4, y: 4, z: 8, core: 2. Of those that a mesh axis runs over, the one named last changes fastest.
Arguments:
- qkv: bfloat16 [16384, 3, 4096], P('ctx', None, 'tp'), may hold values from -6 to 6
- short_filter: float32 [7, 3, 4096], P(None, None, 'tp'), may hold values from -2.4 to 2.4
- long_filter: bfloat16 [128, 4096], P(None, 'tp'), may hold values from -0.5 to 0.5
- out_weight: bfloat16 [4096, 4096], P('tp'), may hold values from -0.125 to 0.125
- cotangent: bfloat16 [16384, 4096], P('ctx', 'tp'), may hold values from -6 to 6
- valid_len: int32 [32], P('ctx'), may hold values from 128 to 512, as said below
Outputs:
- mixed: bfloat16 [16384, 4096], P('ctx', 'tp')
- d_qkv: bfloat16 [16384, 3, 4096], P('ctx', None, 'tp')
- d_weight: float32 [4096, 4096], P('tp', 'ctx')
Inputs may be any that keep to these rules, and one draw needn't show every extreme that they name: `valid_len`: shards of even index are fully valid.
All inputs are finite; a program needn't handle non-finite values.
Results may differ from a plain program's by a relative error of at most 0.0058.
Values may be sent and summed in bfloat16 or wider, within the bound.
No kernel may reach another device: no remote copies, remote signals or barrier semaphores. Data moves between devices by JAX's collectives and lax.ppermute only.
A program may use at most 128 MiB of HBM per device.

v0:
```python
import jax
import jax.numpy as jnp
from jax import lax
from jax.sharding import PartitionSpec as P

SHORT = 7
LONG = 128


def from_behind(array, axis, by):
    count = lax.axis_size(axis)
    pairs = [(i, i + by) for i in range(count) if 0 <= i + by < count]
    return lax.ppermute(array, axis, pairs)


def band_table(causal):
    out_idx = jnp.arange(LONG)[:, None, None]
    in_idx = jnp.arange(2 * LONG)[None, :, None]
    tap_idx = jnp.arange(LONG)[None, None, :]
    if causal:
        return (out_idx + LONG - in_idx == tap_idx).astype(jnp.bfloat16)
    return (in_idx - out_idx == tap_idx).astype(jnp.bfloat16)


def banded(windows, filters, table):
    blocks, width, channels = windows.shape
    group = min(channels, 128)
    count = channels // group
    win_groups = windows.reshape(blocks, width, count, group).transpose(2, 0, 1, 3)
    filt_groups = filters.reshape(LONG, count, group).transpose(1, 0, 2)

    def apply_group(pair):
        window_part, filt_part = pair
        toeplitz = jnp.einsum(
            "ijl,lc->cij", table, filt_part, preferred_element_type=jnp.float32
        ).astype(jnp.bfloat16)
        return jnp.einsum("cij,bjc->bic", toeplitz, window_part, preferred_element_type=jnp.float32)

    result = lax.map(apply_group, (win_groups, filt_groups))
    return result.transpose(1, 2, 0, 3).reshape(blocks * LONG, channels)


def causal_conv(values, head_rows, filters):
    length, channels = values.shape
    blocks = length // LONG
    joined = jnp.concatenate([head_rows, values], axis=0)
    before = joined[:length].reshape(blocks, LONG, channels)
    windows = jnp.concatenate([before, values.reshape(blocks, LONG, channels)], axis=1)
    return banded(windows, filters, band_table(True))


def anti_conv(values, tail_rows, filters):
    length, channels = values.shape
    blocks = length // LONG
    joined = jnp.concatenate([values, tail_rows], axis=0)
    after_rows = joined[LONG:].reshape(blocks, LONG, channels)
    windows = jnp.concatenate([values.reshape(blocks, LONG, channels), after_rows], axis=1)
    return banded(windows, filters, band_table(False))


def local(qkv, short_filter, long_filter, out_weight, cotangent, valid_len):
    tok_rows = qkv.shape[0]
    live_mask = (jnp.arange(tok_rows) < valid_len[0]).astype(jnp.float32)[:, None]
    streams = qkv * live_mask[:, :, None].astype(jnp.bfloat16)
    rim_rows = from_behind(streams[tok_rows - (SHORT - 1) :], "ctx", 1)
    padded = jnp.concatenate([rim_rows, streams], axis=0).astype(jnp.float32)
    filtered = jnp.zeros(streams.shape, jnp.float32)
    for tap_index in range(SHORT):
        filtered = (
            filtered
            + short_filter[tap_index]
            * padded[SHORT - 1 - tap_index : SHORT - 1 - tap_index + tok_rows]
        )
    q_side, k_side, v_side = (filtered[:, 0], filtered[:, 1], filtered[:, 2])
    gated = (k_side * v_side).astype(jnp.bfloat16)
    head_rows = from_behind(gated[tok_rows - LONG :], "ctx", 1)
    conv_out = causal_conv(gated, head_rows, long_filter)
    mix_in = (live_mask * q_side * conv_out).astype(jnp.bfloat16)
    partial_out = jnp.dot(mix_in, out_weight, preferred_element_type=jnp.float32)
    mixed = lax.psum_scatter(partial_out, "tp", scatter_dimension=1, tiled=True).astype(
        jnp.bfloat16
    )
    cot_piece = lax.all_gather(cotangent, "tp", axis=1, tiled=True)
    d_acc = lax.dot_general(
        cot_piece, out_weight, (((1,), (1,)), ((), ())), preferred_element_type=jnp.float32
    )
    w_block = lax.dot_general(
        mix_in, cot_piece, (((0,), (0,)), ((), ())), preferred_element_type=jnp.float32
    )
    d_mix = live_mask * d_acc
    d_conv = (d_mix * q_side).astype(jnp.bfloat16)
    d_q = d_mix * conv_out
    tail_rows = from_behind(d_conv[:LONG], "ctx", -1)
    d_gated = anti_conv(d_conv, tail_rows, long_filter)
    d_filtered = jnp.stack([d_q, d_gated * v_side, d_gated * k_side], axis=1)
    next_rows = from_behind(d_filtered[: SHORT - 1].astype(jnp.bfloat16), "ctx", -1).astype(
        jnp.float32
    )
    padded_back = jnp.concatenate([d_filtered, next_rows], axis=0)
    summed = jnp.zeros(d_filtered.shape, jnp.float32)
    for tap_index in range(SHORT):
        summed = summed + short_filter[tap_index] * padded_back[tap_index : tap_index + tok_rows]
    d_qkv = (summed * live_mask[:, :, None]).astype(jnp.bfloat16)
    grad_scale = 1.0 / jnp.sqrt(jnp.float32(tok_rows * lax.axis_size("ctx")))
    d_weight = lax.psum_scatter(w_block * grad_scale, "ctx", scatter_dimension=1, tiled=True)
    return (mixed, d_qkv, d_weight)


def solution(mesh):
    in_specs = (
        P("ctx", None, "tp"),
        P(None, None, "tp"),
        P(None, "tp"),
        P("tp", None),
        P("ctx", "tp"),
        P("ctx"),
    )
    out_specs = (P("ctx", "tp"), P("ctx", None, "tp"), P("tp", "ctx"))
    return jax.shard_map(local, mesh=mesh, in_specs=in_specs, out_specs=out_specs, check_vma=False)
```

profile of v0, /device:TPU:102, one launch (start us, length us, event | category | flops | bytes accessed | tf_op | source)
XLA Modules:
  0.0 505.1 jit_solution(13005953080140934037)
XLA Ops:
  10.2 5.0 collective-permute-start
  19.8 26.6 %all-gather.2.cloned.1.call-done = bf16[512,4096]{1,0:T(8,128)(2,1)} async-done(((bf16[512,512]{1,0:T(8,128)(2,1)}), bf16[512,4096]{1,0:T(8,128)(2,1)}) %all-gather.2.cloned.1.call-update) | async-done | bytes 4194320 | tf_op jit(solution)/shard_map/all_gather | solution.py:83
  46.4 6.8 %multiply_convert_fusion = (bf16[512,512]{1,0:T(8,128)(2,1)S(1)}, f32[512,512]{1,0:T(8,128)}) fusion(f32[512,3,512]{2,0,1:T(8,128)S(1)} %fusion.38, bf16[512,4096]{1,0:T(8,128)(2,1)} %all-gather.2.cloned.1.call-done, bf16[512,4096]{1,0:T(8,128)(2,1)} %param.13, f32[512]{0:T(512)S(1)} %fusion.44), kind=kOutput, calls=%fused_computation.66 | convolution fusion | flops 2148270080 | bytes 11012096 | tf_op jit(solution)/shard_map/dot_general | solution.py:84
  58.8 6.0 %collective-permute-done.2 = bf16[128,512]{1,0:T(8,128)(2,1)S(1)} collective-permute-done((bf16[128,512]{1,0:T(8,128)(2,1)S(1)}, bf16[128,512]{1,0:T(8,128)(2,1)S(1)}, u32[]{:S(2)}, u32[]{:S(2)}) %collective-permute-start.2) | collective-permute-done | bytes 131104 | tf_op jit(solution)/shard_map/ppermute | solution.py:13
  67.2 57.6 %while.23 = (s32[]{:T(128)}, f32[4,4,128,128]{2,1,3,0:T(4,128)S(1)}, bf16[4,4,256,128]{2,1,3,0:T(4,128)(2,1)S(1)}, bf16[4,128,128]{2,1,0:T(8,128)(2,1)S(1)}, s32[128,256]{1,0:T(8,128)S(1)}, /*index=5*/s32[]{:T(128)}) while((s32[]{:T(128)}, f32[4,4,128,128]{2,1,3,0:T(4,128)S(1)}, bf16[4,4,256,128]{2,1,3,0:T(4,128)(2,1)S(1)}, ...), condition=%wide.region_4.5_spmd.clone, body=%wide.region_3.4_spmd.clone.sunk | while | flops 1115684864 | bytes 17466440 | solution.py:39
  67.2 9.8 %fusion.72 = bf16[128,128,256]{2,0,1:T(8,128)(2,1)S(1)} fusion(s32[128,256]{1,0:T(8,128)S(1)} %get-tuple-element.213, bf16[4,128,128]{2,1,0:T(8,128)(2,1)S(1)} %get-tuple-element.212, s32[]{:T(128)} %get-tuple-element.203), kind=kOutput, calls=%fused_computation.19.clone.1 | convolution fusion | flops 1082130432 | bytes 8552452 | tf_op jit(solution)/shard_map/while/body/eval_jaxpr/ijl,lc->cij/dot_general | solution.py:34
  77.0 4.6 fusion.73
  81.6 9.8 %fusion.72 = bf16[128,128,256]{2,0,1:T(8,128)(2,1)S(1)} fusion(s32[128,256]{1,0:T(8,128)S(1)} %get-tuple-element.213, bf16[4,128,128]{2,1,0:T(8,128)(2,1)S(1)} %get-tuple-element.212, s32[]{:T(128)} %get-tuple-element.203), kind=kOutput, calls=%fused_computation.19.clone.1 | convolution fusion | flops 1082130432 | bytes 8552452 | tf_op jit(solution)/shard_map/while/body/eval_jaxpr/ijl,lc->cij/dot_general | solution.py:34
  96.0 9.8 %fusion.72 = bf16[128,128,256]{2,0,1:T(8,128)(2,1)S(1)} fusion(s32[128,256]{1,0:T(8,128)S(1)} %get-tuple-element.213, bf16[4,128,128]{2,1,0:T(8,128)(2,1)S(1)} %get-tuple-element.212, s32[]{:T(128)} %get-tuple-element.203), kind=kOutput, calls=%fused_computation.19.clone.1 | convolution fusion | flops 1082130432 | bytes 8552452 | tf_op jit(solution)/shard_map/while/body/eval_jaxpr/ijl,lc->cij/dot_general | solution.py:34
  110.4 9.8 %fusion.72 = bf16[128,128,256]{2,0,1:T(8,128)(2,1)S(1)} fusion(s32[128,256]{1,0:T(8,128)S(1)} %get-tuple-element.213, bf16[4,128,128]{2,1,0:T(8,128)(2,1)S(1)} %get-tuple-element.212, s32[]{:T(128)} %get-tuple-element.203), kind=kOutput, calls=%fused_computation.19.clone.1 | convolution fusion | flops 1082130432 | bytes 8552452 | tf_op jit(solution)/shard_map/while/body/eval_jaxpr/ijl,lc->cij/dot_general | solution.py:34
  140.7 60.1 %while.22 = (s32[]{:T(128)}, f32[4,4,128,128]{2,1,3,0:T(4,128)}, bf16[4,4,256,128]{2,1,3,0:T(4,128)(2,1)S(1)}, bf16[4,128,128]{2,1,0:T(8,128)(2,1)S(1)}, s32[128,256]{1,0:T(8,128)S(1)}, /*index=5*/s32[]{:T(128)}) while((s32[]{:T(128)}, f32[4,4,128,128]{2,1,3,0:T(4,128)}, bf16[4,4,256,128]{2,1,3,0:T(4,128)(2,1)S(1)}, ...), condition=%wide.region_1.2_spmd.clone, body=%wide.region_0.1_spmd.clone.sunk | while | flops 1115684864 | bytes 17466440 | solution.py:39
  140.7 9.8 %fusion.67 = bf16[128,128,256]{2,0,1:T(8,128)(2,1)S(1)} fusion(s32[128,256]{1,0:T(8,128)S(1)} %get-tuple-element.231, bf16[4,128,128]{2,1,0:T(8,128)(2,1)S(1)} %get-tuple-element.230, s32[]{:T(128)} %get-tuple-element.221), kind=kOutput, calls=%fused_computation.5.clone.1 | convolution fusion | flops 1082130432 | bytes 8552452 | tf_op jit(solution)/shard_map/while/body/eval_jaxpr/ijl,lc->cij/dot_general | solution.py:34
  150.5 5.3 %fusion.68 = f32[4,4,128,128]{2,1,3,0:T(4,128)} fusion(f32[4,4,128,128]{2,1,3,0:T(4,128)} %get-tuple-element.222, s32[]{:T(128)} %get-tuple-element.221, bf16[128,128,256]{2,0,1:T(8,128)(2,1)S(1)} %fusion.67, bf16[4,4,256,128]{2,1,3,0:T(4,128)(2,1)S(1)} %get-tuple-element.229), kind=kOutput, calls=%fused_computation.9.clone.1 | convolution fusion | flops 33554432 | bytes 8913920 | tf_op jit(solution)/shard_map/while/body/eval_jaxpr/cij,bjc->bic/dot_general | solution.py:37
  155.8 9.8 %fusion.67 = bf16[128,128,256]{2,0,1:T(8,128)(2,1)S(1)} fusion(s32[128,256]{1,0:T(8,128)S(1)} %get-tuple-element.231, bf16[4,128,128]{2,1,0:T(8,128)(2,1)S(1)} %get-tuple-element.230, s32[]{:T(128)} %get-tuple-element.221), kind=kOutput, calls=%fused_computation.5.clone.1 | convolution fusion | flops 1082130432 | bytes 8552452 | tf_op jit(solution)/shard_map/while/body/eval_jaxpr/ijl,lc->cij/dot_general | solution.py:34
  165.5 5.3 %fusion.68 = f32[4,4,128,128]{2,1,3,0:T(4,128)} fusion(f32[4,4,128,128]{2,1,3,0:T(4,128)} %get-tuple-element.222, s32[]{:T(128)} %get-tuple-element.221, bf16[128,128,256]{2,0,1:T(8,128)(2,1)S(1)} %fusion.67, bf16[4,4,256,128]{2,1,3,0:T(4,128)(2,1)S(1)} %get-tuple-element.229), kind=kOutput, calls=%fused_computation.9.clone.1 | convolution fusion | flops 33554432 | bytes 8913920 | tf_op jit(solution)/shard_map/while/body/eval_jaxpr/cij,bjc->bic/dot_general | solution.py:37
  170.8 9.8 %fusion.67 = bf16[128,128,256]{2,0,1:T(8,128)(2,1)S(1)} fusion(s32[128,256]{1,0:T(8,128)S(1)} %get-tuple-element.231, bf16[4,128,128]{2,1,0:T(8,128)(2,1)S(1)} %get-tuple-element.230, s32[]{:T(128)} %get-tuple-element.221), kind=kOutput, calls=%fused_computation.5.clone.1 | convolution fusion | flops 1082130432 | bytes 8552452 | tf_op jit(solution)/shard_map/while/body/eval_jaxpr/ijl,lc->cij/dot_general | solution.py:34
  180.5 5.2 %fusion.68 = f32[4,4,128,128]{2,1,3,0:T(4,128)} fusion(f32[4,4,128,128]{2,1,3,0:T(4,128)} %get-tuple-element.222, s32[]{:T(128)} %get-tuple-element.221, bf16[128,128,256]{2,0,1:T(8,128)(2,1)S(1)} %fusion.67, bf16[4,4,256,128]{2,1,3,0:T(4,128)(2,1)S(1)} %get-tuple-element.229), kind=kOutput, calls=%fused_computation.9.clone.1 | convolution fusion | flops 33554432 | bytes 8913920 | tf_op jit(solution)/shard_map/while/body/eval_jaxpr/cij,bjc->bic/dot_general | solution.py:37
  185.8 9.8 %fusion.67 = bf16[128,128,256]{2,0,1:T(8,128)(2,1)S(1)} fusion(s32[128,256]{1,0:T(8,128)S(1)} %get-tuple-element.231, bf16[4,128,128]{2,1,0:T(8,128)(2,1)S(1)} %get-tuple-element.230, s32[]{:T(128)} %get-tuple-element.221), kind=kOutput, calls=%fused_computation.5.clone.1 | convolution fusion | flops 1082130432 | bytes 8552452 | tf_op jit(solution)/shard_map/while/body/eval_jaxpr/ijl,lc->cij/dot_general | solution.py:34
  195.5 5.3 %fusion.68 = f32[4,4,128,128]{2,1,3,0:T(4,128)} fusion(f32[4,4,128,128]{2,1,3,0:T(4,128)} %get-tuple-element.222, s32[]{:T(128)} %get-tuple-element.221, bf16[128,128,256]{2,0,1:T(8,128)(2,1)S(1)} %fusion.67, bf16[4,4,256,128]{2,1,3,0:T(4,128)(2,1)S(1)} %get-tuple-element.229), kind=kOutput, calls=%fused_computation.9.clone.1 | convolution fusion | flops 33554432 | bytes 8913920 | tf_op jit(solution)/shard_map/while/body/eval_jaxpr/cij,bjc->bic/dot_general | solution.py:37
  206.6 5.6 %fusion.47 = f32[512,4096]{1,0:T(8,128)} fusion(bf16[512,512]{1,0:T(8,128)(2,1)S(1)} %get-tuple-element.119, bf16[512,4096]{1,0:T(8,128)(2,1)S(1)} %copy-done.2), kind=kOutput, calls=%fused_computation.91 | convolution fusion | flops 2147483648 | bytes 13107200 | tf_op jit(solution)/shard_map/dot_general | solution.py:79
  212.3 8.0 %convolution_multiply_fusion = f32[512,4096]{1,0:T(8,128)} fusion(bf16[512,512]{1,0:T(8,128)(2,1)} %copy-done.1, bf16[512,4096]{1,0:T(8,128)(2,1)} %all-gather.2.cloned.1.call-done), kind=kOutput, calls=%fused_computation.30 | convolution fusion | flops 2149580800 | bytes 13107200 | tf_op jit(solution)/shard_map/dot_general | solution.py:87
  222.6 7.1 %collective-permute-done.3 = bf16[6,3,512]{2,0,1:T(8,128)(2,1)S(1)} collective-permute-done((bf16[6,3,512]{2,0,1:T(8,128)(2,1)S(1)}, bf16[6,3,512]{2,0,1:T(8,128)(2,1)S(1)}, u32[]{:S(2)}, u32[]{:S(2)}) %collective-permute-start.3) | collective-permute-done | bytes 18464 | tf_op jit(solution)/shard_map/ppermute | solution.py:13
  234.3 31.6 %reduce-scatter.3.cloned.1.call-done = f32[512,512]{1,0:T(8,128)} async-done(((f32[512,4096]{1,0:T(8,128)}), f32[512,512]{1,0:T(8,128)}) %reduce-scatter.3.cloned.1.call-update) | async-done | bytes 1048592 | tf_op jit(solution)/shard_map/reduce_scatter | solution.py:80
  267.9 230.7 %reduce-scatter.5.cloned.1.call-done = f32[512,128]{1,0:T(8,128)} async-done(((f32[512,4096]{1,0:T(8,128)}), f32[512,128]{1,0:T(8,128)}) %reduce-scatter.5.cloned.1.call-update) | async-done | bytes 262160 | tf_op jit(solution)/shard_map/reduce_scatter | solution.py:105
  (94 shorter events, 59.1 us)
Async XLA Ops:
  7.2 8.0 %copy-start.15 = (f32[7,3,512]{2,0,1:T(8,128)S(1)}, f32[7,3,512]{2,0,1:T(8,128)}, u32[]{:S(2)}) copy-start(f32[7,3,512]{2,0,1:T(8,128)} %param.11) | copy-start | bytes 129028
  7.2 39.2 %all-gather.2.cloned.1.call-start = ((), (), s32[]{:S(2)}) async-start(), calls=%async_computation.3 | async-start | bytes 4718592 | tf_op jit(solution)/shard_map/all_gather | solution.py:83
  7.9 257.9 %reduce-scatter.3.cloned.1.call-start = ((), (), s32[]{:S(2)}) async-start(), calls=%async_computation.2 | async-start | bytes 9437184 | tf_op jit(solution)/shard_map/reduce_scatter | solution.py:80
  10.2 6.5 %collective-permute-start = (bf16[6,3,512]{2,0,1:T(8,128)(2,1)S(1)}, bf16[6,3,512]{2,0,1:T(8,128)(2,1)S(1)}, u32[]{:S(2)}, u32[]{:S(2)}) collective-permute-start(bf16[6,3,512]{2,0,1:T(8,128)(2,1)S(1)} %slice.128), channel_id=1, source_target_pairs={{0,8},{8,16},{16,24},{24,32},{32,40},{40,48},{48,56},{56,64},{64,7... | collective-permute-start | bytes 55304 | tf_op jit(solution)/shard_map/ppermute | solution.py:13
  15.3 1.9 copy-start.5
  15.3 1.9 copy-start.7
  15.3 1.9 copy-start.9
  15.3 1.9 copy-start.11
  15.3 31.1 %copy-start.16 = (f32[512]{0:T(512)}, f32[512]{0:T(512)S(1)}, u32[]{:S(2)}) copy-start(f32[512]{0:T(512)S(1)} %fusion.44) | copy-start | bytes 6148
  15.3 1.9 copy-start.13
  19.8 33.4 %copy-start = (f32[512,3,512]{2,0,1:T(8,128)}, f32[512,3,512]{2,0,1:T(8,128)S(1)}, u32[]{:S(2)}) copy-start(f32[512,3,512]{2,0,1:T(8,128)S(1)} %fusion.38) | copy-start | bytes 9437188
  19.8 37.1 %copy-start.4 = (bf16[128,512]{1,0:T(8,128)(2,1)S(1)}, bf16[128,512]{1,0:T(8,128)(2,1)}, u32[]{:S(2)}) copy-start(bf16[128,512]{1,0:T(8,128)(2,1)} %param.12) | copy-start | bytes 393220
  53.2 0.8 copy-start.3
  54.0 10.9 %collective-permute-start.2 = (bf16[128,512]{1,0:T(8,128)(2,1)S(1)}, bf16[128,512]{1,0:T(8,128)(2,1)S(1)}, u32[]{:S(2)}, u32[]{:S(2)}) collective-permute-start(bf16[128,512]{1,0:T(8,128)(2,1)S(1)} %slice.140), channel_id=1, source_target_pairs={{8,0},{16,8},{24,16},{32,24},{40,32},{48,40},{56,48},{64,56},{72,6... | collective-permute-start | bytes 393224 | tf_op jit(solution)/shard_map/ppermute | solution.py:13
  129.5 7.1 %collective-permute-start.1 = (bf16[128,512]{1,0:T(8,128)(2,1)}, bf16[128,512]{1,0:T(8,128)(2,1)S(1)}, u32[]{:S(2)}, u32[]{:S(2)}) collective-permute-start(bf16[128,512]{1,0:T(8,128)(2,1)} %slice_bitcast_fusion.1), channel_id=1, source_target_pairs={{0,8},{8,16},{16,24},{24,32},{32,40},{40,48},{48,56},{56,64},{64,7... | collective-permute-start | bytes 393224 | tf_op jit(solution)/shard_map/ppermute | solution.py:13
  200.8 2.6 copy-start.17
  203.4 3.1 copy-start.2
  205.6 0.8 copy-start.1
  212.2 286.4 %reduce-scatter.5.cloned.1.call-start = ((), (), s32[]{:S(2)}) async-start(), calls=%async_computation.4 | async-start | bytes 8650752 | tf_op jit(solution)/shard_map/reduce_scatter | solution.py:105
  220.6 9.0 %collective-permute-start.3 = (bf16[6,3,512]{2,0,1:T(8,128)(2,1)S(1)}, bf16[6,3,512]{2,0,1:T(8,128)(2,1)S(1)}, u32[]{:S(2)}, u32[]{:S(2)}) collective-permute-start(bf16[6,3,512]{2,0,1:T(8,128)(2,1)S(1)} %slice.222), channel_id=1, source_target_pairs={{8,0},{16,8},{24,16},{32,24},{40,32},{48,40},{56,48},{64,56},{72,6... | collective-permute-start | bytes 55304 | tf_op jit(solution)/shard_map/ppermute | solution.py:13
  229.7 0.7 copy-start.8
  229.7 0.7 copy-start.10
  229.7 0.7 copy-start.12
  229.7 0.7 copy-start.14
  (1 other events, 0.7 us)
Sparse Core Ops, SparseCore 0:
  9.8 36.4 all-gather.1
  212.3 53.4 reduce-scatter.2
  270.4 228.0 reduce-scatter.4
where the time goes:
time: 508 us; the launch traced here: 505 us
  waiting for transfers between devices  307 us (60%)
  matrix products  138 us (27%)
  other arithmetic  19.2 us (4%)
  between operations  14.8 us (3%)
  local copies, waits for them, and re-layouts  13.4 us (3%)
  starting transfers between devices  12.1 us (2%)
    reduce_scatter x1, waiting for transfers between devices, local(): lax.psum_scatter(w_block * grad_scale, 'ctx', scatter_dimension=1, tiled=...  231 us
    dot_general x8, matrix products, apply_group(): jnp.einsum('ijl,lc->cij', table, filt_part, preferred_element_type=jnp.fl...  78.1 us
    dot_general x8, matrix products, apply_group(): jnp.einsum('cij,bjc->bic', toeplitz, window_part, preferred_element_type=...  39.5 us
    reduce_scatter x1, waiting for transfers between devices, local(): lax.psum_scatter(partial_out, 'tp', scatter_dimension=1, tiled=True)  31.6 us
    all_gather x1, waiting for transfers between devices, local(): cot_piece = lax.all_gather(cotangent, 'tp', axis=1, tiled=True)  26.6 us
    ppermute x4, waiting for transfers between devices, from_behind(): return lax.ppermute(array, axis, pairs)  18 us
    ppermute x4, starting transfers between devices, from_behind(): return lax.ppermute(array, axis, pairs)  11.9 us
  transfers between devices with their start and end apart: 7, of which 7 were waited for; matrix products, arithmetic and copies ran while one was open for 4% of the time, Pallas kernels for 0%

commit v1 on v0

v1 whole, which is shorter than its diff:
```python
import functools

import jax
import jax.numpy as jnp
import ml_dtypes
import numpy as np
from jax import lax
from jax.experimental import pallas as pl
from jax.experimental.pallas import tpu as pltpu
from jax.sharding import PartitionSpec as P

SHORT = 7
LONG = 128
ROWS = 512
CH = 512
LANES = 128
TAIL = 144
RIM = 16
STEP = 64
NZ, NX, NY = 8, 4, 4
F32, BF16 = jnp.float32, jnp.bfloat16


def split_bf16(table):
    high = table.astype(ml_dtypes.bfloat16)
    low = (table - high.astype(np.float64)).astype(ml_dtypes.bfloat16)
    return high, low


def tables():
    size = 2 * LONG
    freq = np.arange(LONG)[:, None]
    angle = 2.0 * np.pi * freq * np.arange(size)[None, :] / size
    real = np.concatenate([np.cos(angle), np.sin(angle)], axis=0)
    real[LONG] = (-1.0) ** np.arange(size)
    high, low = split_bf16(real[:, :LONG])
    forward = np.concatenate([high, low], axis=1)
    weight = np.full((2 * LONG, 1), 2.0 / size)
    weight[0] = weight[LONG] = 1.0 / size
    inverse = (real * weight).T
    causal = np.concatenate(split_bf16(inverse[LONG:]), axis=0)
    anti = np.concatenate(split_bf16(inverse[:LONG]), axis=0)
    return forward, causal, anti


def signs(rows):
    row = lax.broadcasted_iota(jnp.int32, (rows, LANES), 0)
    return jnp.where(row % 2 == 0, 1.0, -1.0).astype(F32)


def spectrum(forward, block):
    return jnp.dot(forward, jnp.concatenate([block, block], axis=0), preferred_element_type=F32)


def filter_spectrum(forward, taps):
    both = spectrum(forward, taps)
    cos_part, sin_part = both[:LONG], both[LONG:]
    first = lax.broadcasted_iota(jnp.int32, (LONG, LANES), 0) == 0
    return cos_part, jnp.where(first, 0.0, sin_part), jnp.where(first, sin_part, cos_part)


def back(table, product):
    high = product.astype(BF16)
    low = (product - high.astype(F32)).astype(BF16)
    half = table.shape[0] // 2
    both = jnp.dot(table, high, preferred_element_type=F32)
    rest = jnp.dot(table[:half], low, preferred_element_type=F32)
    return both[:half] + both[half:] + rest


def live_rows(valid, start, rows):
    row = lax.broadcasted_iota(jnp.int32, (rows, LANES), 0) + start
    return jnp.where(row < valid, 1.0, 0.0).astype(F32)


def forward_kernel(
    valid_ref, qkv_ref, halo_ref, short_ref, long_ref, fwd_ref, inv_ref,
    mix_ref, q_ref, k_ref, v_ref, conv_ref, ext_ref, gate_ref,
):
    valid = valid_ref[0]
    ext_ref[0, TAIL - RIM : TAIL] = halo_ref[0:RIM].astype(F32)
    ext_ref[1, 0:TAIL] = halo_ref[RIM : RIM + TAIL].astype(F32)
    ext_ref[2, 0:TAIL] = halo_ref[RIM + TAIL : RIM + 2 * TAIL].astype(F32)
    for start in range(0, ROWS, STEP):
        live = live_rows(valid, start, STEP)
        for stream in range(3):
            ext_ref[stream, TAIL + start : TAIL + start + STEP] = (
                qkv_ref[stream, start : start + STEP].astype(F32) * live
            )

    def filtered(stream, start):
        total = short_ref[stream, 0:1] * ext_ref[stream, start : start + STEP]
        for tap in range(1, SHORT):
            total += short_ref[stream, tap : tap + 1] * ext_ref[stream, start - tap : start - tap + STEP]
        return total

    for start in range(-LONG, ROWS, STEP):
        k_side = filtered(1, TAIL + start)
        v_side = filtered(2, TAIL + start)
        if start >= 0:
            k_ref[start : start + STEP] = k_side
            v_ref[start : start + STEP] = v_side
            q_ref[start : start + STEP] = filtered(0, TAIL + start)
        gate_ref[LONG + start : LONG + start + STEP] = (k_side * v_side).astype(BF16)

    fwd = fwd_ref[...]
    inv = inv_ref[...]
    cos_h, sin_h, alt_h = filter_spectrum(fwd, long_ref[...])
    sign = signs(2 * LONG)
    before = spectrum(fwd, gate_ref[0:LONG])
    for block in range(ROWS // LONG):
        start = block * LONG
        now = spectrum(fwd, gate_ref[LONG + start : 2 * LONG + start])
        window = before + sign * now
        before = now
        cos_x, sin_x = window[:LONG], window[LONG:]
        product = jnp.concatenate(
            [cos_x * cos_h - sin_x * sin_h, cos_x * sin_h + sin_x * alt_h], axis=0
        )
        conv = back(inv, product)
        conv_ref[start : start + LONG] = conv
        live = live_rows(valid, start, LONG)
        mix_ref[start : start + LONG] = (live * q_ref[start : start + LONG] * conv).astype(BF16)


def backward_kernel(
    valid_ref, dconv_ref, msg_ref, dq_ref, k_ref, v_ref, short_ref, long_ref, fwd_ref, inv_ref,
    out_ref, ext_ref, gate_ref,
):
    valid = valid_ref[0]
    fwd = fwd_ref[...]
    inv = inv_ref[...]
    gate_ref[0:TAIL] = msg_ref[0:TAIL]
    gate_ref[TAIL : 2 * LONG] = jnp.zeros((2 * LONG - TAIL, LANES), BF16)
    cos_h, sin_h, alt_h = filter_spectrum(fwd, long_ref[...])
    sign = signs(2 * LONG)
    blocks = ROWS // LONG
    ext_ref[0, 0:ROWS] = dq_ref[...]
    ext_ref[0, ROWS : ROWS + RIM] = msg_ref[TAIL : TAIL + RIM].astype(F32)
    now = spectrum(fwd, dconv_ref[0:LONG])
    for block in range(blocks + 1):
        start = block * LONG
        if block + 1 < blocks:
            after = spectrum(fwd, dconv_ref[start + LONG : start + 2 * LONG])
        else:
            rim = (block + 1 - blocks) * LONG
            after = spectrum(fwd, gate_ref[rim : rim + LONG])
        window = now + sign * after
        now = after
        cos_x, sin_x = window[:LONG], window[LONG:]
        product = jnp.concatenate(
            [cos_x * cos_h + sin_x * sin_h, sin_x * alt_h - cos_x * sin_h], axis=0
        )
        gated = back(inv, product)
        if block < blocks:
            ext_ref[1, start : start + LONG] = gated * v_ref[start : start + LONG]
            ext_ref[2, start : start + LONG] = gated * k_ref[start : start + LONG]
        else:
            rim = gated[:RIM]
            v_rim = msg_ref[TAIL + RIM : TAIL + 2 * RIM].astype(F32)
            k_rim = msg_ref[TAIL + 2 * RIM : TAIL + 3 * RIM].astype(F32)
            ext_ref[1, ROWS : ROWS + RIM] = rim * v_rim
            ext_ref[2, ROWS : ROWS + RIM] = rim * k_rim
    for start in range(0, ROWS, STEP):
        live = live_rows(valid, start, STEP)
        for stream in range(3):
            total = short_ref[stream, 0:1] * ext_ref[stream, start : start + STEP]
            for tap in range(1, SHORT):
                total += short_ref[stream, tap : tap + 1] * ext_ref[stream, start + tap : start + tap + STEP]
            out_ref[stream, start : start + STEP] = (total * live).astype(BF16)


def params(mib=40):
    return pltpu.CompilerParams(vmem_limit_bytes=mib * 2**20)


def cost(flops, moved):
    return pl.CostEstimate(flops=flops, bytes_accessed=moved, transcendentals=0)


SMEM = pl.BlockSpec(memory_space=pltpu.SMEM)
VMEM = pl.BlockSpec(memory_space=pltpu.VMEM)


def lane_spec(*lead):
    return pl.BlockSpec(lead + (LANES,), lambda i: (0,) * len(lead) + (i,))


def whole(*shape):
    return pl.BlockSpec(shape, lambda i: (0,) * len(shape))


def run_forward(valid, streams, halo, short, long_taps, fwd, inv):
    side = jax.ShapeDtypeStruct((ROWS, CH), F32)
    return pl.pallas_call(
        forward_kernel,
        grid=(CH // LANES,),
        in_specs=[
            SMEM, lane_spec(3, ROWS), lane_spec(RIM + 2 * TAIL), lane_spec(3, SHORT), lane_spec(LONG),
            whole(2 * LONG, 2 * LONG), whole(2 * LONG, 2 * LONG),
        ],
        out_specs=[lane_spec(ROWS)] * 5,
        out_shape=[jax.ShapeDtypeStruct((ROWS, CH), BF16), side, side, side, side],
        scratch_shapes=[
            pltpu.VMEM((3, TAIL + ROWS, LANES), F32),
            pltpu.VMEM((LONG + ROWS, LANES), BF16),
        ],
        compiler_params=params(),
        cost_estimate=cost(5_000_000_000, 7_000_000),
        name="forward",
    )(valid, streams, halo, short, long_taps, fwd, inv)


def run_backward(valid, d_conv, msg, d_q, k_side, v_side, short, long_taps, fwd, inv):
    return pl.pallas_call(
        backward_kernel,
        grid=(CH // LANES,),
        in_specs=[
            SMEM, lane_spec(ROWS), lane_spec(TAIL + 3 * RIM), lane_spec(ROWS), lane_spec(ROWS),
            lane_spec(ROWS), lane_spec(3, SHORT), lane_spec(LONG),
            whole(2 * LONG, 2 * LONG), whole(2 * LONG, 2 * LONG),
        ],
        out_specs=lane_spec(3, ROWS),
        out_shape=jax.ShapeDtypeStruct((3, ROWS, CH), BF16),
        scratch_shapes=[
            pltpu.VMEM((3, ROWS + RIM, LANES), F32),
            pltpu.VMEM((2 * LONG, LANES), BF16),
        ],
        compiler_params=params(),
        cost_estimate=cost(5_000_000_000, 7_000_000),
        name="backward",
    )(valid, d_conv, msg, d_q, k_side, v_side, short, long_taps, fwd, inv)


def project_kernel(order_ref, mix_ref, weight_ref, out_ref):
    out_ref[0] = jnp.dot(mix_ref[...], weight_ref[...], preferred_element_type=F32).astype(BF16)


def run_project(order, mix_in, weight):
    count = order.shape[0]
    return pl.pallas_call(
        project_kernel,
        grid_spec=pltpu.PrefetchScalarGridSpec(
            num_scalar_prefetch=1,
            grid=(count,),
            in_specs=[
                pl.BlockSpec((ROWS, CH), lambda i, order: (0, 0)),
                pl.BlockSpec((CH, CH), lambda i, order: (0, order[i])),
            ],
            out_specs=pl.BlockSpec((1, ROWS, CH), lambda i, order: (i, 0, 0)),
        ),
        out_shape=jax.ShapeDtypeStruct((count, ROWS, CH), BF16),
        compiler_params=params(),
        cost_estimate=cost(2 * count * ROWS * CH * CH, 4_500_000),
        name="project",
    )(order, mix_in, weight)


def project_add_kernel(order_ref, mix_ref, weight_ref, other_ref, one_ref, two_ref, three_ref, own_ref):
    step = pl.program_id(0)
    total = jnp.dot(mix_ref[...], weight_ref[...], preferred_element_type=F32)
    total += other_ref[0].astype(F32)
    for place, ref in enumerate((one_ref, two_ref, three_ref, own_ref)):

        @pl.when(step == place)
        def _(ref=ref):
            ref[...] = total.astype(ref.dtype)


def run_project_add(order, mix_in, weight, other):
    piece = jax.ShapeDtypeStruct((ROWS, CH), BF16)
    fixed = pl.BlockSpec((ROWS, CH), lambda i, order: (0, 0))
    return pl.pallas_call(
        project_add_kernel,
        grid_spec=pltpu.PrefetchScalarGridSpec(
            num_scalar_prefetch=1,
            grid=(4,),
            in_specs=[
                fixed,
                pl.BlockSpec((CH, CH), lambda i, order: (0, order[i])),
                pl.BlockSpec((1, ROWS, CH), lambda i, order: (i, 0, 0)),
            ],
            out_specs=[fixed] * 4,
        ),
        out_shape=[piece, piece, piece, jax.ShapeDtypeStruct((ROWS, CH), F32)],
        compiler_params=params(),
        cost_estimate=cost(8 * ROWS * CH * CH, 7_000_000),
        name="project_add",
    )(order, mix_in, weight, other)


def outer_kernel(count, place_ref, mix_ref, *refs):
    pieces, (own_ref, one_ref, two_ref, three_ref, work_ref) = refs[:count], refs[count:]
    mine = place_ref[0]
    mix_in = mix_ref[...]
    for slot, piece in enumerate(pieces):
        work_ref[...] = lax.dot_general(
            mix_in, piece[...], (((0,), (0,)), ((), ())), preferred_element_type=F32
        )
        for ahead, ref in enumerate((own_ref, one_ref, two_ref, three_ref)):
            column = pl.multiple_of(lax.rem(mine + ahead, NX) * LANES, LANES)
            ref[slot] = work_ref[:, pl.ds(column, LANES)].astype(ref.dtype)


def run_outer(place, mix_in, pieces):
    count = len(pieces)
    sent = jax.ShapeDtypeStruct((count, CH, LANES), BF16)
    return pl.pallas_call(
        functools.partial(outer_kernel, count),
        in_specs=[SMEM, VMEM] + [VMEM] * count,
        out_specs=[VMEM] * 4,
        out_shape=[jax.ShapeDtypeStruct((count, CH, LANES), F32), sent, sent, sent],
        scratch_shapes=[pltpu.VMEM((CH, CH), F32)],
        compiler_params=params(),
        cost_estimate=cost(2 * count * ROWS * CH * CH, 1_300_000 * count),
        name="outer",
    )(place, mix_in, *pieces)


def gather_x_kernel(counts, offset_ref, *refs):
    inputs, outputs, work_ref = refs[: 4 * len(counts)], refs[4 * len(counts) : -1], refs[-1]
    slab = 0
    for group, count in enumerate(counts):
        own, one, two, three = inputs[4 * group : 4 * group + 4]
        for slot in range(count):
            total = own[slot] + one[slot].astype(F32) + two[slot].astype(F32) + three[slot].astype(F32)
            work_ref[offset_ref[slab]] = total
            slab += 1
    for ahead, ref in enumerate(outputs):
        ref[...] = work_ref[ahead].astype(ref.dtype)


def run_gather_x(offsets, groups):
    counts = [group[0].shape[0] for group in groups]
    sent = jax.ShapeDtypeStruct((CH, LANES), BF16)
    return pl.pallas_call(
        functools.partial(gather_x_kernel, counts),
        in_specs=[SMEM] + [VMEM] * (4 * len(groups)),
        out_specs=[VMEM] * NZ,
        out_shape=[jax.ShapeDtypeStruct((CH, LANES), F32)] + [sent] * (NZ - 1),
        scratch_shapes=[pltpu.VMEM((NZ, CH, LANES), F32)],
        compiler_params=params(),
        cost_estimate=cost(4_000_000, 6_500_000),
        name="gather_x",
    )(offsets, *[array for group in groups for array in group])


def d_mix_kernel(count, last, info_ref, weight_ref, *refs):
    pieces, rest = refs[:count], refs[count:]
    total = None
    for slot, piece in enumerate(pieces):
        column = pl.multiple_of(info_ref[1 + slot] * CH, CH)
        part = lax.dot_general(
            piece[...], weight_ref[:, pl.ds(column, CH)], (((1,), (1,)), ((), ())),
            preferred_element_type=F32,
        )
        total = part if total is None else total + part
    if not last:
        rest[0][...] = total
        return
    acc_ref, q_ref, k_ref, v_ref, conv_ref, dconv_ref, dq_ref, msg_ref = rest
    row = lax.broadcasted_iota(jnp.int32, (ROWS, CH), 0)
    d_mix = jnp.where(row < info_ref[0], total + acc_ref[...], 0.0)
    d_conv = (d_mix * q_ref[...]).astype(BF16)
    d_q = d_mix * conv_ref[...]
    dconv_ref[...] = d_conv
    dq_ref[...] = d_q
    msg_ref[0:TAIL] = d_conv[:TAIL]
    msg_ref[TAIL : TAIL + RIM] = d_q[:RIM].astype(BF16)
    msg_ref[TAIL + RIM : TAIL + 2 * RIM] = v_ref[0:RIM].astype(BF16)
    msg_ref[TAIL + 2 * RIM : TAIL + 3 * RIM] = k_ref[0:RIM].astype(BF16)


def run_d_mix(info, weight, pieces, extra=()):
    count = len(pieces)
    full = jax.ShapeDtypeStruct((ROWS, CH), F32)
    if extra:
        shapes = [
            jax.ShapeDtypeStruct((ROWS, CH), BF16), full,
            jax.ShapeDtypeStruct((TAIL + 3 * RIM, CH), BF16),
        ]
    else:
        shapes = [full]
    return pl.pallas_call(
        functools.partial(d_mix_kernel, count, bool(extra)),
        in_specs=[SMEM, VMEM] + [VMEM] * (count + len(extra)),
        out_specs=[VMEM] * len(shapes),
        out_shape=shapes,
        compiler_params=params(),
        cost_estimate=cost(2 * count * ROWS * CH * CH, 8_000_000),
        name="d_mix",
    )(info, weight, *pieces, *extra)


def ctx_pairs(ahead_z, ahead_x):
    return [
        (z * NX + x, (z + ahead_z) % NZ * NX + (x + ahead_x) % NX) for z in range(NZ) for x in range(NX)
    ]


def along_x(array, ahead):
    return lax.ppermute(array, "ctx", ctx_pairs(0, ahead))


def along_z(array, ahead):
    return lax.ppermute(array, "ctx", ctx_pairs(ahead, 0))


def along_y(array, ahead):
    pairs = [(2 * y + core, 2 * ((y + ahead) % NY) + core) for y in range(NY) for core in range(2)]
    return lax.ppermute(array, "tp", pairs)


def other_core(array):
    return lax.ppermute(array, "tp", [(i, i ^ 1) for i in range(2 * NY)])


def neighbour(array, by):
    count = NZ * NX
    return lax.ppermute(array, "ctx", [(i, i + by) for i in range(count) if 0 <= i + by < count])


def local(qkv, short_filter, long_filter, out_weight, cotangent, valid_len):
    forward_table, causal_table, anti_table = (jnp.asarray(table) for table in tables())
    ctx, tp = lax.axis_index("ctx"), lax.axis_index("tp")
    z, x = ctx // NX, ctx % NX
    y, core = tp // 2, tp % 2
    streams = qkv.transpose(1, 0, 2)
    short = short_filter.transpose(1, 0, 2)

    def masked_tail(stream, rows):
        alive = (jnp.arange(ROWS - rows, ROWS) < valid_len[0])[:, None]
        return jnp.where(alive, streams[stream, ROWS - rows :], jnp.zeros((), BF16))

    tail = jnp.concatenate([masked_tail(0, RIM), masked_tail(1, TAIL), masked_tail(2, TAIL)], axis=0)
    halo = neighbour(tail, 1)

    def block_of(ahead, other=0):
        return (y + ahead) % NY * 2 + (core + other) % 2

    own_other = other_core(cotangent)
    below = along_y(cotangent, 1)
    above = along_y(cotangent, -1)
    held, halo = lax.optimization_barrier((cotangent, halo))
    far = along_y(held, 2)

    mix_in, q_side, k_side, v_side, conv = run_forward(
        valid_len, streams, halo, short, long_filter, forward_table, causal_table
    )

    below_other, above_other = other_core(below), other_core(above)
    far_other = other_core(far)
    near = [cotangent, own_other, below, below_other, above, above_other]
    near_blocks = [block_of(0), block_of(0, 1), block_of(-1), block_of(-1, 1), block_of(1), block_of(1, 1)]
    last = [far, far_other]
    last_blocks = [block_of(2), block_of(2, 1)]

    given = run_project(
        jnp.stack([block_of(1, 1), block_of(2, 1), block_of(3, 1), block_of(0, 1)]), mix_in, out_weight
    )
    taken = other_core(given)

    place = x.reshape(1)
    groups = []
    for pieces in (near, last):
        own, *sent = run_outer(place, mix_in, pieces)
        groups.append([own] + [along_x(array, ahead + 1) for ahead, array in enumerate(sent)])

    acc = run_d_mix(jnp.stack([valid_len[0]] + near_blocks), out_weight, near)[0]
    d_conv, d_q, msg = run_d_mix(
        jnp.stack([valid_len[0]] + last_blocks), out_weight, last, (acc, q_side, k_side, v_side, conv)
    )
    msg = neighbour(msg, -1)

    one, two, three, own_out = run_project_add(
        jnp.stack([block_of(1), block_of(2), block_of(3), block_of(0)]), mix_in, out_weight, taken
    )
    arrived = [along_y(one, 1), along_y(two, 2), along_y(three, 3)]
    mixed = own_out
    for array in arrived:
        mixed = mixed + array.astype(F32)
    mixed = mixed.astype(BF16)

    d_streams = run_backward(
        valid_len, d_conv, msg, d_q, k_side, v_side, short, long_filter, forward_table, anti_table
    )
    d_qkv = d_streams.transpose(1, 0, 2)

    offsets = jnp.stack([(block - z) % NZ for block in near_blocks + last_blocks])
    total, *sent = run_gather_x(offsets, groups)
    for ahead, array in enumerate(sent):
        total = total + along_z(array, ahead + 1).astype(F32)
    d_weight = total * (1.0 / jnp.sqrt(jnp.float32(ROWS * NZ * NX)))
    return mixed, d_qkv, d_weight


def solution(mesh):
    in_specs = (
        P("ctx", None, "tp"),
        P(None, None, "tp"),
        P(None, "tp"),
        P("tp", None),
        P("ctx", "tp"),
        P("ctx"),
    )
    out_specs = (P("ctx", "tp"), P("ctx", None, "tp"), P("tp", "ctx"))
    return jax.shard_map(local, mesh=mesh, in_specs=in_specs, out_specs=out_specs, check_vma=False)
```

time: 508 us -> 190 us (0.37)
  the two profiles are of different devices: /device:TPU:102 before, /device:TPU:194 now
where the time goes in v1:
time: 190 us; the launch traced here: 189 us
  waiting for transfers between devices  74.6 us (39%)
  starting transfers between devices  47.3 us (25%)
  Pallas kernels  40.3 us (21%)
  local copies, waits for them, and re-layouts  21.2 us (11%)
  other arithmetic  4.07 us (2%)
    ppermute x6, waiting for transfers between devices, along_x(): return lax.ppermute(array, 'ctx', ctx_pairs(0, ahead))  38.2 us
    ppermute x6, waiting for transfers between devices, along_y(): return lax.ppermute(array, 'tp', pairs)  26.6 us
    ppermute x7, starting transfers between devices, along_z(): return lax.ppermute(array, 'ctx', ctx_pairs(ahead, 0))  21.9 us
    unnamed x76, local copies, waits for them, and re-layouts  21 us
    pallas_call x2, Pallas kernels, run_outer(): pl.pallas_call(functools.partial(outer_kernel, count), in_specs=[SMEM, VM...  9.42 us
    pallas_call x1, Pallas kernels, run_backward(): pl.pallas_call(backward_kernel, grid=(CH // LANES,), in_specs=[SMEM, lane...  8.88 us
    ppermute x6, starting transfers between devices, along_x(): return lax.ppermute(array, 'ctx', ctx_pairs(0, ahead))  8.74 us
    ppermute x6, starting transfers between devices, along_y(): return lax.ppermute(array, 'tp', pairs)  8.62 us
  transfers between devices with their start and end apart: 26, of which 8 were waited for; matrix products, arithmetic and copies ran while one was open for 1% of the time, Pallas kernels for 21%

profile of v1, /device:TPU:194, one launch (start us, length us, event | category | flops | bytes accessed | tf_op | source)
XLA Modules:
  0.0 189.4 jit_solution(204063645278805878)
XLA Ops:
  3.2 3.4 %collective-permute-start = (bf16[304,512]{1,0:T(8,128)(2,1)S(1)}, bf16[304,512]{1,0:T(8,128)(2,1)S(1)}, u32[]{:S(2)}, u32[]{:S(2)}) collective-permute-start(bf16[304,512]{1,0:T(8,128)(2,1)S(1)} %pad_maximum_fusion), channel_id=1, source_target_pairs={{0,8},{8,16},{16,24},{24,32},{32,40},{40,48},{48,56},{56,64},{64,7... | collective-permute-start | bytes 933896 | tf_op jit(solution)/shard_map/ppermute | solution.py:420
  6.8 7.4 %collective-permute-done.halo_ref = bf16[304,512]{1,0:T(8,128)(2,1)S(1)} collective-permute-done((bf16[304,512]{1,0:T(8,128)(2,1)S(1)}, bf16[304,512]{1,0:T(8,128)(2,1)S(1)}, u32[]{:S(2)}, u32[]{:S(2)}) %collective-permute-start) | collective-permute-done | bytes 311328 | tf_op jit(solution)/shard_map/ppermute | solution.py:420
  14.2 3.2 %collective-permute-start.5 = (bf16[512,512]{1,0:T(8,128)(2,1)}, bf16[512,512]{1,0:T(8,128)(2,1)}, u32[]{:S(2)}, u32[]{:S(2)}) collective-permute-start(bf16[512,512]{1,0:T(8,128)(2,1)} %refs_0_.3), channel_id=1, source_target_pairs={{0,4},{1,5},{2,6},{3,7},{4,0},{5,1},{6,2},{7,3},{8,12},{9,13},{10,... | collective-permute-start | bytes 1572872 | tf_op jit(solution)/shard_map/ppermute | solution.py:411
  22.3 7.0 %forward.1 = (bf16[512,512]{1,0:T(8,128)(2,1)S(1)}, f32[512,512]{1,0:T(8,128)S(1)}, f32[512,512]{1,0:T(8,128)S(1)}, f32[512,512]{1,0:T(8,128)S(1)}, f32[512,512]{1,0:T(8,128)S(1)}) custom-call(s32[1]{0:T(128)} %copy.12.valid_ref, bf16[3,512,512]{2,1,0:T(8,128)(2,1)S(1)} %bitcast.39, bf16[304,512]{1,0:T(8,128)(2,1)S(1)} %collective-permute-done.halo_ref, ...), custom_call_target="tpu_custom_call" | custom-call | flops 5000000000 | bytes 7000000 | tf_op jit(solution)/shard_map/forward/pallas_call | solution.py:195
  32.3 3.6 %project.1 = bf16[4,512,512]{2,1,0:T(8,128)(2,1)} custom-call(s32[4]{0:T(128)S(1)} %pad_add_fusion.1.order_ref, bf16[512,512]{1,0:T(8,128)(2,1)S(1)} %get-tuple-element.34.mix_ref, bf16[512,4096]{1,0:T(8,128)(2,1)S(1)} %copy-done), custom_call_target="tpu_custom_call" | custom-call | flops 1073741824 | bytes 4500000 | tf_op jit(solution)/shard_map/project/pallas_call | solution.py:241
  38.6 11.8 %collective-permute-done.10.refs_4_ = bf16[512,512]{1,0:T(8,128)(2,1)} collective-permute-done((bf16[512,512]{1,0:T(8,128)(2,1)S(1)}, bf16[512,512]{1,0:T(8,128)(2,1)}, u32[]{:S(2)}, u32[]{:S(2)}) %collective-permute-start.10) | collective-permute-done | bytes 524320 | tf_op jit(solution)/shard_map/ppermute | solution.py:411
  50.4 2.0 %collective-permute-done.8.refs_2_ = bf16[512,512]{1,0:T(8,128)(2,1)} collective-permute-done((bf16[512,512]{1,0:T(8,128)(2,1)S(1)}, bf16[512,512]{1,0:T(8,128)(2,1)}, u32[]{:S(2)}, u32[]{:S(2)}) %collective-permute-start.8) | collective-permute-done | bytes 524320 | tf_op jit(solution)/shard_map/ppermute | solution.py:411
  52.4 3.0 %outer.3 = (f32[2,512,128]{2,1,0:T(8,128)S(1)}, bf16[2,512,128]{2,1,0:T(8,128)(2,1)S(1)}, bf16[2,512,128]{2,1,0:T(8,128)(2,1)}, bf16[2,512,128]{2,1,0:T(8,128)(2,1)S(1)}) custom-call(s32[1]{0:T(128)} %bitcast.25.place_ref, bf16[512,512]{1,0:T(8,128)(2,1)S(1)} %get-tuple-element.34.mix_ref, bf16[512,512]{1,0:T(8,128)(2,1)} %collective-permute-done.5.refs_0_, ...), custom_call_target="tpu_custom_call" | custom-call | flops 536870912 | bytes 2600000 | tf_op jit(solution)/shard_map/outer/pallas_call | solution.py:308
  57.7 6.4 %outer.2 = (f32[6,512,128]{2,1,0:T(8,128)S(1)}, bf16[6,512,128]{2,1,0:T(8,128)(2,1)}, bf16[6,512,128]{2,1,0:T(8,128)(2,1)}, bf16[6,512,128]{2,1,0:T(8,128)(2,1)}) custom-call(s32[1]{0:T(128)} %bitcast.25.place_ref, bf16[512,512]{1,0:T(8,128)(2,1)S(1)} %get-tuple-element.34.mix_ref, bf16[512,512]{1,0:T(8,128)(2,1)S(1)} %copy-done.16, ...), custom_call_target="tpu_custom_call" | custom-call | flops 1610612736 | bytes 7800000 | tf_op jit(solution)/shard_map/outer/pallas_call | solution.py:308
  66.3 2.2 %collective-permute-start.14 = (bf16[6,512,128]{2,1,0:T(8,128)(2,1)}, bf16[6,512,128]{2,1,0:T(8,128)(2,1)}, u32[]{:S(2)}, u32[]{:S(2)}) collective-permute-start(bf16[6,512,128]{2,1,0:T(8,128)(2,1)} %get-tuple-element.49), channel_id=1, source_target_pairs={{0,16},{8,24},{16,0},{24,8},{32,48},{40,56},{48,32},{56,40},{64,80... | collective-permute-start | bytes 2359304 | tf_op jit(solution)/shard_map/ppermute | solution.py:402
  68.6 2.5 %collective-permute-start.15 = (bf16[6,512,128]{2,1,0:T(8,128)(2,1)}, bf16[6,512,128]{2,1,0:T(8,128)(2,1)}, u32[]{:S(2)}, u32[]{:S(2)}) collective-permute-start(bf16[6,512,128]{2,1,0:T(8,128)(2,1)} %get-tuple-element.50), channel_id=1, source_target_pairs={{0,24},{8,0},{16,8},{24,16},{32,56},{40,32},{48,40},{56,48},{64,88... | collective-permute-start | bytes 2359304 | tf_op jit(solution)/shard_map/ppermute | solution.py:402
  71.8 38.2 %collective-permute-done.17.refs_6_ = bf16[2,512,128]{2,1,0:T(8,128)(2,1)} collective-permute-done((bf16[2,512,128]{2,1,0:T(8,128)(2,1)}, bf16[2,512,128]{2,1,0:T(8,128)(2,1)}, u32[]{:S(2)}, u32[]{:S(2)}) %collective-permute-start.17) | collective-permute-done | bytes 262176 | tf_op jit(solution)/shard_map/ppermute | solution.py:402
  111.5 2.2 %copy-done.1 = bf16[512,4096]{1,0:T(8,128)(2,1)S(1)} copy-done((bf16[512,4096]{1,0:T(8,128)(2,1)S(1)}, bf16[512,4096]{1,0:T(8,128)(2,1)}, u32[]{:S(2)}) %copy-start.1) | copy-done | bytes 4194328
  114.8 3.7 %d_mix.2.refs_2_ = f32[512,512]{1,0:T(8,128)S(1)} custom-call(s32[7]{0:T(128)S(1)} %stack.88.info_ref, bf16[512,4096]{1,0:T(8,128)(2,1)S(1)} %copy-done.1, bf16[512,512]{1,0:T(8,128)(2,1)S(1)} %copy-done.17, bf16[512,512]{1,0:T(8,128)(2,1)} %collective-permute-done.7.refs_1_, bf16[512,512]{1,0:T(8,128)(2,1)} %collective-permute-done.8.refs_2_, ...), custom_call_target="tpu_custom_call" | custom-call | flops 1610612736 | bytes 8000000 | tf_op jit(solution)/shard_map/d_mix/pallas_call | solution.py:384
  119.0 2.7 %d_mix.3 = (bf16[512,512]{1,0:T(8,128)(2,1)S(1)}, f32[512,512]{1,0:T(8,128)S(1)}, bf16[192,512]{1,0:T(8,128)(2,1)}) custom-call(s32[3]{0:T(128)S(1)} %pad_add_fusion.2.info_ref, bf16[512,4096]{1,0:T(8,128)(2,1)S(1)} %copy-done.2, bf16[512,512]{1,0:T(8,128)(2,1)} %collective-permute-done.5.refs_0_, bf16[512,512]{1,0:T(8,128)(2,1)} %collective-permute-done.6.refs_1_, ...), custom_call_target="tpu_custom_call" | custom-call | flops 536870912 | bytes 8000000 | tf_op jit(solution)/shard_map/d_mix/pallas_call | solution.py:384
  124.1 4.2 %collective-permute-start.12 = (bf16[192,512]{1,0:T(8,128)(2,1)}, bf16[192,512]{1,0:T(8,128)(2,1)}, u32[]{:S(2)}, u32[]{:S(2)}) collective-permute-start(bf16[192,512]{1,0:T(8,128)(2,1)} %get-tuple-element.45), channel_id=1, source_target_pairs={{8,0},{16,8},{24,16},{32,24},{40,32},{48,40},{56,48},{64,56},{72,6... | collective-permute-start | bytes 589832 | tf_op jit(solution)/shard_map/ppermute | solution.py:420
  133.0 2.2 %gather_x.1 = (f32[512,128]{1,0:T(8,128)S(1)}, bf16[512,128]{1,0:T(8,128)(2,1)S(1)}, bf16[512,128]{1,0:T(8,128)(2,1)S(1)}, bf16[512,128]{1,0:T(8,128)(2,1)S(1)},...) custom-call(s32[8]{0:T(128)S(1)} %stack.97.offset_ref, ...), custom_call_target="tpu_custom_call" | custom-call | flops 4000000 | bytes 6500000 | tf_op jit(solution)/shard_map/gather_x/pallas_call | solution.py:336
  136.3 5.8 %collective-permute-start.21 = (bf16[512,128]{1,0:T(8,128)(2,1)S(1)}, bf16[512,128]{1,0:T(8,128)(2,1)S(1)}, u32[]{:S(2)}, u32[]{:S(2)}) collective-permute-start(bf16[512,128]{1,0:T(8,128)(2,1)S(1)} %get-tuple-element.58), channel_id=1, source_target_pairs={{0,96},{8,104},{16,112},{24,120},{32,128},{40,136},{48,144},{56,15... | collective-permute-start | bytes 393224 | tf_op jit(solution)/shard_map/ppermute | solution.py:406
  142.3 4.3 %collective-permute-start.23 = (bf16[512,128]{1,0:T(8,128)(2,1)S(1)}, bf16[512,128]{1,0:T(8,128)(2,1)S(1)}, u32[]{:S(2)}, u32[]{:S(2)}) collective-permute-start(bf16[512,128]{1,0:T(8,128)(2,1)S(1)} %get-tuple-element.60), channel_id=1, source_target_pairs={{0,160},{8,168},{16,176},{24,184},{32,192},{40,200},{48,208},{56,2... | collective-permute-start | bytes 393224 | tf_op jit(solution)/shard_map/ppermute | solution.py:406
  146.7 2.8 %project_add.1 = (bf16[512,512]{1,0:T(8,128)(2,1)S(1)}, bf16[512,512]{1,0:T(8,128)(2,1)S(1)}, bf16[512,512]{1,0:T(8,128)(2,1)S(1)}, f32[512,512]{1,0:T(8,128)S(1)}) custom-call(s32[4]{0:T(128)S(1)} %pad_add_fusion.order_ref, bf16[512,512]{1,0:T(8,128)(2,1)S(1)} %get-tuple-element.34.mix_ref, bf16[512,4096]{1,0:T(8,128)(2,1)S(1)} %copy-done.3, ...), custom_call_target="tpu_custom_call" | custom-call | flops 1073741824 | bytes 7000000 | tf_op jit(solution)/shard_map/project_add/pallas_call | solution.py:273
  150.9 10.4 %collective-permute-start.25 = (bf16[512,128]{1,0:T(8,128)(2,1)S(1)}, bf16[512,128]{1,0:T(8,128)(2,1)S(1)}, u32[]{:S(2)}, u32[]{:S(2)}) collective-permute-start(bf16[512,128]{1,0:T(8,128)(2,1)S(1)} %get-tuple-element.62), channel_id=1, source_target_pairs={{0,224},{8,232},{16,240},{24,248},{32,0},{40,8},{48,16},{56,24},{6... | collective-permute-start | bytes 393224 | tf_op jit(solution)/shard_map/ppermute | solution.py:406
  163.7 2.1 %collective-permute-start.4 = (bf16[512,512]{1,0:T(8,128)(2,1)S(1)}, bf16[512,512]{1,0:T(8,128)(2,1)S(1)}, u32[]{:S(2)}, u32[]{:S(2)}) collective-permute-start(bf16[512,512]{1,0:T(8,128)(2,1)S(1)} %get-tuple-element.38), channel_id=1, source_target_pairs={{0,6},{1,7},{2,0},{3,1},{4,2},{5,3},{6,4},{7,5},{8,14},{9,15},{10,... | collective-permute-start | bytes 1572872 | tf_op jit(solution)/shard_map/ppermute | solution.py:411
  165.8 8.9 %backward.1 = bf16[3,512,512]{2,1,0:T(8,128)(2,1)} custom-call(s32[1]{0:T(128)} %copy.12.valid_ref, bf16[512,512]{1,0:T(8,128)(2,1)S(1)} %copy-done.28, bf16[192,512]{1,0:T(8,128)(2,1)} %collective-permute-done.12.msg_ref, f32[512,512]{1,0:T(8,128)S(1)} %copy-done.26, f32[512,512]{1,0:T(8,128)S(1)} %copy-done.8, f32[512,512]{1,0:T(8,128)S(1)} %copy-done.11, ...), custom_call_target="tpu_custom_call" | custom-call | flops 5000000000 | bytes 7000000 | tf_op jit(solution)/shard_map/backward/pallas_call | solution.py:215
  175.5 12.1 %collective-permute-done.2 = bf16[512,512]{1,0:T(8,128)(2,1)S(1)} collective-permute-done((bf16[512,512]{1,0:T(8,128)(2,1)S(1)}, bf16[512,512]{1,0:T(8,128)(2,1)S(1)}, u32[]{:S(2)}, u32[]{:S(2)}) %collective-permute-start.2) | collective-permute-done | bytes 524320 | tf_op jit(solution)/shard_map/ppermute | solution.py:411
  (125 shorter events, 35.5 us)
Async XLA Ops:
  3.2 11.0 %collective-permute-start = (bf16[304,512]{1,0:T(8,128)(2,1)S(1)}, bf16[304,512]{1,0:T(8,128)(2,1)S(1)}, u32[]{:S(2)}, u32[]{:S(2)}) collective-permute-start(bf16[304,512]{1,0:T(8,128)(2,1)S(1)} %pad_maximum_fusion), channel_id=1, source_target_pairs={{0,8},{8,16},{16,24},{24,32},{32,40},{40,48},{48,56},{56,64},{64,7... | collective-permute-start | bytes 933896 | tf_op jit(solution)/shard_map/ppermute | solution.py:420
  14.2 23.9 %collective-permute-start.5 = (bf16[512,512]{1,0:T(8,128)(2,1)}, bf16[512,512]{1,0:T(8,128)(2,1)}, u32[]{:S(2)}, u32[]{:S(2)}) collective-permute-start(bf16[512,512]{1,0:T(8,128)(2,1)} %refs_0_.3), channel_id=1, source_target_pairs={{0,4},{1,5},{2,6},{3,7},{4,0},{5,1},{6,2},{7,3},{8,12},{9,13},{10,... | collective-permute-start | bytes 1572872 | tf_op jit(solution)/shard_map/ppermute | solution.py:411
  36.0 106.3 %collective-permute-start.1 = (bf16[4,512,512]{2,1,0:T(8,128)(2,1)}, bf16[4,512,512]{2,1,0:T(8,128)(2,1)S(1)}, u32[]{:S(2)}, u32[]{:S(2)}) collective-permute-start(bf16[4,512,512]{2,1,0:T(8,128)(2,1)} %project.1), channel_id=1, source_target_pairs={{0,1},{1,0},{2,3},{3,2},{4,5},{5,4},{6,7},{7,6},{8,9},{9,8},{10,11... | collective-permute-start | bytes 6291464 | tf_op jit(solution)/shard_map/ppermute | solution.py:415
  36.0 14.5 %collective-permute-start.10 = (bf16[512,512]{1,0:T(8,128)(2,1)S(1)}, bf16[512,512]{1,0:T(8,128)(2,1)}, u32[]{:S(2)}, u32[]{:S(2)}) collective-permute-start(bf16[512,512]{1,0:T(8,128)(2,1)S(1)} %copy-done.16), channel_id=1, source_target_pairs={{0,6},{1,7},{2,0},{3,1},{4,2},{5,3},{6,4},{7,5},{8,14},{9,15},{10,... | collective-permute-start | bytes 1572872 | tf_op jit(solution)/shard_map/ppermute | solution.py:411
  37.1 15.3 %collective-permute-start.8 = (bf16[512,512]{1,0:T(8,128)(2,1)S(1)}, bf16[512,512]{1,0:T(8,128)(2,1)}, u32[]{:S(2)}, u32[]{:S(2)}) collective-permute-start(bf16[512,512]{1,0:T(8,128)(2,1)S(1)} %copy-done.16), channel_id=1, source_target_pairs={{0,2},{1,3},{2,4},{3,5},{4,6},{5,7},{6,0},{7,1},{8,10},{9,11},{10,... | collective-permute-start | bytes 1572872 | tf_op jit(solution)/shard_map/ppermute | solution.py:411
  38.1 14.3 %collective-permute-start.6 = (bf16[512,512]{1,0:T(8,128)(2,1)}, bf16[512,512]{1,0:T(8,128)(2,1)}, u32[]{:S(2)}, u32[]{:S(2)}) collective-permute-start(bf16[512,512]{1,0:T(8,128)(2,1)} %collective-permute-done.5.refs_0_), channel_id=1, source_target_pairs={{0,1},{1,0},{2,3},{3,2},{4,5},{5,4},{6,7},{7,6},{8,9},{9,8},{10,11... | collective-permute-start | bytes 1572872 | tf_op jit(solution)/shard_map/ppermute | solution.py:415
  38.1 19.6 %collective-permute-start.7 = (bf16[512,512]{1,0:T(8,128)(2,1)S(1)}, bf16[512,512]{1,0:T(8,128)(2,1)}, u32[]{:S(2)}, u32[]{:S(2)}) collective-permute-start(bf16[512,512]{1,0:T(8,128)(2,1)S(1)} %copy-done.16), channel_id=1, source_target_pairs={{0,1},{1,0},{2,3},{3,2},{4,5},{5,4},{6,7},{7,6},{8,9},{9,8},{10,11... | collective-permute-start | bytes 1572872 | tf_op jit(solution)/shard_map/ppermute | solution.py:415
  56.2 14.9 %collective-permute-start.16 = (bf16[2,512,128]{2,1,0:T(8,128)(2,1)S(1)}, bf16[2,512,128]{2,1,0:T(8,128)(2,1)S(1)}, u32[]{:S(2)}, u32[]{:S(2)}) collective-permute-start(bf16[2,512,128]{2,1,0:T(8,128)(2,1)S(1)} %get-tuple-element.52), channel_id=1, source_target_pairs={{0,8},{8,16},{16,24},{24,0},{32,40},{40,48},{48,56},{56,32},{64,72... | collective-permute-start | bytes 786440 | tf_op jit(solution)/shard_map/ppermute | solution.py:402
  65.2 63.4 %collective-permute-start.13 = (bf16[6,512,128]{2,1,0:T(8,128)(2,1)}, bf16[6,512,128]{2,1,0:T(8,128)(2,1)S(1)}, u32[]{:S(2)}, u32[]{:S(2)}) collective-permute-start(bf16[6,512,128]{2,1,0:T(8,128)(2,1)} %get-tuple-element.48), channel_id=1, source_target_pairs={{0,8},{8,16},{16,24},{24,0},{32,40},{40,48},{48,56},{56,32},{64,72... | collective-permute-start | bytes 2359304 | tf_op jit(solution)/shard_map/ppermute | solution.py:402
  66.3 62.2 %collective-permute-start.14 = (bf16[6,512,128]{2,1,0:T(8,128)(2,1)}, bf16[6,512,128]{2,1,0:T(8,128)(2,1)}, u32[]{:S(2)}, u32[]{:S(2)}) collective-permute-start(bf16[6,512,128]{2,1,0:T(8,128)(2,1)} %get-tuple-element.49), channel_id=1, source_target_pairs={{0,16},{8,24},{16,0},{24,8},{32,48},{40,56},{48,32},{56,40},{64,80... | collective-permute-start | bytes 2359304 | tf_op jit(solution)/shard_map/ppermute | solution.py:402
  68.6 60.0 %collective-permute-start.15 = (bf16[6,512,128]{2,1,0:T(8,128)(2,1)}, bf16[6,512,128]{2,1,0:T(8,128)(2,1)}, u32[]{:S(2)}, u32[]{:S(2)}) collective-permute-start(bf16[6,512,128]{2,1,0:T(8,128)(2,1)} %get-tuple-element.50), channel_id=1, source_target_pairs={{0,24},{8,0},{16,8},{24,16},{32,56},{40,32},{48,40},{56,48},{64,88... | collective-permute-start | bytes 2359304 | tf_op jit(solution)/shard_map/ppermute | solution.py:402
  71.7 38.3 %collective-permute-start.17 = (bf16[2,512,128]{2,1,0:T(8,128)(2,1)}, bf16[2,512,128]{2,1,0:T(8,128)(2,1)}, u32[]{:S(2)}, u32[]{:S(2)}) collective-permute-start(bf16[2,512,128]{2,1,0:T(8,128)(2,1)} %get-tuple-element.53), channel_id=1, source_target_pairs={{0,16},{8,24},{16,0},{24,8},{32,48},{40,56},{48,32},{56,40},{64,80... | collective-permute-start | bytes 786440 | tf_op jit(solution)/shard_map/ppermute | solution.py:402
  110.1 13.4 %collective-permute-start.18 = (bf16[2,512,128]{2,1,0:T(8,128)(2,1)}, bf16[2,512,128]{2,1,0:T(8,128)(2,1)S(1)}, u32[]{:S(2)}, u32[]{:S(2)}) collective-permute-start(bf16[2,512,128]{2,1,0:T(8,128)(2,1)} %copy-done.29), channel_id=1, source_target_pairs={{0,24},{8,0},{16,8},{24,16},{32,56},{40,32},{48,40},{56,48},{64,88... | collective-permute-start | bytes 786440 | tf_op jit(solution)/shard_map/ppermute | solution.py:402
  124.1 17.9 %collective-permute-start.12 = (bf16[192,512]{1,0:T(8,128)(2,1)}, bf16[192,512]{1,0:T(8,128)(2,1)}, u32[]{:S(2)}, u32[]{:S(2)}) collective-permute-start(bf16[192,512]{1,0:T(8,128)(2,1)} %get-tuple-element.45), channel_id=1, source_target_pairs={{8,0},{16,8},{24,16},{32,24},{40,32},{48,40},{56,48},{64,56},{72,6... | collective-permute-start | bytes 589832 | tf_op jit(solution)/shard_map/ppermute | solution.py:420
  135.2 14.4 %collective-permute-start.19 = (bf16[512,128]{1,0:T(8,128)(2,1)S(1)}, bf16[512,128]{1,0:T(8,128)(2,1)S(1)}, u32[]{:S(2)}, u32[]{:S(2)}) collective-permute-start(bf16[512,128]{1,0:T(8,128)(2,1)S(1)} %get-tuple-element.56), channel_id=1, source_target_pairs={{0,32},{8,40},{16,48},{24,56},{32,64},{40,72},{48,80},{56,88},{64,... | collective-permute-start | bytes 393224 | tf_op jit(solution)/shard_map/ppermute | solution.py:406
  136.3 14.7 %collective-permute-start.20 = (bf16[512,128]{1,0:T(8,128)(2,1)S(1)}, bf16[512,128]{1,0:T(8,128)(2,1)S(1)}, u32[]{:S(2)}, u32[]{:S(2)}) collective-permute-start(bf16[512,128]{1,0:T(8,128)(2,1)S(1)} %get-tuple-element.57), channel_id=1, source_target_pairs={{0,64},{8,72},{16,80},{24,88},{32,96},{40,104},{48,112},{56,120},{... | collective-permute-start | bytes 393224 | tf_op jit(solution)/shard_map/ppermute | solution.py:406
  136.3 26.2 %collective-permute-start.21 = (bf16[512,128]{1,0:T(8,128)(2,1)S(1)}, bf16[512,128]{1,0:T(8,128)(2,1)S(1)}, u32[]{:S(2)}, u32[]{:S(2)}) collective-permute-start(bf16[512,128]{1,0:T(8,128)(2,1)S(1)} %get-tuple-element.58), channel_id=1, source_target_pairs={{0,96},{8,104},{16,112},{24,120},{32,128},{40,136},{48,144},{56,15... | collective-permute-start | bytes 393224 | tf_op jit(solution)/shard_map/ppermute | solution.py:406
  142.0 20.4 %collective-permute-start.22 = (bf16[512,128]{1,0:T(8,128)(2,1)S(1)}, bf16[512,128]{1,0:T(8,128)(2,1)S(1)}, u32[]{:S(2)}, u32[]{:S(2)}) collective-permute-start(bf16[512,128]{1,0:T(8,128)(2,1)S(1)} %get-tuple-element.59), channel_id=1, source_target_pairs={{0,128},{8,136},{16,144},{24,152},{32,160},{40,168},{48,176},{56,1... | collective-permute-start | bytes 393224 | tf_op jit(solution)/shard_map/ppermute | solution.py:406
  142.3 21.4 %collective-permute-start.23 = (bf16[512,128]{1,0:T(8,128)(2,1)S(1)}, bf16[512,128]{1,0:T(8,128)(2,1)S(1)}, u32[]{:S(2)}, u32[]{:S(2)}) collective-permute-start(bf16[512,128]{1,0:T(8,128)(2,1)S(1)} %get-tuple-element.60), channel_id=1, source_target_pairs={{0,160},{8,168},{16,176},{24,184},{32,192},{40,200},{48,208},{56,2... | collective-permute-start | bytes 393224 | tf_op jit(solution)/shard_map/ppermute | solution.py:406
  149.5 25.1 %collective-permute-start.24 = (bf16[512,128]{1,0:T(8,128)(2,1)S(1)}, bf16[512,128]{1,0:T(8,128)(2,1)S(1)}, u32[]{:S(2)}, u32[]{:S(2)}) collective-permute-start(bf16[512,128]{1,0:T(8,128)(2,1)S(1)} %get-tuple-element.61), channel_id=1, source_target_pairs={{0,192},{8,200},{16,208},{24,216},{32,224},{40,232},{48,240},{56,2... | collective-permute-start | bytes 393224 | tf_op jit(solution)/shard_map/ppermute | solution.py:406
  150.9 23.7 %collective-permute-start.25 = (bf16[512,128]{1,0:T(8,128)(2,1)S(1)}, bf16[512,128]{1,0:T(8,128)(2,1)S(1)}, u32[]{:S(2)}, u32[]{:S(2)}) collective-permute-start(bf16[512,128]{1,0:T(8,128)(2,1)S(1)} %get-tuple-element.62), channel_id=1, source_target_pairs={{0,224},{8,232},{16,240},{24,248},{32,0},{40,8},{48,16},{56,24},{6... | collective-permute-start | bytes 393224 | tf_op jit(solution)/shard_map/ppermute | solution.py:406
  162.4 25.2 %collective-permute-start.2 = (bf16[512,512]{1,0:T(8,128)(2,1)S(1)}, bf16[512,512]{1,0:T(8,128)(2,1)S(1)}, u32[]{:S(2)}, u32[]{:S(2)}) collective-permute-start(bf16[512,512]{1,0:T(8,128)(2,1)S(1)} %get-tuple-element.36), channel_id=1, source_target_pairs={{0,2},{1,3},{2,4},{3,5},{4,6},{5,7},{6,0},{7,1},{8,10},{9,11},{10,... | collective-permute-start | bytes 1572872 | tf_op jit(solution)/shard_map/ppermute | solution.py:411
  162.4 25.2 %collective-permute-start.3 = (bf16[512,512]{1,0:T(8,128)(2,1)S(1)}, bf16[512,512]{1,0:T(8,128)(2,1)S(1)}, u32[]{:S(2)}, u32[]{:S(2)}) collective-permute-start(bf16[512,512]{1,0:T(8,128)(2,1)S(1)} %get-tuple-element.37), channel_id=1, source_target_pairs={{0,4},{1,5},{2,6},{3,7},{4,0},{5,1},{6,2},{7,3},{8,12},{9,13},{10,... | collective-permute-start | bytes 1572872 | tf_op jit(solution)/shard_map/ppermute | solution.py:411
  163.7 24.6 %collective-permute-start.4 = (bf16[512,512]{1,0:T(8,128)(2,1)S(1)}, bf16[512,512]{1,0:T(8,128)(2,1)S(1)}, u32[]{:S(2)}, u32[]{:S(2)}) collective-permute-start(bf16[512,512]{1,0:T(8,128)(2,1)S(1)} %get-tuple-element.38), channel_id=1, source_target_pairs={{0,6},{1,7},{2,0},{3,1},{4,2},{5,3},{6,4},{7,5},{8,14},{9,15},{10,... | collective-permute-start | bytes 1572872 | tf_op jit(solution)/shard_map/ppermute | solution.py:411
  (40 other events, 243.7 us)

commit v2 on v1

v2 whole, which is shorter than its diff:
```python
import functools

import jax
import jax.numpy as jnp
import ml_dtypes
import numpy as np
from jax import lax
from jax.experimental import pallas as pl
from jax.experimental.pallas import tpu as pltpu
from jax.sharding import PartitionSpec as P

SHORT = 7
LONG = 128
ROWS = 512
CH = 512
LANES = 128
TAIL = 144
RIM = 16
STEP = 64
NZ, NX, NY = 8, 4, 4
F32, BF16 = jnp.float32, jnp.bfloat16


def split_bf16(table):
    high = table.astype(ml_dtypes.bfloat16)
    low = (table - high.astype(np.float64)).astype(ml_dtypes.bfloat16)
    return high, low


def tables():
    size = 2 * LONG
    freq = np.arange(LONG)[:, None]
    angle = 2.0 * np.pi * freq * np.arange(size)[None, :] / size
    real = np.concatenate([np.cos(angle), np.sin(angle)], axis=0)
    real[LONG] = (-1.0) ** np.arange(size)
    high, low = split_bf16(real[:, :LONG])
    forward = np.concatenate([high, low], axis=1)
    weight = np.full((2 * LONG, 1), 2.0 / size)
    weight[0] = weight[LONG] = 1.0 / size
    inverse = (real * weight).T
    causal = np.concatenate(split_bf16(inverse[LONG:]), axis=0)
    anti = np.concatenate(split_bf16(inverse[:LONG]), axis=0)
    return forward, causal, anti


def signs(rows):
    row = lax.broadcasted_iota(jnp.int32, (rows, LANES), 0)
    return jnp.where(row % 2 == 0, 1.0, -1.0).astype(F32)


def spectrum(forward, block):
    return jnp.dot(forward, jnp.concatenate([block, block], axis=0), preferred_element_type=F32)


def filter_spectrum(forward, taps):
    both = spectrum(forward, taps)
    cos_part, sin_part = both[:LONG], both[LONG:]
    first = lax.broadcasted_iota(jnp.int32, (LONG, LANES), 0) == 0
    return cos_part, jnp.where(first, 0.0, sin_part), jnp.where(first, sin_part, cos_part)


def back(table, product):
    high = product.astype(BF16)
    low = (product - high.astype(F32)).astype(BF16)
    half = table.shape[0] // 2
    both = jnp.dot(table, high, preferred_element_type=F32)
    rest = jnp.dot(table[:half], low, preferred_element_type=F32)
    return both[:half] + both[half:] + rest


def live_rows(valid, start, rows):
    row = lax.broadcasted_iota(jnp.int32, (rows, LANES), 0) + start
    return jnp.where(row < valid, 1.0, 0.0).astype(F32)


def filtered(short_ref, ext_ref, stream, start, rows):
    total = short_ref[stream, 0:1] * ext_ref[stream, start : start + rows]
    for tap in range(1, SHORT):
        total += short_ref[stream, tap : tap + 1] * ext_ref[stream, start - tap : start - tap + rows]
    return total


def convolve(before, now, sign, inv, cos_h, sin_h, alt_h):
    window = before + sign * now
    cos_x, sin_x = window[:LONG], window[LONG:]
    product = jnp.concatenate(
        [cos_x * cos_h - sin_x * sin_h, cos_x * sin_h + sin_x * alt_h], axis=0
    )
    return back(inv, product)


def forward_kernel(valid_ref, qkv_ref, short_ref, long_ref, fwd_ref, inv_ref, *refs):
    mix_ref, turned_ref, q_ref, k_ref, v_ref, conv_ref, gate_ref, ext_ref = refs[-8:]
    valid = valid_ref[0]
    ext_ref[:, 0:RIM] = jnp.zeros((3, RIM, LANES), F32)
    for start in range(0, ROWS, STEP):
        live = live_rows(valid, start, STEP)
        for stream in range(3):
            ext_ref[stream, RIM + start : RIM + start + STEP] = (
                qkv_ref[stream, start : start + STEP].astype(F32) * live
            )
    for start in range(0, ROWS, STEP):
        k_side = filtered(short_ref, ext_ref, 1, RIM + start, STEP)
        v_side = filtered(short_ref, ext_ref, 2, RIM + start, STEP)
        k_ref[start : start + STEP] = k_side
        v_ref[start : start + STEP] = v_side
        q_ref[start : start + STEP] = filtered(short_ref, ext_ref, 0, RIM + start, STEP)
        gate_ref[start : start + STEP] = (k_side * v_side).astype(BF16)
    fwd = fwd_ref[...]
    inv = inv_ref[...]
    taps = filter_spectrum(fwd, long_ref[...])
    sign = signs(2 * LONG)
    before = spectrum(fwd, gate_ref[LONG : 2 * LONG])
    for start in range(2 * LONG, ROWS, LONG):
        now = spectrum(fwd, gate_ref[start : start + LONG])
        conv = convolve(before, now, sign, inv, *taps)
        before = now
        conv_ref[start : start + LONG] = conv
        mix_in = live_rows(valid, start, LONG) * q_ref[start : start + LONG] * conv
        mix_ref[start : start + LONG] = mix_in.astype(BF16)
        turned_ref[:, start : start + LONG] = mix_in.T.astype(BF16)


def finish_kernel(
    valid_ref, qkv_ref, halo_ref, short_ref, long_ref, fwd_ref, inv_ref, q_in, k_in, v_in, gate_in, *refs
):
    mix_ref, turned_ref, q_ref, k_ref, v_ref, conv_ref, ext_ref, gate_ref = refs[-8:]
    valid = valid_ref[0]
    ext_ref[0, TAIL - RIM : TAIL] = halo_ref[0:RIM].astype(F32)
    ext_ref[1, 0:TAIL] = halo_ref[RIM : RIM + TAIL].astype(F32)
    ext_ref[2, 0:TAIL] = halo_ref[RIM + TAIL : RIM + 2 * TAIL].astype(F32)
    live = live_rows(valid, 0, RIM)
    for stream in range(3):
        ext_ref[stream, TAIL : TAIL + RIM] = qkv_ref[stream].astype(F32) * live
    for start in range(0, LONG, STEP):
        k_side = filtered(short_ref, ext_ref, 1, RIM + start, STEP)
        v_side = filtered(short_ref, ext_ref, 2, RIM + start, STEP)
        gate_ref[start : start + STEP] = (k_side * v_side).astype(BF16)
    q_rim = filtered(short_ref, ext_ref, 0, TAIL, RIM)
    k_rim = filtered(short_ref, ext_ref, 1, TAIL, RIM)
    v_rim = filtered(short_ref, ext_ref, 2, TAIL, RIM)
    q_ref[...] = q_rim
    k_ref[...] = k_rim
    v_ref[...] = v_rim
    gate_ref[LONG : LONG + RIM] = (k_rim * v_rim).astype(BF16)
    gate_ref[LONG + RIM : 3 * LONG] = gate_in[RIM:]
    fwd = fwd_ref[...]
    inv = inv_ref[...]
    taps = filter_spectrum(fwd, long_ref[...])
    sign = signs(2 * LONG)
    before = spectrum(fwd, gate_ref[0:LONG])
    for start in range(0, 2 * LONG, LONG):
        now = spectrum(fwd, gate_ref[LONG + start : 2 * LONG + start])
        conv = convolve(before, now, sign, inv, *taps)
        before = now
        conv_ref[start : start + LONG] = conv
        q_side = q_in[start : start + LONG]
        if start == 0:
            q_side = jnp.concatenate([q_rim, q_side[RIM:]], axis=0)
        mix_in = live_rows(valid, start, LONG) * q_side * conv
        mix_ref[start : start + LONG] = mix_in.astype(BF16)
        turned_ref[:, start : start + LONG] = mix_in.T.astype(BF16)


def backward_kernel(
    valid_ref, dconv_ref, msg_ref, dq_ref, k_ref, v_ref, short_ref, long_ref, fwd_ref, inv_ref,
    *refs,
):
    out_ref, ext_ref, gate_ref = refs[-3:]
    valid = valid_ref[0]
    fwd = fwd_ref[...]
    inv = inv_ref[...]
    gate_ref[0:TAIL] = msg_ref[0:TAIL]
    gate_ref[TAIL : 2 * LONG] = jnp.zeros((2 * LONG - TAIL, LANES), BF16)
    cos_h, sin_h, alt_h = filter_spectrum(fwd, long_ref[...])
    sign = signs(2 * LONG)
    blocks = ROWS // LONG
    ext_ref[0, 0:ROWS] = dq_ref[...]
    ext_ref[0, ROWS : ROWS + RIM] = msg_ref[TAIL : TAIL + RIM].astype(F32)
    now = spectrum(fwd, dconv_ref[0:LONG])
    for block in range(blocks + 1):
        start = block * LONG
        if block + 1 < blocks:
            after = spectrum(fwd, dconv_ref[start + LONG : start + 2 * LONG])
        else:
            rim = (block + 1 - blocks) * LONG
            after = spectrum(fwd, gate_ref[rim : rim + LONG])
        window = now + sign * after
        now = after
        cos_x, sin_x = window[:LONG], window[LONG:]
        product = jnp.concatenate(
            [cos_x * cos_h + sin_x * sin_h, sin_x * alt_h - cos_x * sin_h], axis=0
        )
        gated = back(inv, product)
        if block < blocks:
            ext_ref[1, start : start + LONG] = gated * v_ref[start : start + LONG]
            ext_ref[2, start : start + LONG] = gated * k_ref[start : start + LONG]
        else:
            rim = gated[:RIM]
            v_rim = msg_ref[TAIL + RIM : TAIL + 2 * RIM].astype(F32)
            k_rim = msg_ref[TAIL + 2 * RIM : TAIL + 3 * RIM].astype(F32)
            ext_ref[1, ROWS : ROWS + RIM] = rim * v_rim
            ext_ref[2, ROWS : ROWS + RIM] = rim * k_rim
    for start in range(0, ROWS, STEP):
        live = live_rows(valid, start, STEP)
        for stream in range(3):
            total = short_ref[stream, 0:1] * ext_ref[stream, start : start + STEP]
            for tap in range(1, SHORT):
                total += short_ref[stream, tap : tap + 1] * ext_ref[stream, start + tap : start + tap + STEP]
            out_ref[stream, start : start + STEP] = (total * live).astype(BF16)


def params(mib=20):
    return pltpu.CompilerParams(vmem_limit_bytes=mib * 2**20)


def cost(flops, moved):
    return pl.CostEstimate(flops=flops, bytes_accessed=moved, transcendentals=0)


SMEM = pl.BlockSpec(memory_space=pltpu.SMEM)
VMEM = pl.BlockSpec(memory_space=pltpu.VMEM)
ANY = pl.BlockSpec(memory_space=pl.ANY)


def lane_spec(*lead):
    return pl.BlockSpec(lead + (LANES,), lambda i: (0,) * len(lead) + (i,))


def whole(*shape):
    return pl.BlockSpec(shape, lambda i: (0,) * len(shape))


def forward_shapes():
    side = jax.ShapeDtypeStruct((ROWS, CH), F32)
    square = jax.ShapeDtypeStruct((ROWS, CH), BF16)
    return [square, square, side, side, side, side]


def run_forward(info, streams, short, long_taps, fwd, inv, after=()):
    return pl.pallas_call(
        forward_kernel,
        grid=(CH // LANES,),
        in_specs=[
            SMEM, lane_spec(3, ROWS), lane_spec(3, SHORT), lane_spec(LONG),
            whole(2 * LONG, 2 * LONG), whole(2 * LONG, 2 * LONG),
        ] + [ANY] * len(after),
        out_specs=[lane_spec(ROWS), pl.BlockSpec((LANES, ROWS), lambda i: (i, 0))] + [lane_spec(ROWS)] * 5,
        out_shape=forward_shapes() + [jax.ShapeDtypeStruct((ROWS, CH), BF16)],
        scratch_shapes=[pltpu.VMEM((3, RIM + ROWS, LANES), F32)],
        compiler_params=params(),
        cost_estimate=cost(1000, 1000),
        name="forward",
    )(info, streams, short, long_taps, fwd, inv, *after)


def run_finish(info, streams, halo, short, long_taps, fwd, inv, own, after=()):
    mix_in, turned, q_side, k_side, v_side, conv, gate = own
    top = lane_spec(2 * LONG)
    rim = lane_spec(RIM)
    return pl.pallas_call(
        finish_kernel,
        grid=(CH // LANES,),
        in_specs=[
            SMEM, lane_spec(3, RIM), lane_spec(RIM + 2 * TAIL), lane_spec(3, SHORT), lane_spec(LONG),
            whole(2 * LONG, 2 * LONG), whole(2 * LONG, 2 * LONG), top, rim, rim, top,
        ] + [ANY] * (3 + len(after)),
        out_specs=[top, pl.BlockSpec((LANES, 2 * LONG), lambda i: (i, 0)), rim, rim, rim, top],
        out_shape=forward_shapes(),
        input_output_aliases={7: 2, 8: 3, 9: 4, 11: 0, 12: 1, 13: 5},
        scratch_shapes=[
            pltpu.VMEM((3, TAIL + RIM, LANES), F32),
            pltpu.VMEM((3 * LONG, LANES), BF16),
        ],
        compiler_params=params(),
        cost_estimate=cost(1000, 1000),
        name="finish",
    )(info, streams, halo, short, long_taps, fwd, inv, q_side, k_side, v_side, gate, mix_in, turned, conv, *after)


def run_backward(valid, d_conv, msg, d_q, k_side, v_side, short, long_taps, fwd, inv, after=()):
    return pl.pallas_call(
        backward_kernel,
        grid=(CH // LANES,),
        in_specs=[
            SMEM, lane_spec(ROWS), lane_spec(TAIL + 3 * RIM), lane_spec(ROWS), lane_spec(ROWS),
            lane_spec(ROWS), lane_spec(3, SHORT), lane_spec(LONG),
            whole(2 * LONG, 2 * LONG), whole(2 * LONG, 2 * LONG),
        ] + [ANY] * len(after),
        out_specs=lane_spec(3, ROWS),
        out_shape=jax.ShapeDtypeStruct((3, ROWS, CH), BF16),
        scratch_shapes=[
            pltpu.VMEM((3, ROWS + RIM, LANES), F32),
            pltpu.VMEM((2 * LONG, LANES), BF16),
        ],
        compiler_params=params(),
        cost_estimate=cost(1000, 1000),
        name="backward",
    )(valid, d_conv, msg, d_q, k_side, v_side, short, long_taps, fwd, inv, *after)


def project_kernel(order_ref, mix_ref, weight_ref, *refs):
    out_ref = refs[-1]
    out_ref[0] = jnp.dot(mix_ref[...], weight_ref[...], preferred_element_type=F32).astype(BF16)


def block_at(other):
    return lambda i, info: (0, info[2 + other + 2 * ((0x0132 >> (4 * i)) & 15)])


def run_project(info, mix_in, weight, after=()):
    count = 4
    return pl.pallas_call(
        project_kernel,
        grid_spec=pltpu.PrefetchScalarGridSpec(
            num_scalar_prefetch=1,
            grid=(count,),
            in_specs=[
                pl.BlockSpec((ROWS, CH), lambda i, order: (0, 0)),
                pl.BlockSpec((CH, CH), block_at(1)),
            ] + [ANY] * len(after),
            out_specs=pl.BlockSpec((1, ROWS, CH), lambda i, order: (i, 0, 0)),
        ),
        out_shape=jax.ShapeDtypeStruct((count, ROWS, CH), BF16),
        compiler_params=params(),
        cost_estimate=cost(1000, 1000),
        name="project",
    )(info, mix_in, weight, *after)


def project_add_kernel(order_ref, mix_ref, weight_ref, other_ref, *refs):
    one_ref, two_ref, three_ref, own_ref = refs[-4:]
    step = pl.program_id(0)
    total = jnp.dot(mix_ref[...], weight_ref[...], preferred_element_type=F32)
    total += other_ref[0].astype(F32)
    for place, ref in enumerate((one_ref, two_ref, three_ref, own_ref)):

        @pl.when(step == place)
        def _(ref=ref):
            ref[...] = total.astype(ref.dtype)


def run_project_add(info, mix_in, weight, other, after=()):
    piece = jax.ShapeDtypeStruct((ROWS, CH), BF16)
    fixed = pl.BlockSpec((ROWS, CH), lambda i, order: (0, 0))
    return pl.pallas_call(
        project_add_kernel,
        grid_spec=pltpu.PrefetchScalarGridSpec(
            num_scalar_prefetch=1,
            grid=(4,),
            in_specs=[
                fixed,
                pl.BlockSpec((CH, CH), block_at(0)),
                pl.BlockSpec((1, ROWS, CH), lambda i, order: (i, 0, 0)),
            ] + [ANY] * len(after),
            out_specs=[fixed] * 4,
        ),
        out_shape=[piece, piece, piece, jax.ShapeDtypeStruct((ROWS, CH), F32)],
        compiler_params=params(),
        cost_estimate=cost(1000, 1000),
        name="project_add",
    )(info, mix_in, weight, other, *after)


def prepare_kernel(info_ref, qkv_ref, cot_ref, tail_ref, *refs):
    live = live_rows(info_ref[0], ROWS - TAIL, TAIL)[:, 0:1]
    place = 0
    for stream, rows in ((0, RIM), (1, TAIL), (2, TAIL)):
        masked = qkv_ref[stream, TAIL - rows :].astype(F32) * live[TAIL - rows :]
        tail_ref[place : place + rows] = masked.astype(BF16)
        place += rows
    for ahead, ref in enumerate(refs):
        column = pl.multiple_of(lax.rem(info_ref[1] + ahead, NX) * LANES, LANES)
        ref[...] = cot_ref[:, pl.ds(column, LANES)]


def run_prepare(info, streams, cotangent):
    return pl.pallas_call(
        prepare_kernel,
        in_specs=[SMEM, VMEM, VMEM],
        out_specs=[VMEM] * (1 + NX),
        out_shape=[jax.ShapeDtypeStruct((RIM + 2 * TAIL, CH), BF16)]
        + [jax.ShapeDtypeStruct((ROWS, LANES), BF16)] * NX,
        compiler_params=params(),
        cost_estimate=cost(1000, 1000),
        name="prepare",
    )(info, streams[:, ROWS - TAIL :], cotangent)


def outer_kernel(info_ref, *refs):
    turned, mine, theirs, outputs, work_ref = refs[0], refs[1], refs[2], refs[-1 - NZ : -1], refs[-1]
    for pair in range(NZ // 2):
        total = None
        for ahead in range(NX):
            both = jnp.concatenate([mine[pair, ahead], theirs[pair, ahead]], axis=1)
            part = jnp.dot(turned[lax.rem(info_ref[1] + NX - ahead, NX)], both, preferred_element_type=F32)
            total = part if total is None else total + part
        work_ref[info_ref[10 + 2 * pair]] = total[:, :LANES]
        work_ref[info_ref[11 + 2 * pair]] = total[:, LANES:]
    for ahead, ref in enumerate(outputs):
        ref[...] = work_ref[ahead].astype(ref.dtype)


def run_outer(info, turned, slabs, slabs_other, after=()):
    sent = jax.ShapeDtypeStruct((CH, LANES), BF16)
    return pl.pallas_call(
        outer_kernel,
        in_specs=[SMEM] + [VMEM] * 3 + [ANY] * len(after),
        out_specs=[VMEM] * NZ,
        out_shape=[jax.ShapeDtypeStruct((CH, LANES), F32)] + [sent] * (NZ - 1),
        scratch_shapes=[pltpu.VMEM((NZ, CH, LANES), F32)],
        compiler_params=params(),
        cost_estimate=cost(1000, 1000),
        name="outer",
    )(info, turned, slabs, slabs_other, *after)


def d_mix_kernel(info_ref, weight_ref, mine, theirs, q_ref, k_ref, v_ref, conv_ref, *refs):
    dconv_ref, dq_ref, msg_ref = refs[-3:]
    total = None
    for slot in range(2 * NY):
        column = pl.multiple_of(info_ref[2 + slot] * CH, CH)
        piece = (mine, theirs)[slot % 2][slot // 2]
        part = lax.dot_general(
            piece, weight_ref[:, pl.ds(column, CH)], (((1,), (1,)), ((), ())),
            preferred_element_type=F32,
        )
        total = part if total is None else total + part
    row = lax.broadcasted_iota(jnp.int32, (ROWS, CH), 0)
    d_mix = jnp.where(row < info_ref[0], total, 0.0)
    d_conv = (d_mix * q_ref[...]).astype(BF16)
    d_q = d_mix * conv_ref[...]
    dconv_ref[...] = d_conv
    dq_ref[...] = d_q
    msg_ref[0:TAIL] = d_conv[:TAIL]
    msg_ref[TAIL : TAIL + RIM] = d_q[:RIM].astype(BF16)
    msg_ref[TAIL + RIM : TAIL + 2 * RIM] = v_ref[0:RIM].astype(BF16)
    msg_ref[TAIL + 2 * RIM : TAIL + 3 * RIM] = k_ref[0:RIM].astype(BF16)


def run_d_mix(info, weight, mine, theirs, sides, after=()):
    return pl.pallas_call(
        d_mix_kernel,
        in_specs=[SMEM] + [VMEM] * 7 + [ANY] * len(after),
        out_specs=[VMEM] * 3,
        out_shape=[
            jax.ShapeDtypeStruct((ROWS, CH), BF16), jax.ShapeDtypeStruct((ROWS, CH), F32),
            jax.ShapeDtypeStruct((TAIL + 3 * RIM, CH), BF16),
        ],
        compiler_params=params(),
        cost_estimate=cost(1000, 1000),
        name="d_mix",
    )(info, weight, mine, theirs, *sides, *after)


def ctx_pairs(ahead_z, ahead_x):
    return [
        (z * NX + x, (z + ahead_z) % NZ * NX + (x + ahead_x) % NX) for z in range(NZ) for x in range(NX)
    ]


def along_x(array, ahead):
    return lax.ppermute(array, "ctx", ctx_pairs(0, ahead))


def along_z(array, ahead):
    return lax.ppermute(array, "ctx", ctx_pairs(ahead, 0))


def along_y(array, ahead):
    pairs = [(2 * y + core, 2 * ((y + ahead) % NY) + core) for y in range(NY) for core in range(2)]
    return lax.ppermute(array, "tp", pairs)


def other_core(array):
    return lax.ppermute(array, "tp", [(i, i ^ 1) for i in range(2 * NY)])


def neighbour(array, by):
    count = NZ * NX
    return lax.ppermute(array, "ctx", [(i, i + by) for i in range(count) if 0 <= i + by < count])


def local(qkv, short_filter, long_filter, out_weight, cotangent, valid_len):
    forward_table, causal_table, anti_table = (jnp.asarray(table) for table in tables())
    ctx, tp = lax.axis_index("ctx"), lax.axis_index("tp")
    z, x, y, core = ctx >> 2, ctx & 3, tp >> 1, tp & 1
    ahead = jnp.array([0, 0, -1, -1, 1, 1, 2, 2], jnp.int32)
    other = jnp.array([0, 1, 0, 1, 0, 1, 0, 1], jnp.int32)
    blocks = (((y + ahead) & 3) << 1) + ((core + other) & 1)
    info = jnp.concatenate([valid_len, x[None].astype(jnp.int32), blocks, (blocks - z) & 7])
    streams = qkv.transpose(1, 0, 2)
    short = short_filter.transpose(1, 0, 2)

    tail, *quarters = run_prepare(info, streams, cotangent)
    halo = neighbour(tail, 1)
    first, second, third = (along_x(quarters[ahead], ahead) for ahead in (1, 2, 3))
    below, above = along_y(cotangent, 1), along_y(cotangent, -1)
    own = run_forward(info, streams, short, long_filter, forward_table, causal_table, (tail,))
    first, second, third, halo, *own = lax.optimization_barrier([first, second, third, halo, *own])
    slab = jnp.stack([quarters[0], first, second, third])
    slabs = [slab] + [along_y(slab, ahead) for ahead in (1, -1, 2)]
    mix_in, turned, q_side, k_side, v_side, conv = run_finish(
        info, streams, halo, short, long_filter, forward_table, causal_table, own, (slab, below)
    )
    copies = jnp.broadcast_to(turned[None], (NX, CH, ROWS))
    turned = lax.all_to_all(
        copies, "ctx", 0, 0, axis_index_groups=[[z * NX + x for x in range(NX)] for z in range(NZ)], tiled=True
    )
    turned, above, mix_in, cotangent, *slabs = lax.optimization_barrier(
        [turned, above, mix_in, cotangent, *slabs]
    )
    slabs = jnp.stack(slabs)
    slabs_other = other_core(slabs)
    far = along_y(cotangent, 2)
    given = run_project(info, mix_in, out_weight)
    taken = other_core(given)
    total, *sent = run_outer(info, turned, slabs, slabs_other, (taken,))
    sums = [along_z(sent[ahead - 1], ahead) for ahead in (1, 7, 2, 6)]
    one, two, three, own_out = run_project_add(info, mix_in, out_weight, taken, (total,))
    arrived = [along_y(one, 1), along_y(three, 3)]
    far, below, above, sums[0], sums[1], two = lax.optimization_barrier(
        (far, below, above, sums[0], sums[1], two)
    )
    cots = jnp.stack([cotangent, below, above, far])
    cots_other = other_core(cots)
    d_conv, d_q, msg = run_d_mix(info, out_weight, cots, cots_other, (q_side, k_side, v_side, conv))
    msg = neighbour(msg, -1)
    arrived.append(along_y(two, 2))
    msg, *rest = lax.optimization_barrier([msg] + [sent[ahead - 1] for ahead in (3, 5, 4)])
    sums += [along_z(array, ahead) for array, ahead in zip(rest, (3, 5, 4))]

    d_streams = run_backward(
        info, d_conv, msg, d_q, k_side, v_side, short, long_filter, forward_table, anti_table
    )
    d_qkv = d_streams.transpose(1, 0, 2)
    mixed = own_out
    for array in arrived:
        mixed = mixed + array.astype(F32)
    mixed = mixed.astype(BF16)
    for array in sums:
        total = total + array.astype(F32)
    d_weight = total * (1.0 / jnp.sqrt(jnp.float32(ROWS * NZ * NX)))
    return mixed, d_qkv, d_weight


def solution(mesh):
    in_specs = (
        P("ctx", None, "tp"),
        P(None, None, "tp"),
        P(None, "tp"),
        P("tp", None),
        P("ctx", "tp"),
        P("ctx"),
    )
    out_specs = (P("ctx", "tp"), P("ctx", None, "tp"), P("tp", "ctx"))
    return jax.shard_map(local, mesh=mesh, in_specs=in_specs, out_specs=out_specs, check_vma=False)
```

time: 190 us -> 147 us (0.77)
  the two profiles are of different devices: /device:TPU:194 before, /device:TPU:62 now
where the time goes in v2:
time: 147 us
  starting transfers between devices  49.9 us (34%)
  waiting for transfers between devices  45.1 us (31%)
  Pallas kernels  32.3 us (22%)
  local copies, waits for them, and re-layouts  12.1 us (8%)
  other arithmetic  5.57 us (4%)
  between operations  1.68 us (1%)
    ppermute x9, waiting for transfers between devices, along_y(): return lax.ppermute(array, 'tp', pairs)  33.4 us
    ppermute x7, starting transfers between devices, along_z(): return lax.ppermute(array, 'ctx', ctx_pairs(ahead, 0))  21.4 us
    ppermute x9, starting transfers between devices, along_y(): return lax.ppermute(array, 'tp', pairs)  10.9 us
    unnamed x48, local copies, waits for them, and re-layouts  9.55 us
    pallas_call x1, Pallas kernels, run_backward(): pl.pallas_call(backward_kernel, grid=(CH // LANES,), in_specs=[SMEM, lane...  8.8 us
    all_to_all x1, starting transfers between devices, local(): lax.all_to_all(copies, 'ctx', 0, 0, axis_index_groups=[[z * NX + x for x...  7.73 us
    ppermute x2, starting transfers between devices, neighbour(): lax.ppermute(array, 'ctx', [(i, i + by) for i in range(count) if 0 <= i +...  6.64 us
    pallas_call x1, Pallas kernels, run_forward(): pl.pallas_call(forward_kernel, grid=(CH // LANES,), in_specs=[SMEM, lane_...  5.91 us
  transfers between devices with their start and end apart: 25, of which 10 were waited for; matrix products, arithmetic and copies ran while one was open for 3% of the time, Pallas kernels for 17%

profile of v2, /device:TPU:62, one launch (start us, length us, event | category | flops | bytes accessed | tf_op | source)
XLA Modules:
  0.0 146.6 jit_solution(10165462595043676291)
XLA Ops:
  5.2 3.7 %collective-permute-start.3 = (bf16[304,512]{1,0:T(8,128)(2,1)S(1)}, bf16[304,512]{1,0:T(8,128)(2,1)S(1)}, u32[]{:S(2)}, u32[]{:S(2)}) collective-permute-start(bf16[304,512]{1,0:T(8,128)(2,1)S(1)} %get-tuple-element.68.refs_0_), channel_id=1, source_target_pairs={{0,8},{8,16},{16,24},{24,32},{32,40},{40,48},{48,56},{56,64},{64,7... | collective-permute-start | bytes 933896 | tf_op jit(solution)/shard_map/ppermute | solution.py:481
  9.2 2.1 %collective-permute-start.1 = (bf16[512,128]{1,0:T(8,128)(2,1)S(1)}, bf16[512,128]{1,0:T(8,128)(2,1)S(1)}, u32[]{:S(2)}, u32[]{:S(2)}) collective-permute-start(bf16[512,128]{1,0:T(8,128)(2,1)S(1)} %get-tuple-element.66), channel_id=1, source_target_pairs={{0,16},{8,24},{16,0},{24,8},{32,48},{40,56},{48,32},{56,40},{64,80... | collective-permute-start | bytes 393224 | tf_op jit(solution)/shard_map/ppermute | solution.py:463
  15.1 5.9 %forward.1 = (bf16[512,512]{1,0:T(8,128)(2,1)S(1)}, bf16[512,512]{1,0:T(8,128)(2,1)S(1)}, f32[512,512]{1,0:T(8,128)S(1)}, f32[512,512]{1,0:T(8,128)S(1)}, f32[51...) custom-call(s32[18]{0:T(128)S(1)} %pad_add_fusion.info_ref.valid_ref.order_ref, ...), custom_call_target="tpu_custom_call" | custom-call | flops 1000 | bytes 1000 | tf_op jit(solution)/shard_map/forward/pallas_call | solution.py:241
  21.1 4.4 %finish.1 = (bf16[512,512]{1,0:T(8,128)(2,1)S(1)}, bf16[512,512]{1,0:T(8,128)(2,1)S(1)}, f32[512,512]{1,0:T(8,128)S(1)}, f32[512,512]{1,0:T(8,128)S(1)}, f32[512,512]{1,0:T(8,128)S(1)}, /*index=5*/f32[512,512]{1,0:T(8,128)S(1)}) custom-call(s32[18]{0:T(128)S(1)} %pad_add_fusion.info_ref.valid_ref, ...), custom_call_target="tpu_custom_call", output_to_operand_aliasing={{2}: (7, {}), {3}: (8, {}), {4}: (9, {}), {0}: (11, {}), {1... | custom-call | flops 1000 | bytes 1000 | tf_op jit(solution)/shard_map/finish/pallas_call | solution.py:261
  29.0 7.7 %all-to-all-start = ((bf16[4,512,512]{2,1,0:T(8,128)(2,1)}), bf16[4,512,512]{2,1,0:T(8,128)(2,1)}, u32[]{:S(2)}, u32[]{:S(2)}) async-start(bf16[4,512,512]{2,1,0:T(8,128)(2,1)} %broadcast_in_dim.10), calls=%async_computation | async-start | bytes 4194304 | tf_op jit(solution)/shard_map/all_to_all | solution.py:507
  40.8 2.1 %collective-permute-start.6 = (bf16[4,512,128]{2,1,0:T(8,128)(2,1)S(1)}, bf16[4,512,128]{2,1,0:T(8,128)(2,1)}, u32[]{:S(2)}, u32[]{:S(2)}) collective-permute-start(bf16[4,512,128]{2,1,0:T(8,128)(2,1)S(1)} %pad_maximum_fusion.2.refs_3_), channel_id=1, source_target_pairs={{0,2},{1,3},{2,4},{3,5},{4,6},{5,7},{6,0},{7,1},{8,10},{9,11},{10,... | collective-permute-start | bytes 1572872 | tf_op jit(solution)/shard_map/ppermute | solution.py:472
  42.9 21.3 %collective-permute-done.5 = bf16[512,512]{1,0:T(8,128)(2,1)S(1)} collective-permute-done((bf16[512,512]{1,0:T(8,128)(2,1)}, bf16[512,512]{1,0:T(8,128)(2,1)S(1)}, u32[]{:S(2)}, u32[]{:S(2)}) %collective-permute-start.5) | collective-permute-done | bytes 524320 | tf_op jit(solution)/shard_map/ppermute | solution.py:472
  64.3 8.7 %collective-permute-done.7 = bf16[4,512,128]{2,1,0:T(8,128)(2,1)S(1)} collective-permute-done((bf16[4,512,128]{2,1,0:T(8,128)(2,1)S(1)}, bf16[4,512,128]{2,1,0:T(8,128)(2,1)S(1)}, u32[]{:S(2)}, u32[]{:S(2)}) %collective-permute-start.7) | collective-permute-done | bytes 524320 | tf_op jit(solution)/shard_map/ppermute | solution.py:472
  73.7 2.2 %copy-done = bf16[512,4096]{1,0:T(8,128)(2,1)S(1)} copy-done((bf16[512,4096]{1,0:T(8,128)(2,1)S(1)}, bf16[512,4096]{1,0:T(8,128)(2,1)}, u32[]{:S(2)}) %copy-start) | copy-done | bytes 4194328
  75.9 2.5 %project.1 = bf16[4,512,512]{2,1,0:T(8,128)(2,1)S(1)} custom-call(s32[18]{0:T(128)S(1)} %pad_add_fusion.info_ref.valid_ref.order_ref, bf16[512,512]{1,0:T(8,128)(2,1)S(1)} %get-tuple-element.90.mix_ref, bf16[512,4096]{1,0:T(8,128)(2,1)S(1)} %copy-done), custom_call_target="tpu_custom_call" | custom-call | flops 1000 | bytes 1000 | tf_op jit(solution)/shard_map/project/pallas_call | solution.py:313
  82.7 3.0 %collective-permute-done.10.refs_2_ = bf16[4,4,512,128]{3,2,1,0:T(8,128)(2,1)S(1)} collective-permute-done((bf16[4,4,512,128]{3,2,1,0:T(8,128)(2,1)S(1)}, bf16[4,4,512,128]{3,2,1,0:T(8,128)(2,1)S(1)}, u32[]{:S(2)}, u32[]{:S(2)}) %collective-permute-start.10) | collective-permute-done | bytes 2097184 | tf_op jit(solution)/shard_map/ppermute | solution.py:476
  85.7 4.3 %outer.1 = (f32[512,128]{1,0:T(8,128)S(1)}, bf16[512,128]{1,0:T(8,128)(2,1)S(1)}, bf16[512,128]{1,0:T(8,128)(2,1)S(1)}, bf16[512,128]{1,0:T(8,128)(2,1)S(1)}, bf...) custom-call(s32[18]{0:T(128)S(1)} %pad_add_fusion.info_ref.valid_ref, ...), custom_call_target="tpu_custom_call" | custom-call | flops 1000 | bytes 1000 | tf_op jit(solution)/shard_map/outer/pallas_call | solution.py:406
  90.0 2.0 %collective-permute-start.14 = (bf16[512,128]{1,0:T(8,128)(2,1)S(1)}, bf16[512,128]{1,0:T(8,128)(2,1)S(1)}, u32[]{:S(2)}, u32[]{:S(2)}) collective-permute-start(bf16[512,128]{1,0:T(8,128)(2,1)S(1)} %get-tuple-element.102), channel_id=1, source_target_pairs={{0,32},{8,40},{16,48},{24,56},{32,64},{40,72},{48,80},{56,88},{64,... | collective-permute-start | bytes 393224 | tf_op jit(solution)/shard_map/ppermute | solution.py:467
  92.1 2.8 %project_add.1 = (bf16[512,512]{1,0:T(8,128)(2,1)S(1)}, bf16[512,512]{1,0:T(8,128)(2,1)S(1)}, bf16[512,512]{1,0:T(8,128)(2,1)S(1)}, f32[512,512]{1,0:T(8,128)S(1)}) custom-call(s32[18]{0:T(128)S(1)} %pad_add_fusion.info_ref.valid_ref.order_ref, bf16[512,512]{1,0:T(8,128)(2,1)S(1)} %get-tuple-element.90.mix_ref, bf16[512,4096]{1,0:T(8,128)(2,1)S(1)} %copy-done.1, ...), custom_call_target="tpu_custom_call" | custom-call | flops 1000 | bytes 1000 | tf_op jit(solution)/shard_map/project_add/pallas_call | solution.py:346
  103.3 2.9 %d_mix.1 = (bf16[512,512]{1,0:T(8,128)(2,1)S(1)}, f32[512,512]{1,0:T(8,128)S(1)}, bf16[192,512]{1,0:T(8,128)(2,1)S(1)}) custom-call(s32[18]{0:T(128)S(1)} %pad_add_fusion.info_ref.valid_ref.order_ref, bf16[512,4096]{1,0:T(8,128)(2,1)S(1)} %copy-done.1, bf16[4,512,512]{2,1,0:T(8,128)(2,1)S(1)} %pad_maximum_fusion.1.mine, ...), custom_call_target="tpu_custom_call" | custom-call | flops 1000 | bytes 1000 | tf_op jit(solution)/shard_map/d_mix/pallas_call | solution.py:442
  106.3 2.9 %collective-permute-start.18 = (bf16[192,512]{1,0:T(8,128)(2,1)S(1)}, bf16[192,512]{1,0:T(8,128)(2,1)S(1)}, u32[]{:S(2)}, u32[]{:S(2)}) collective-permute-start(bf16[192,512]{1,0:T(8,128)(2,1)S(1)} %get-tuple-element.114), channel_id=1, source_target_pairs={{8,0},{16,8},{24,16},{32,24},{40,32},{48,40},{56,48},{64,56},{72,6... | collective-permute-start | bytes 589832 | tf_op jit(solution)/shard_map/ppermute | solution.py:481
  109.2 5.4 %collective-permute-start.19 = (bf16[512,128]{1,0:T(8,128)(2,1)S(1)}, bf16[512,128]{1,0:T(8,128)(2,1)S(1)}, u32[]{:S(2)}, u32[]{:S(2)}) collective-permute-start(bf16[512,128]{1,0:T(8,128)(2,1)S(1)} %get-tuple-element.122), channel_id=1, source_target_pairs={{0,64},{8,72},{16,80},{24,88},{32,96},{40,104},{48,112},{56,120},{... | collective-permute-start | bytes 393224 | tf_op jit(solution)/shard_map/ppermute | solution.py:467
  114.6 2.8 %collective-permute-done.18.msg_ref = bf16[192,512]{1,0:T(8,128)(2,1)S(1)} collective-permute-done((bf16[192,512]{1,0:T(8,128)(2,1)S(1)}, bf16[192,512]{1,0:T(8,128)(2,1)S(1)}, u32[]{:S(2)}, u32[]{:S(2)}) %collective-permute-start.18) | collective-permute-done | bytes 196640 | tf_op jit(solution)/shard_map/ppermute | solution.py:481
  118.3 5.6 %collective-permute-start.21 = (bf16[512,128]{1,0:T(8,128)(2,1)S(1)}, bf16[512,128]{1,0:T(8,128)(2,1)S(1)}, u32[]{:S(2)}, u32[]{:S(2)}) collective-permute-start(bf16[512,128]{1,0:T(8,128)(2,1)S(1)} %get-tuple-element.124), channel_id=1, source_target_pairs={{0,96},{8,104},{16,112},{24,120},{32,128},{40,136},{48,144},{56,15... | collective-permute-start | bytes 393224 | tf_op jit(solution)/shard_map/ppermute | solution.py:467
  123.9 2.2 %collective-permute-done.12 = bf16[512,512]{1,0:T(8,128)(2,1)S(1)} collective-permute-done((bf16[512,512]{1,0:T(8,128)(2,1)S(1)}, bf16[512,512]{1,0:T(8,128)(2,1)S(1)}, u32[]{:S(2)}, u32[]{:S(2)}) %collective-permute-start.12) | collective-permute-done | bytes 524320 | tf_op jit(solution)/shard_map/ppermute | solution.py:472
  126.0 4.5 %collective-permute-start.22 = (bf16[512,128]{1,0:T(8,128)(2,1)S(1)}, bf16[512,128]{1,0:T(8,128)(2,1)S(1)}, u32[]{:S(2)}, u32[]{:S(2)}) collective-permute-start(bf16[512,128]{1,0:T(8,128)(2,1)S(1)} %get-tuple-element.125), channel_id=1, source_target_pairs={{0,160},{8,168},{16,176},{24,184},{32,192},{40,200},{48,208},{56,2... | collective-permute-start | bytes 393224 | tf_op jit(solution)/shard_map/ppermute | solution.py:467
  130.5 2.8 %collective-permute-start.23 = (bf16[512,128]{1,0:T(8,128)(2,1)S(1)}, bf16[512,128]{1,0:T(8,128)(2,1)S(1)}, u32[]{:S(2)}, u32[]{:S(2)}) collective-permute-start(bf16[512,128]{1,0:T(8,128)(2,1)S(1)} %get-tuple-element.126), channel_id=1, source_target_pairs={{0,128},{8,136},{16,144},{24,152},{32,160},{40,168},{48,176},{56,1... | collective-permute-start | bytes 393224 | tf_op jit(solution)/shard_map/ppermute | solution.py:467
  134.5 8.8 %backward.1 = bf16[3,512,512]{2,1,0:T(8,128)(2,1)} custom-call(s32[18]{0:T(128)S(1)} %pad_add_fusion.info_ref.valid_ref.order_ref, bf16[512,512]{1,0:T(8,128)(2,1)S(1)} %get-tuple-element.113.dconv_ref, bf16[192,512]{1,0:T(8,128)(2,1)S(1)} %collective-permute-done.18.msg_ref, f32[512,512]{1,0:T(8,128)S(1)} %get-tuple-element.119.dq_ref, ...), custom_call_target="tpu_custom_call" | custom-call | flops 1000 | bytes 1000 | tf_op jit(solution)/shard_map/backward/pallas_call | solution.py:282
  143.3 2.5 %collective-permute-done.23 = bf16[512,128]{1,0:T(8,128)(2,1)S(1)} collective-permute-done((bf16[512,128]{1,0:T(8,128)(2,1)S(1)}, bf16[512,128]{1,0:T(8,128)(2,1)S(1)}, u32[]{:S(2)}, u32[]{:S(2)}) %collective-permute-start.23) | collective-permute-done | bytes 131104 | tf_op jit(solution)/shard_map/ppermute | solution.py:467
  (91 shorter events, 31.8 us)
Async XLA Ops:
  0.6 20.5 %collective-permute-start.4 = (bf16[512,512]{1,0:T(8,128)(2,1)}, bf16[512,512]{1,0:T(8,128)(2,1)}, u32[]{:S(2)}, u32[]{:S(2)}) collective-permute-start(bf16[512,512]{1,0:T(8,128)(2,1)} %cot_ref.1), channel_id=1, source_target_pairs={{0,2},{1,3},{2,4},{3,5},{4,6},{5,7},{6,0},{7,1},{8,10},{9,11},{10,... | collective-permute-start | bytes 1572872 | tf_op jit(solution)/shard_map/ppermute | solution.py:472
  5.2 15.8 %collective-permute-start.3 = (bf16[304,512]{1,0:T(8,128)(2,1)S(1)}, bf16[304,512]{1,0:T(8,128)(2,1)S(1)}, u32[]{:S(2)}, u32[]{:S(2)}) collective-permute-start(bf16[304,512]{1,0:T(8,128)(2,1)S(1)} %get-tuple-element.68.refs_0_), channel_id=1, source_target_pairs={{0,8},{8,16},{16,24},{24,32},{32,40},{40,48},{48,56},{56,64},{64,7... | collective-permute-start | bytes 933896 | tf_op jit(solution)/shard_map/ppermute | solution.py:481
  9.0 12.0 %collective-permute-start = (bf16[512,128]{1,0:T(8,128)(2,1)S(1)}, bf16[512,128]{1,0:T(8,128)(2,1)S(1)}, u32[]{:S(2)}, u32[]{:S(2)}) collective-permute-start(bf16[512,128]{1,0:T(8,128)(2,1)S(1)} %get-tuple-element.65), channel_id=1, source_target_pairs={{0,8},{8,16},{16,24},{24,0},{32,40},{40,48},{48,56},{56,32},{64,72... | collective-permute-start | bytes 393224 | tf_op jit(solution)/shard_map/ppermute | solution.py:463
  9.2 11.8 %collective-permute-start.1 = (bf16[512,128]{1,0:T(8,128)(2,1)S(1)}, bf16[512,128]{1,0:T(8,128)(2,1)S(1)}, u32[]{:S(2)}, u32[]{:S(2)}) collective-permute-start(bf16[512,128]{1,0:T(8,128)(2,1)S(1)} %get-tuple-element.66), channel_id=1, source_target_pairs={{0,16},{8,24},{16,0},{24,8},{32,48},{40,56},{48,32},{56,40},{64,80... | collective-permute-start | bytes 393224 | tf_op jit(solution)/shard_map/ppermute | solution.py:463
  11.3 9.7 %collective-permute-start.2 = (bf16[512,128]{1,0:T(8,128)(2,1)S(1)}, bf16[512,128]{1,0:T(8,128)(2,1)S(1)}, u32[]{:S(2)}, u32[]{:S(2)}) collective-permute-start(bf16[512,128]{1,0:T(8,128)(2,1)S(1)} %get-tuple-element.67), channel_id=1, source_target_pairs={{0,24},{8,0},{16,8},{24,16},{32,56},{40,32},{48,40},{56,48},{64,88... | collective-permute-start | bytes 393224 | tf_op jit(solution)/shard_map/ppermute | solution.py:463
  29.0 44.7 %all-to-all-start = ((bf16[4,512,512]{2,1,0:T(8,128)(2,1)}), bf16[4,512,512]{2,1,0:T(8,128)(2,1)}, u32[]{:S(2)}, u32[]{:S(2)}) async-start(bf16[4,512,512]{2,1,0:T(8,128)(2,1)} %broadcast_in_dim.10), calls=%async_computation | async-start | bytes 4194304 | tf_op jit(solution)/shard_map/all_to_all | solution.py:507
  36.7 27.5 %collective-permute-start.5 = (bf16[512,512]{1,0:T(8,128)(2,1)}, bf16[512,512]{1,0:T(8,128)(2,1)S(1)}, u32[]{:S(2)}, u32[]{:S(2)}) collective-permute-start(bf16[512,512]{1,0:T(8,128)(2,1)} %cot_ref.1), channel_id=1, source_target_pairs={{0,6},{1,7},{2,0},{3,1},{4,2},{5,3},{6,4},{7,5},{8,14},{9,15},{10,... | collective-permute-start | bytes 1572872 | tf_op jit(solution)/shard_map/ppermute | solution.py:472
  38.5 25.8 %collective-permute-start.8 = (bf16[4,512,128]{2,1,0:T(8,128)(2,1)S(1)}, bf16[4,512,128]{2,1,0:T(8,128)(2,1)S(1)}, u32[]{:S(2)}, u32[]{:S(2)}) collective-permute-start(bf16[4,512,128]{2,1,0:T(8,128)(2,1)S(1)} %pad_maximum_fusion.2.refs_3_), channel_id=1, source_target_pairs={{0,4},{1,5},{2,6},{3,7},{4,0},{5,1},{6,2},{7,3},{8,12},{9,13},{10,... | collective-permute-start | bytes 1572872 | tf_op jit(solution)/shard_map/ppermute | solution.py:472
  39.7 33.2 %collective-permute-start.7 = (bf16[4,512,128]{2,1,0:T(8,128)(2,1)S(1)}, bf16[4,512,128]{2,1,0:T(8,128)(2,1)S(1)}, u32[]{:S(2)}, u32[]{:S(2)}) collective-permute-start(bf16[4,512,128]{2,1,0:T(8,128)(2,1)S(1)} %pad_maximum_fusion.2.refs_3_), channel_id=1, source_target_pairs={{0,6},{1,7},{2,0},{3,1},{4,2},{5,3},{6,4},{7,5},{8,14},{9,15},{10,... | collective-permute-start | bytes 1572872 | tf_op jit(solution)/shard_map/ppermute | solution.py:472
  40.8 32.9 %collective-permute-start.6 = (bf16[4,512,128]{2,1,0:T(8,128)(2,1)S(1)}, bf16[4,512,128]{2,1,0:T(8,128)(2,1)}, u32[]{:S(2)}, u32[]{:S(2)}) collective-permute-start(bf16[4,512,128]{2,1,0:T(8,128)(2,1)S(1)} %pad_maximum_fusion.2.refs_3_), channel_id=1, source_target_pairs={{0,2},{1,3},{2,4},{3,5},{4,6},{5,7},{6,0},{7,1},{8,10},{9,11},{10,... | collective-permute-start | bytes 1572872 | tf_op jit(solution)/shard_map/ppermute | solution.py:472
  78.5 4.2 %collective-permute-start.9 = (bf16[4,512,512]{2,1,0:T(8,128)(2,1)S(1)}, bf16[4,512,512]{2,1,0:T(8,128)(2,1)S(1)}, u32[]{:S(2)}, u32[]{:S(2)}) collective-permute-start(bf16[4,512,512]{2,1,0:T(8,128)(2,1)S(1)} %project.1), channel_id=1, source_target_pairs={{0,1},{1,0},{2,3},{3,2},{4,5},{5,4},{6,7},{7,6},{8,9},{9,8},{10,11... | collective-permute-start | bytes 6291464 | tf_op jit(solution)/shard_map/ppermute | solution.py:476
  80.0 5.7 %collective-permute-start.10 = (bf16[4,4,512,128]{3,2,1,0:T(8,128)(2,1)S(1)}, bf16[4,4,512,128]{3,2,1,0:T(8,128)(2,1)S(1)}, u32[]{:S(2)}, u32[]{:S(2)}) collective-permute-start(bf16[4,4,512,128]{3,2,1,0:T(8,128)(2,1)S(1)} %pad_maximum_fusion.refs_1_), channel_id=1, source_target_pairs={{0,1},{1,0},{2,3},{3,2},{4,5},{5,4},{6,7},{7,6},{8,9},{9,8},{10,11... | collective-permute-start | bytes 6291464 | tf_op jit(solution)/shard_map/ppermute | solution.py:476
  80.5 15.6 %collective-permute-start.13 = (bf16[512,512]{1,0:T(8,128)(2,1)S(1)}, bf16[512,512]{1,0:T(8,128)(2,1)S(1)}, u32[]{:S(2)}, u32[]{:S(2)}) collective-permute-start(bf16[512,512]{1,0:T(8,128)(2,1)S(1)} %copy-done.8), channel_id=1, source_target_pairs={{0,4},{1,5},{2,6},{3,7},{4,0},{5,1},{6,2},{7,3},{8,12},{9,13},{10,... | collective-permute-start | bytes 1572872 | tf_op jit(solution)/shard_map/ppermute | solution.py:472
  90.0 6.1 %collective-permute-start.14 = (bf16[512,128]{1,0:T(8,128)(2,1)S(1)}, bf16[512,128]{1,0:T(8,128)(2,1)S(1)}, u32[]{:S(2)}, u32[]{:S(2)}) collective-permute-start(bf16[512,128]{1,0:T(8,128)(2,1)S(1)} %get-tuple-element.102), channel_id=1, source_target_pairs={{0,32},{8,40},{16,48},{24,56},{32,64},{40,72},{48,80},{56,88},{64,... | collective-permute-start | bytes 393224 | tf_op jit(solution)/shard_map/ppermute | solution.py:467
  92.0 5.6 %collective-permute-start.15 = (bf16[512,128]{1,0:T(8,128)(2,1)S(1)}, bf16[512,128]{1,0:T(8,128)(2,1)S(1)}, u32[]{:S(2)}, u32[]{:S(2)}) collective-permute-start(bf16[512,128]{1,0:T(8,128)(2,1)S(1)} %get-tuple-element.103), channel_id=1, source_target_pairs={{0,224},{8,232},{16,240},{24,248},{32,0},{40,8},{48,16},{56,24},{6... | collective-permute-start | bytes 393224 | tf_op jit(solution)/shard_map/ppermute | solution.py:467
  99.2 19.1 %collective-permute-start.11 = (bf16[512,512]{1,0:T(8,128)(2,1)S(1)}, bf16[512,512]{1,0:T(8,128)(2,1)S(1)}, u32[]{:S(2)}, u32[]{:S(2)}) collective-permute-start(bf16[512,512]{1,0:T(8,128)(2,1)S(1)} %get-tuple-element.98), channel_id=1, source_target_pairs={{0,2},{1,3},{2,4},{3,5},{4,6},{5,7},{6,0},{7,1},{8,10},{9,11},{10,... | collective-permute-start | bytes 1572872 | tf_op jit(solution)/shard_map/ppermute | solution.py:472
  99.6 26.4 %collective-permute-start.12 = (bf16[512,512]{1,0:T(8,128)(2,1)S(1)}, bf16[512,512]{1,0:T(8,128)(2,1)S(1)}, u32[]{:S(2)}, u32[]{:S(2)}) collective-permute-start(bf16[512,512]{1,0:T(8,128)(2,1)S(1)} %get-tuple-element.99), channel_id=1, source_target_pairs={{0,6},{1,7},{2,0},{3,1},{4,2},{5,3},{6,4},{7,5},{8,14},{9,15},{10,... | collective-permute-start | bytes 1572872 | tf_op jit(solution)/shard_map/ppermute | solution.py:472
  101.3 29.3 %collective-permute-start.16 = (bf16[512,512]{1,0:T(8,128)(2,1)S(1)}, bf16[512,512]{1,0:T(8,128)(2,1)S(1)}, u32[]{:S(2)}, u32[]{:S(2)}) collective-permute-start(bf16[512,512]{1,0:T(8,128)(2,1)S(1)} %get-tuple-element.105), channel_id=1, source_target_pairs={{0,4},{1,5},{2,6},{3,7},{4,0},{5,1},{6,2},{7,3},{8,12},{9,13},{10,... | collective-permute-start | bytes 1572872 | tf_op jit(solution)/shard_map/ppermute | solution.py:472
  106.3 11.1 %collective-permute-start.18 = (bf16[192,512]{1,0:T(8,128)(2,1)S(1)}, bf16[192,512]{1,0:T(8,128)(2,1)S(1)}, u32[]{:S(2)}, u32[]{:S(2)}) collective-permute-start(bf16[192,512]{1,0:T(8,128)(2,1)S(1)} %get-tuple-element.114), channel_id=1, source_target_pairs={{8,0},{16,8},{24,16},{32,24},{40,32},{48,40},{56,48},{64,56},{72,6... | collective-permute-start | bytes 589832 | tf_op jit(solution)/shard_map/ppermute | solution.py:481
  109.2 34.1 %collective-permute-start.19 = (bf16[512,128]{1,0:T(8,128)(2,1)S(1)}, bf16[512,128]{1,0:T(8,128)(2,1)S(1)}, u32[]{:S(2)}, u32[]{:S(2)}) collective-permute-start(bf16[512,128]{1,0:T(8,128)(2,1)S(1)} %get-tuple-element.122), channel_id=1, source_target_pairs={{0,64},{8,72},{16,80},{24,88},{32,96},{40,104},{48,112},{56,120},{... | collective-permute-start | bytes 393224 | tf_op jit(solution)/shard_map/ppermute | solution.py:467
  117.3 25.9 %collective-permute-start.20 = (bf16[512,128]{1,0:T(8,128)(2,1)S(1)}, bf16[512,128]{1,0:T(8,128)(2,1)S(1)}, u32[]{:S(2)}, u32[]{:S(2)}) collective-permute-start(bf16[512,128]{1,0:T(8,128)(2,1)S(1)} %get-tuple-element.123), channel_id=1, source_target_pairs={{0,192},{8,200},{16,208},{24,216},{32,224},{40,232},{48,240},{56,2... | collective-permute-start | bytes 393224 | tf_op jit(solution)/shard_map/ppermute | solution.py:467
  118.3 25.0 %collective-permute-start.21 = (bf16[512,128]{1,0:T(8,128)(2,1)S(1)}, bf16[512,128]{1,0:T(8,128)(2,1)S(1)}, u32[]{:S(2)}, u32[]{:S(2)}) collective-permute-start(bf16[512,128]{1,0:T(8,128)(2,1)S(1)} %get-tuple-element.124), channel_id=1, source_target_pairs={{0,96},{8,104},{16,112},{24,120},{32,128},{40,136},{48,144},{56,15... | collective-permute-start | bytes 393224 | tf_op jit(solution)/shard_map/ppermute | solution.py:467
  126.0 17.3 %collective-permute-start.22 = (bf16[512,128]{1,0:T(8,128)(2,1)S(1)}, bf16[512,128]{1,0:T(8,128)(2,1)S(1)}, u32[]{:S(2)}, u32[]{:S(2)}) collective-permute-start(bf16[512,128]{1,0:T(8,128)(2,1)S(1)} %get-tuple-element.125), channel_id=1, source_target_pairs={{0,160},{8,168},{16,176},{24,184},{32,192},{40,200},{48,208},{56,2... | collective-permute-start | bytes 393224 | tf_op jit(solution)/shard_map/ppermute | solution.py:467
  130.5 15.2 %collective-permute-start.23 = (bf16[512,128]{1,0:T(8,128)(2,1)S(1)}, bf16[512,128]{1,0:T(8,128)(2,1)S(1)}, u32[]{:S(2)}, u32[]{:S(2)}) collective-permute-start(bf16[512,128]{1,0:T(8,128)(2,1)S(1)} %get-tuple-element.126), channel_id=1, source_target_pairs={{0,128},{8,136},{16,144},{24,152},{32,160},{40,168},{48,176},{56,1... | collective-permute-start | bytes 393224 | tf_op jit(solution)/shard_map/ppermute | solution.py:467
  (25 other events, 145.8 us)

commit v3 on v2

--- a/solution.py
+++ b/solution.py
@@ -210,7 +210,7 @@
             out_ref[stream, start : start + STEP] = (total * live).astype(BF16)
 
 
-def params(mib=20):
+def params(mib=56):
     return pltpu.CompilerParams(vmem_limit_bytes=mib * 2**20)
 
 
@@ -304,8 +304,12 @@
     out_ref[0] = jnp.dot(mix_ref[...], weight_ref[...], preferred_element_type=F32).astype(BF16)
 
 
-def block_at(other):
-    return lambda i, info: (0, info[2 + other + 2 * ((0x0132 >> (4 * i)) & 15)])
+def own_block(i, info):
+    return 0, 2 * ((info[3] + 1 + i) & 3) + info[1]
+
+
+def other_block(i, info):
+    return 0, 2 * ((info[3] + 1 + i) & 3) + 1 - info[1]
 
 
 def run_project(info, mix_in, weight, after=()):
@@ -317,7 +321,7 @@
             grid=(count,),
             in_specs=[
                 pl.BlockSpec((ROWS, CH), lambda i, order: (0, 0)),
-                pl.BlockSpec((CH, CH), block_at(1)),
+                pl.BlockSpec((CH, CH), other_block),
             ] + [ANY] * len(after),
             out_specs=pl.BlockSpec((1, ROWS, CH), lambda i, order: (i, 0, 0)),
         ),
@@ -328,20 +332,17 @@
     )(info, mix_in, weight, *after)
 
 
-def project_add_kernel(order_ref, mix_ref, weight_ref, other_ref, *refs):
-    one_ref, two_ref, three_ref, own_ref = refs[-4:]
-    step = pl.program_id(0)
+def project_add_kernel(info_ref, mix_ref, weight_ref, other_ref, *refs):
     total = jnp.dot(mix_ref[...], weight_ref[...], preferred_element_type=F32)
     total += other_ref[0].astype(F32)
-    for place, ref in enumerate((one_ref, two_ref, three_ref, own_ref)):
-
-        @pl.when(step == place)
+    for place, ref in enumerate(refs[-NY:]):
+
+        @pl.when(pl.program_id(0) == place)
         def _(ref=ref):
             ref[...] = total.astype(ref.dtype)
 
 
 def run_project_add(info, mix_in, weight, other, after=()):
-    piece = jax.ShapeDtypeStruct((ROWS, CH), BF16)
     fixed = pl.BlockSpec((ROWS, CH), lambda i, order: (0, 0))
     return pl.pallas_call(
         project_add_kernel,
@@ -350,76 +351,78 @@
             grid=(4,),
             in_specs=[
                 fixed,
-                pl.BlockSpec((CH, CH), block_at(0)),
+                pl.BlockSpec((CH, CH), own_block),
                 pl.BlockSpec((1, ROWS, CH), lambda i, order: (i, 0, 0)),
             ] + [ANY] * len(after),
-            out_specs=[fixed] * 4,
+            out_specs=[fixed] * NY,
         ),
-        out_shape=[piece, piece, piece, jax.ShapeDtypeStruct((ROWS, CH), F32)],
+        out_shape=[jax.ShapeDtypeStruct((ROWS, CH), BF16)] * (NY - 1) + [jax.ShapeDtypeStruct((ROWS, CH), F32)],
         compiler_params=params(),
         cost_estimate=cost(1000, 1000),
         name="project_add",
     )(info, mix_in, weight, other, *after)
 
 
-def prepare_kernel(info_ref, qkv_ref, cot_ref, tail_ref, *refs):
-    live = live_rows(info_ref[0], ROWS - TAIL, TAIL)[:, 0:1]
+def prepare_kernel(info_ref, qkv_ref, cot_ref, tail_ref, quarter_ref):
+    live = live_rows(info_ref[0], ROWS // 2, ROWS // 2)[:, 0:1]
     place = 0
     for stream, rows in ((0, RIM), (1, TAIL), (2, TAIL)):
-        masked = qkv_ref[stream, TAIL - rows :].astype(F32) * live[TAIL - rows :]
+        masked = qkv_ref[stream, ROWS // 2 - rows :].astype(F32) * live[ROWS // 2 - rows :]
         tail_ref[place : place + rows] = masked.astype(BF16)
         place += rows
-    for ahead, ref in enumerate(refs):
-        column = pl.multiple_of(lax.rem(info_ref[1] + ahead, NX) * LANES, LANES)
-        ref[...] = cot_ref[:, pl.ds(column, LANES)]
+    for quarter in range(NX):
+        quarter_ref[quarter] = cot_ref[:, quarter * LANES : (quarter + 1) * LANES]
 
 
 def run_prepare(info, streams, cotangent):
     return pl.pallas_call(
         prepare_kernel,
-        in_specs=[SMEM, VMEM, VMEM],
-        out_specs=[VMEM] * (1 + NX),
-        out_shape=[jax.ShapeDtypeStruct((RIM + 2 * TAIL, CH), BF16)]
-        + [jax.ShapeDtypeStruct((ROWS, LANES), BF16)] * NX,
+        grid=(1,),
+        in_specs=[SMEM, pl.BlockSpec((3, ROWS // 2, CH), lambda i: (0, 1, 0)), whole(ROWS, CH)],
+        out_specs=[whole(RIM + 2 * TAIL, CH), whole(NX, ROWS, LANES)],
+        out_shape=[
+            jax.ShapeDtypeStruct((RIM + 2 * TAIL, CH), BF16),
+            jax.ShapeDtypeStruct((NX, ROWS, LANES), BF16),
+        ],
         compiler_params=params(),
         cost_estimate=cost(1000, 1000),
         name="prepare",
-    )(info, streams[:, ROWS - TAIL :], cotangent)
-
-
-def outer_kernel(info_ref, *refs):
-    turned, mine, theirs, outputs, work_ref = refs[0], refs[1], refs[2], refs[-1 - NZ : -1], refs[-1]
-    for pair in range(NZ // 2):
+    )(info, streams, cotangent)
+
+
+def outer_kernel(info_ref, mine, theirs, *refs):
+    turned, out_ref = refs[:NX], refs[-1]
+    core = info_ref[1]
+    for y in range(NY):
         total = None
-        for ahead in range(NX):
-            both = jnp.concatenate([mine[pair, ahead], theirs[pair, ahead]], axis=1)
-            part = jnp.dot(turned[lax.rem(info_ref[1] + NX - ahead, NX)], both, preferred_element_type=F32)
+        for behind in range(NX):
+            x = (info_ref[2] - behind) & 3
+            both = jnp.concatenate([mine[y, x], theirs[y, x]], axis=1)
+            part = jnp.dot(turned[behind][...], both, preferred_element_type=F32)
             total = part if total is None else total + part
-        work_ref[info_ref[10 + 2 * pair]] = total[:, :LANES]
-        work_ref[info_ref[11 + 2 * pair]] = total[:, LANES:]
-    for ahead, ref in enumerate(outputs):
-        ref[...] = work_ref[ahead].astype(ref.dtype)
-
-
-def run_outer(info, turned, slabs, slabs_other, after=()):
-    sent = jax.ShapeDtypeStruct((CH, LANES), BF16)
+        out_ref[2 * y + core] = total[:, :LANES].astype(BF16)
+        out_ref[2 * y + 1 - core] = total[:, LANES:].astype(BF16)
+
+
+def run_outer(info, turned, mine, theirs, after=()):
     return pl.pallas_call(
         outer_kernel,
-        in_specs=[SMEM] + [VMEM] * 3 + [ANY] * len(after),
-        out_specs=[VMEM] * NZ,
-        out_shape=[jax.ShapeDtypeStruct((CH, LANES), F32)] + [sent] * (NZ - 1),
-        scratch_shapes=[pltpu.VMEM((NZ, CH, LANES), F32)],
+        in_specs=[SMEM] + [VMEM] * 6 + [ANY] * len(after),
+        out_specs=VMEM,
+        out_shape=jax.ShapeDtypeStruct((NZ, CH, LANES), BF16),
         compiler_params=params(),
         cost_estimate=cost(1000, 1000),
         name="outer",
-    )(info, turned, slabs, slabs_other, *after)
+    )(info, mine, theirs, *turned, *after)
 
 
 def d_mix_kernel(info_ref, weight_ref, mine, theirs, q_ref, k_ref, v_ref, conv_ref, *refs):
     dconv_ref, dq_ref, msg_ref = refs[-3:]
     total = None
     for slot in range(2 * NY):
-        column = pl.multiple_of(info_ref[2 + slot] * CH, CH)
+        ahead = (0, -1, 1, 2)[slot // 2]
+        block = 2 * ((info_ref[3] + ahead) & 3) + (info_ref[1] if slot % 2 == 0 else 1 - info_ref[1])
+        column = pl.multiple_of(block * CH, CH)
         piece = (mine, theirs)[slot % 2][slot // 2]
         part = lax.dot_general(
             piece, weight_ref[:, pl.ds(column, CH)], (((1,), (1,)), ((), ())),
@@ -453,23 +456,29 @@
     )(info, weight, mine, theirs, *sides, *after)
 
 
-def ctx_pairs(ahead_z, ahead_x):
-    return [
-        (z * NX + x, (z + ahead_z) % NZ * NX + (x + ahead_x) % NX) for z in range(NZ) for x in range(NX)
-    ]
+def exchange(array, axis):
+    groups = {
+        "x": [[z * NX + x for x in range(NX)] for z in range(NZ)],
+        "z": [[z * NX + x for z in range(NZ)] for x in range(NX)],
+        "y": [[2 * y + core for y in range(NY)] for core in range(2)],
+    }[axis]
+    return lax.all_to_all(
+        array, "tp" if axis == "y" else "ctx", 0, 0, axis_index_groups=groups, tiled=True
+    )
 
 
 def along_x(array, ahead):
-    return lax.ppermute(array, "ctx", ctx_pairs(0, ahead))
-
-
-def along_z(array, ahead):
-    return lax.ppermute(array, "ctx", ctx_pairs(ahead, 0))
+    pairs = [(i, i // NX * NX + (i + ahead) % NX) for i in range(NZ * NX)]
+    return lax.ppermute(array, "ctx", pairs)
 
 
 def along_y(array, ahead):
-    pairs = [(2 * y + core, 2 * ((y + ahead) % NY) + core) for y in range(NY) for core in range(2)]
+    pairs = [(i, (i + 2 * ahead) % (2 * NY)) for i in range(2 * NY)]
     return lax.ppermute(array, "tp", pairs)
+
+
+def copies(array):
+    return jnp.broadcast_to(array[None], (NY, *array.shape))
 
 
 def other_core(array):
@@ -484,63 +493,46 @@
 def local(qkv, short_filter, long_filter, out_weight, cotangent, valid_len):
     forward_table, causal_table, anti_table = (jnp.asarray(table) for table in tables())
     ctx, tp = lax.axis_index("ctx"), lax.axis_index("tp")
-    z, x, y, core = ctx >> 2, ctx & 3, tp >> 1, tp & 1
-    ahead = jnp.array([0, 0, -1, -1, 1, 1, 2, 2], jnp.int32)
-    other = jnp.array([0, 1, 0, 1, 0, 1, 0, 1], jnp.int32)
-    blocks = (((y + ahead) & 3) << 1) + ((core + other) & 1)
-    info = jnp.concatenate([valid_len, x[None].astype(jnp.int32), blocks, (blocks - z) & 7])
+    info = jnp.stack([valid_len[0], tp & 1, ctx & 3, tp >> 1])
     streams = qkv.transpose(1, 0, 2)
     short = short_filter.transpose(1, 0, 2)
 
-    tail, *quarters = run_prepare(info, streams, cotangent)
+    below, above = along_y(cotangent, 1), along_y(cotangent, -1)
+    tail, quarters = run_prepare(info, streams, cotangent)
     halo = neighbour(tail, 1)
-    first, second, third = (along_x(quarters[ahead], ahead) for ahead in (1, 2, 3))
-    below, above = along_y(cotangent, 1), along_y(cotangent, -1)
+    slab = exchange(quarters, "x")
     own = run_forward(info, streams, short, long_filter, forward_table, causal_table, (tail,))
-    first, second, third, halo, *own = lax.optimization_barrier([first, second, third, halo, *own])
-    slab = jnp.stack([quarters[0], first, second, third])
-    slabs = [slab] + [along_y(slab, ahead) for ahead in (1, -1, 2)]
+    slab, halo, below, above, *own = lax.optimization_barrier([slab, halo, below, above, *own])
+    slab_copies = copies(slab)
+    mine = exchange(slab_copies, "y").reshape(NY, NX, ROWS, LANES)
     mix_in, turned, q_side, k_side, v_side, conv = run_finish(
-        info, streams, halo, short, long_filter, forward_table, causal_table, own, (slab, below)
+        info, streams, halo, short, long_filter, forward_table, causal_table, own, (slab_copies,)
     )
-    copies = jnp.broadcast_to(turned[None], (NX, CH, ROWS))
-    turned = lax.all_to_all(
-        copies, "ctx", 0, 0, axis_index_groups=[[z * NX + x for x in range(NX)] for z in range(NZ)], tiled=True
-    )
-    turned, above, mix_in, cotangent, *slabs = lax.optimization_barrier(
-        [turned, above, mix_in, cotangent, *slabs]
-    )
-    slabs = jnp.stack(slabs)
-    slabs_other = other_core(slabs)
+    turned = [turned] + [along_x(turned, ahead) for ahead in (1, 2, 3)]
+    mine, cotangent, mix_in, *turned = lax.optimization_barrier([mine, cotangent, mix_in, *turned])
+    theirs = other_core(mine)
     far = along_y(cotangent, 2)
     given = run_project(info, mix_in, out_weight)
+    sums = run_outer(info, turned, mine, theirs, (given,))
     taken = other_core(given)
-    total, *sent = run_outer(info, turned, slabs, slabs_other, (taken,))
-    sums = [along_z(sent[ahead - 1], ahead) for ahead in (1, 7, 2, 6)]
-    one, two, three, own_out = run_project_add(info, mix_in, out_weight, taken, (total,))
-    arrived = [along_y(one, 1), along_y(three, 3)]
-    far, below, above, sums[0], sums[1], two = lax.optimization_barrier(
-        (far, below, above, sums[0], sums[1], two)
-    )
+    far, taken, mix_in, sums = lax.optimization_barrier((far, taken, mix_in, sums))
+    one, two, three, own_out = run_project_add(info, mix_in, out_weight, taken)
+    sums = exchange(sums, "z")
     cots = jnp.stack([cotangent, below, above, far])
     cots_other = other_core(cots)
+    arrived = [along_y(one, 1), along_y(two, 2), along_y(three, 3)]
     d_conv, d_q, msg = run_d_mix(info, out_weight, cots, cots_other, (q_side, k_side, v_side, conv))
     msg = neighbour(msg, -1)
-    arrived.append(along_y(two, 2))
-    msg, *rest = lax.optimization_barrier([msg] + [sent[ahead - 1] for ahead in (3, 5, 4)])
-    sums += [along_z(array, ahead) for array, ahead in zip(rest, (3, 5, 4))]
-
     d_streams = run_backward(
         info, d_conv, msg, d_q, k_side, v_side, short, long_filter, forward_table, anti_table
     )
+    sums, d_streams = lax.optimization_barrier((sums, d_streams))
     d_qkv = d_streams.transpose(1, 0, 2)
     mixed = own_out
     for array in arrived:
         mixed = mixed + array.astype(F32)
     mixed = mixed.astype(BF16)
-    for array in sums:
-        total = total + array.astype(F32)
-    d_weight = total * (1.0 / jnp.sqrt(jnp.float32(ROWS * NZ * NX)))
+    d_weight = jnp.sum(sums.astype(F32), axis=0) * (1.0 / jnp.sqrt(jnp.float32(ROWS * NZ * NX)))
     return mixed, d_qkv, d_weight
 
 

time: 147 us -> 143 us (0.973)
  the two profiles are of different devices: /device:TPU:62 before, /device:TPU:102 now
where the time goes in v3:
time: 143 us; the launch traced here: 140 us
  Pallas kernels  50.4 us (35%)
  waiting for transfers between devices  40.7 us (28%)
  starting transfers between devices  39 us (27%)
  local copies, waits for them, and re-layouts  4.63 us (3%)
  other arithmetic  4.28 us (3%)
    ppermute x3, waiting for transfers between devices, along_x(): return lax.ppermute(array, 'ctx', pairs)  23 us
    all_to_all x3, starting transfers between devices, exchange(): lax.all_to_all(array, 'tp' if axis == 'y' else 'ctx', 0, 0, axis_index_gr...  16.2 us
    ppermute x6, waiting for transfers between devices, along_y(): return lax.ppermute(array, 'tp', pairs)  16 us
    ppermute x6, starting transfers between devices, along_y(): return lax.ppermute(array, 'tp', pairs)  11.7 us
    pallas_call x1, Pallas kernels, run_backward(): pl.pallas_call(backward_kernel, grid=(CH // LANES,), in_specs=[SMEM, lane...  9.23 us
    pallas_call x1, Pallas kernels, run_d_mix(): pl.pallas_call(d_mix_kernel, in_specs=[SMEM] + [VMEM] * 7 + [ANY] * len(a...  8.24 us
    pallas_call x1, Pallas kernels, run_forward(): pl.pallas_call(forward_kernel, grid=(CH // LANES,), in_specs=[SMEM, lane_...  6.91 us
    ppermute x2, starting transfers between devices, neighbour(): lax.ppermute(array, 'ctx', [(i, i + by) for i in range(count) if 0 <= i +...  6.72 us
  transfers between devices with their start and end apart: 17, of which 6 were waited for; matrix products, arithmetic and copies ran while one was open for 1% of the time, Pallas kernels for 36%

profile of v3, /device:TPU:102, one launch (start us, length us, event | category | flops | bytes accessed | tf_op | source)
XLA Modules:
  0.0 140.4 jit_solution(7624665236972213484)
XLA Ops:
  2.3 1.7 %collective-permute-start.2 = (bf16[512,512]{1,0:T(8,128)(2,1)}, bf16[512,512]{1,0:T(8,128)(2,1)S(1)}, u32[]{:S(2)}, u32[]{:S(2)}) collective-permute-start(bf16[512,512]{1,0:T(8,128)(2,1)} %cot_ref.1), channel_id=1, source_target_pairs={{0,6},{1,7},{2,0},{3,1},{4,2},{5,3},{6,4},{7,5},{8,14},{9,15},{10,... | collective-permute-start | bytes 1572872 | tf_op jit(solution)/shard_map/ppermute | solution.py:477
  5.2 2.3 %prepare.1 = (bf16[304,512]{1,0:T(8,128)(2,1)}, bf16[4,512,128]{2,1,0:T(8,128)(2,1)}) custom-call(s32[4]{0:T(128)} %pad_add_fusion.info_ref.valid_ref.order_ref, bf16[3,512,512]{2,1,0:T(8,128)(2,1)} %bitcast.10, bf16[512,512]{1,0:T(8,128)(2,1)} %cot_ref.1), custom_call_target="tpu_custom_call" | custom-call | flops 1000 | bytes 1000 | tf_op jit(solution)/shard_map/prepare/pallas_call | solution.py:378
  7.5 4.8 %all-to-all-start = ((bf16[4,512,128]{2,1,0:T(8,128)(2,1)}), bf16[4,512,128]{2,1,0:T(8,128)(2,1)S(1)}, u32[]{:S(2)}, u32[]{:S(2)}) async-start(bf16[4,512,128]{2,1,0:T(8,128)(2,1)} %get-tuple-element.49), calls=%async_computation | async-start | bytes 1048576 | tf_op jit(solution)/shard_map/all_to_all | solution.py:465
  12.3 4.5 %collective-permute-start = (bf16[304,512]{1,0:T(8,128)(2,1)}, bf16[304,512]{1,0:T(8,128)(2,1)S(1)}, u32[]{:S(2)}, u32[]{:S(2)}) collective-permute-start(bf16[304,512]{1,0:T(8,128)(2,1)} %get-tuple-element.50.refs_0_), channel_id=1, source_target_pairs={{0,8},{8,16},{16,24},{24,32},{32,40},{40,48},{48,56},{56,64},{64,7... | collective-permute-start | bytes 933896 | tf_op jit(solution)/shard_map/ppermute | solution.py:490
  16.7 6.9 %forward.1 = (bf16[512,512]{1,0:T(8,128)(2,1)}, bf16[512,512]{1,0:T(8,128)(2,1)}, f32[512,512]{1,0:T(8,128)}, f32[512,512]{1,0:T(8,128)}, f32[512,512]{1,0:T(8,1...) custom-call(s32[4]{0:T(128)} %pad_add_fusion.info_ref.valid_ref.order_ref, bf16[3,512,512]{2,1,0:T(8,128)(2,1)} %bitcast.11, ...), custom_call_target="tpu_custom_call" | custom-call | flops 1000 | bytes 1000 | tf_op jit(solution)/shard_map/forward/pallas_call | solution.py:241
  23.7 1.7 %collective-permute-done.halo_ref = bf16[304,512]{1,0:T(8,128)(2,1)S(1)} collective-permute-done((bf16[304,512]{1,0:T(8,128)(2,1)}, bf16[304,512]{1,0:T(8,128)(2,1)S(1)}, u32[]{:S(2)}, u32[]{:S(2)}) %collective-permute-start) | collective-permute-done | bytes 311328 | tf_op jit(solution)/shard_map/ppermute | solution.py:490
  25.4 1.8 %broadcast_in_dim.2.refs_3_ = bf16[4,4,512,128]{3,2,1,0:T(8,128)(2,1)} broadcast(bf16[4,512,128]{2,1,0:T(8,128)(2,1)S(1)} %all-to-all-done), dimensions={1,2,3} | broadcast | bytes 2621440 | tf_op jit(solution)/shard_map/broadcast_in_dim | solution.py:481
  27.1 3.6 %all-to-all-start.1 = ((bf16[4,4,512,128]{3,2,1,0:T(8,128)(2,1)}), bf16[4,4,512,128]{3,2,1,0:T(8,128)(2,1)S(1)}, u32[]{:S(2)}, u32[]{:S(2)}) async-start(bf16[4,4,512,128]{3,2,1,0:T(8,128)(2,1)} %broadcast_in_dim.2.refs_3_), calls=%async_computation.1 | async-start | bytes 4194304 | tf_op jit(solution)/shard_map/all_to_all | solution.py:465
  30.8 5.6 %finish.1 = (bf16[512,512]{1,0:T(8,128)(2,1)}, bf16[512,512]{1,0:T(8,128)(2,1)}, f32[512,512]{1,0:T(8,128)}, f32[512,512]{1,0:T(8,128)}, f32[512,512]{1,0:T(8,128)}, /*index=5*/f32[512,512]{1,0:T(8,128)}) custom-call(s32[4]{0:T(128)} %pad_add_fusion.info_ref.valid_ref.order_ref, ...), custom_call_target="tpu_custom_call", output_to_operand_aliasing={{2}: (7, {}), {3}: (8, {}), {4}: (9, {}), {0}: (11, {}), {1... | custom-call | flops 1000 | bytes 1000 | tf_op jit(solution)/shard_map/finish/pallas_call | solution.py:261
  36.4 2.7 %collective-permute-start.3 = (bf16[512,512]{1,0:T(8,128)(2,1)}, bf16[512,512]{1,0:T(8,128)(2,1)S(1)}, u32[]{:S(2)}, u32[]{:S(2)}) collective-permute-start(bf16[512,512]{1,0:T(8,128)(2,1)} %get-tuple-element.72.refs_0_), channel_id=1, source_target_pairs={{0,8},{8,16},{16,24},{24,0},{32,40},{40,48},{48,56},{56,32},{64,72... | collective-permute-start | bytes 1572872 | tf_op jit(solution)/shard_map/ppermute | solution.py:472
  40.1 19.3 %collective-permute-done.3.refs_1_ = bf16[512,512]{1,0:T(8,128)(2,1)S(1)} collective-permute-done((bf16[512,512]{1,0:T(8,128)(2,1)}, bf16[512,512]{1,0:T(8,128)(2,1)S(1)}, u32[]{:S(2)}, u32[]{:S(2)}) %collective-permute-start.3) | collective-permute-done | bytes 524320 | tf_op jit(solution)/shard_map/ppermute | solution.py:472
  59.4 3.7 %collective-permute-done.5.refs_3_ = bf16[512,512]{1,0:T(8,128)(2,1)} collective-permute-done((bf16[512,512]{1,0:T(8,128)(2,1)}, bf16[512,512]{1,0:T(8,128)(2,1)}, u32[]{:S(2)}, u32[]{:S(2)}) %collective-permute-start.5) | collective-permute-done | bytes 524320 | tf_op jit(solution)/shard_map/ppermute | solution.py:472
  63.2 5.6 %project.1.refs_4_ = bf16[4,512,512]{2,1,0:T(8,128)(2,1)} custom-call(s32[4]{0:T(128)} %pad_add_fusion.info_ref.valid_ref.order_ref, bf16[512,512]{1,0:T(8,128)(2,1)} %get-tuple-element.76.mix_ref, bf16[512,4096]{1,0:T(8,128)(2,1)} %weight_ref.5), custom_call_target="tpu_custom_call" | custom-call | flops 1000 | bytes 1000 | tf_op jit(solution)/shard_map/project/pallas_call | solution.py:317
  69.2 3.2 %collective-permute-start.6 = (bf16[512,512]{1,0:T(8,128)(2,1)S(1)}, bf16[512,512]{1,0:T(8,128)(2,1)S(1)}, u32[]{:S(2)}, u32[]{:S(2)}) collective-permute-start(bf16[512,512]{1,0:T(8,128)(2,1)S(1)} %copy-done.4), channel_id=1, source_target_pairs={{0,4},{1,5},{2,6},{3,7},{4,0},{5,1},{6,2},{7,3},{8,12},{9,13},{10,... | collective-permute-start | bytes 1572872 | tf_op jit(solution)/shard_map/ppermute | solution.py:477
  73.8 6.2 %outer.1 = bf16[8,512,128]{2,1,0:T(8,128)(2,1)} custom-call(s32[4]{0:T(128)} %pad_add_fusion.info_ref.valid_ref.order_ref, bf16[4,4,512,128]{3,2,1,0:T(8,128)(2,1)} %copy-done, bf16[4,4,512,128]{3,2,1,0:T(8,128)(2,1)} %copy-done.2, bf16[512,512]{1,0:T(8,128)(2,1)} %get-tuple-element.72.refs_0_, bf16[512,512]{1,0:T(8,128)(2,1)} %copy-done.6, ...), custom_call_target="tpu_custom_call" | custom-call | flops 1000 | bytes 1000 | tf_op jit(solution)/shard_map/outer/pallas_call | solution.py:408
  79.9 4.8 %collective-permute-done.6 = bf16[512,512]{1,0:T(8,128)(2,1)S(1)} collective-permute-done((bf16[512,512]{1,0:T(8,128)(2,1)S(1)}, bf16[512,512]{1,0:T(8,128)(2,1)S(1)}, u32[]{:S(2)}, u32[]{:S(2)}) %collective-permute-start.6) | collective-permute-done | bytes 524320 | tf_op jit(solution)/shard_map/ppermute | solution.py:477
  85.5 1.7 %pad_maximum_fusion.mine = bf16[4,512,512]{2,1,0:T(8,128)(2,1)S(1)} fusion(bf16[1,512,512]{2,1,0:T(8,128)(2,1)} %bitcast.17, bf16[1,512,512]{2,1,0:T(8,128)(2,1)} %bitcast.16, bf16[1,512,512]{2,1,0:T(8,128)(2,1)} %bitcast.15, bf16[1,512,512]{2,1,0:T(8,128)(2,1)S(1)} %bitcast.13), kind=kLoop, calls=%fused_computation | loop fusion | flops 3145728 | bytes 4194304 | tf_op jit(solution)/shard_map/stack | solution.py:521
  87.3 7.8 %all-to-all-start.2 = ((bf16[8,512,128]{2,1,0:T(8,128)(2,1)}), bf16[8,512,128]{2,1,0:T(8,128)(2,1)S(1)}, u32[]{:S(2)}, u32[]{:S(2)}) async-start(bf16[8,512,128]{2,1,0:T(8,128)(2,1)} %outer.1), calls=%async_computation.2 | async-start | bytes 2097152 | tf_op jit(solution)/shard_map/all_to_all | solution.py:465
  95.2 6.4 %project_add.1 = (bf16[512,512]{1,0:T(8,128)(2,1)}, bf16[512,512]{1,0:T(8,128)(2,1)}, bf16[512,512]{1,0:T(8,128)(2,1)}, f32[512,512]{1,0:T(8,128)}) custom-call(s32[4]{0:T(128)} %pad_add_fusion.info_ref.valid_ref.order_ref, bf16[512,512]{1,0:T(8,128)(2,1)} %get-tuple-element.76.mix_ref, bf16[512,4096]{1,0:T(8,128)(2,1)} %weight_ref.5, ...), custom_call_target="tpu_custom_call" | custom-call | flops 1000 | bytes 1000 | tf_op jit(solution)/shard_map/project_add/pallas_call | solution.py:347
  101.5 3.2 %collective-permute-start.10 = (bf16[512,512]{1,0:T(8,128)(2,1)}, bf16[512,512]{1,0:T(8,128)(2,1)S(1)}, u32[]{:S(2)}, u32[]{:S(2)}) collective-permute-start(bf16[512,512]{1,0:T(8,128)(2,1)} %get-tuple-element.80), channel_id=1, source_target_pairs={{0,4},{1,5},{2,6},{3,7},{4,0},{5,1},{6,2},{7,3},{8,12},{9,13},{10,... | collective-permute-start | bytes 1572872 | tf_op jit(solution)/shard_map/ppermute | solution.py:477
  106.8 8.2 %d_mix.1 = (bf16[512,512]{1,0:T(8,128)(2,1)}, f32[512,512]{1,0:T(8,128)}, bf16[192,512]{1,0:T(8,128)(2,1)}) custom-call(s32[4]{0:T(128)} %pad_add_fusion.info_ref.valid_ref.order_ref, bf16[512,4096]{1,0:T(8,128)(2,1)} %weight_ref.5, bf16[4,512,512]{2,1,0:T(8,128)(2,1)} %copy-done.1, bf16[4,512,512]{2,1,0:T(8,128)(2,1)} %collective-permute-done.12.theirs, ...), custom_call_target="tpu_custom_call" | custom-call | flops 1000 | bytes 1000 | tf_op jit(solution)/shard_map/d_mix/pallas_call | solution.py:445
  115.0 2.3 %collective-permute-start.13 = (bf16[192,512]{1,0:T(8,128)(2,1)}, bf16[192,512]{1,0:T(8,128)(2,1)S(1)}, u32[]{:S(2)}, u32[]{:S(2)}) collective-permute-start(bf16[192,512]{1,0:T(8,128)(2,1)} %get-tuple-element.91), channel_id=1, source_target_pairs={{8,0},{16,8},{24,16},{32,24},{40,32},{48,40},{56,48},{64,56},{72,6... | collective-permute-start | bytes 589832 | tf_op jit(solution)/shard_map/ppermute | solution.py:490
  118.1 10.4 %collective-permute-done.11 = bf16[512,512]{1,0:T(8,128)(2,1)S(1)} collective-permute-done((bf16[512,512]{1,0:T(8,128)(2,1)}, bf16[512,512]{1,0:T(8,128)(2,1)S(1)}, u32[]{:S(2)}, u32[]{:S(2)}) %collective-permute-start.11) | collective-permute-done | bytes 524320 | tf_op jit(solution)/shard_map/ppermute | solution.py:477
  130.3 9.2 %backward.1 = bf16[3,512,512]{2,1,0:T(8,128)(2,1)} custom-call(s32[4]{0:T(128)} %pad_add_fusion.info_ref.valid_ref.order_ref, bf16[512,512]{1,0:T(8,128)(2,1)} %get-tuple-element.90.dconv_ref, bf16[192,512]{1,0:T(8,128)(2,1)} %copy-done.12, f32[512,512]{1,0:T(8,128)} %get-tuple-element.92.dq_ref, f32[512,512]{1,0:T(8,128)} %get-tuple-element.87.k_ref, ...), custom_call_target="tpu_custom_call" | custom-call | flops 1000 | bytes 1000 | tf_op jit(solution)/shard_map/backward/pallas_call | solution.py:282
  (50 shorter events, 11.6 us)
Async XLA Ops:
  0.6 24.7 %collective-permute-start.1 = (bf16[512,512]{1,0:T(8,128)(2,1)}, bf16[512,512]{1,0:T(8,128)(2,1)S(1)}, u32[]{:S(2)}, u32[]{:S(2)}) collective-permute-start(bf16[512,512]{1,0:T(8,128)(2,1)} %cot_ref.1), channel_id=1, source_target_pairs={{0,2},{1,3},{2,4},{3,5},{4,6},{5,7},{6,0},{7,1},{8,10},{9,11},{10,... | collective-permute-start | bytes 1572872 | tf_op jit(solution)/shard_map/ppermute | solution.py:477
  2.3 23.1 %collective-permute-start.2 = (bf16[512,512]{1,0:T(8,128)(2,1)}, bf16[512,512]{1,0:T(8,128)(2,1)S(1)}, u32[]{:S(2)}, u32[]{:S(2)}) collective-permute-start(bf16[512,512]{1,0:T(8,128)(2,1)} %cot_ref.1), channel_id=1, source_target_pairs={{0,6},{1,7},{2,0},{3,1},{4,2},{5,3},{6,4},{7,5},{8,14},{9,15},{10,... | collective-permute-start | bytes 1572872 | tf_op jit(solution)/shard_map/ppermute | solution.py:477
  7.5 17.8 %all-to-all-start = ((bf16[4,512,128]{2,1,0:T(8,128)(2,1)}), bf16[4,512,128]{2,1,0:T(8,128)(2,1)S(1)}, u32[]{:S(2)}, u32[]{:S(2)}) async-start(bf16[4,512,128]{2,1,0:T(8,128)(2,1)} %get-tuple-element.49), calls=%async_computation | async-start | bytes 1048576 | tf_op jit(solution)/shard_map/all_to_all | solution.py:465
  12.3 13.1 %collective-permute-start = (bf16[304,512]{1,0:T(8,128)(2,1)}, bf16[304,512]{1,0:T(8,128)(2,1)S(1)}, u32[]{:S(2)}, u32[]{:S(2)}) collective-permute-start(bf16[304,512]{1,0:T(8,128)(2,1)} %get-tuple-element.50.refs_0_), channel_id=1, source_target_pairs={{0,8},{8,16},{16,24},{24,32},{32,40},{40,48},{48,56},{56,64},{64,7... | collective-permute-start | bytes 933896 | tf_op jit(solution)/shard_map/ppermute | solution.py:490
  27.1 36.0 %all-to-all-start.1 = ((bf16[4,4,512,128]{3,2,1,0:T(8,128)(2,1)}), bf16[4,4,512,128]{3,2,1,0:T(8,128)(2,1)S(1)}, u32[]{:S(2)}, u32[]{:S(2)}) async-start(bf16[4,4,512,128]{3,2,1,0:T(8,128)(2,1)} %broadcast_in_dim.2.refs_3_), calls=%async_computation.1 | async-start | bytes 4194304 | tf_op jit(solution)/shard_map/all_to_all | solution.py:465
  36.4 23.0 %collective-permute-start.3 = (bf16[512,512]{1,0:T(8,128)(2,1)}, bf16[512,512]{1,0:T(8,128)(2,1)S(1)}, u32[]{:S(2)}, u32[]{:S(2)}) collective-permute-start(bf16[512,512]{1,0:T(8,128)(2,1)} %get-tuple-element.72.refs_0_), channel_id=1, source_target_pairs={{0,8},{8,16},{16,24},{24,0},{32,40},{40,48},{48,56},{56,32},{64,72... | collective-permute-start | bytes 1572872 | tf_op jit(solution)/shard_map/ppermute | solution.py:472
  39.2 20.3 %collective-permute-start.4 = (bf16[512,512]{1,0:T(8,128)(2,1)}, bf16[512,512]{1,0:T(8,128)(2,1)S(1)}, u32[]{:S(2)}, u32[]{:S(2)}) collective-permute-start(bf16[512,512]{1,0:T(8,128)(2,1)} %get-tuple-element.72.refs_0_), channel_id=1, source_target_pairs={{0,16},{8,24},{16,0},{24,8},{32,48},{40,56},{48,32},{56,40},{64,80... | collective-permute-start | bytes 1572872 | tf_op jit(solution)/shard_map/ppermute | solution.py:472
  39.2 23.9 %collective-permute-start.5 = (bf16[512,512]{1,0:T(8,128)(2,1)}, bf16[512,512]{1,0:T(8,128)(2,1)}, u32[]{:S(2)}, u32[]{:S(2)}) collective-permute-start(bf16[512,512]{1,0:T(8,128)(2,1)} %get-tuple-element.72.refs_0_), channel_id=1, source_target_pairs={{0,24},{8,0},{16,8},{24,16},{32,56},{40,32},{48,40},{56,48},{64,88... | collective-permute-start | bytes 1572872 | tf_op jit(solution)/shard_map/ppermute | solution.py:472
  59.4 9.3 %copy-start.6 = (bf16[512,512]{1,0:T(8,128)(2,1)}, bf16[512,512]{1,0:T(8,128)(2,1)S(1)}, u32[]{:S(2)}) copy-start(bf16[512,512]{1,0:T(8,128)(2,1)S(1)} %collective-permute-done.3.refs_1_) | copy-start | bytes 1572868
  59.4 9.3 %copy-start.7 = (bf16[512,512]{1,0:T(8,128)(2,1)}, bf16[512,512]{1,0:T(8,128)(2,1)S(1)}, u32[]{:S(2)}) copy-start(bf16[512,512]{1,0:T(8,128)(2,1)S(1)} %collective-permute-done.4.refs_2_) | copy-start | bytes 1572868
  63.1 5.7 %copy-start = (bf16[4,4,512,128]{3,2,1,0:T(8,128)(2,1)}, bf16[4,4,512,128]{3,2,1,0:T(8,128)(2,1)S(1)}, u32[]{:S(2)}) copy-start(bf16[4,4,512,128]{3,2,1,0:T(8,128)(2,1)S(1)} %all-to-all-done.1.mine) | copy-start | bytes 6291460
  63.1 6.1 %copy-start.4 = (bf16[512,512]{1,0:T(8,128)(2,1)S(1)}, bf16[512,512]{1,0:T(8,128)(2,1)}, u32[]{:S(2)}) copy-start(bf16[512,512]{1,0:T(8,128)(2,1)} %cot_ref.1) | copy-start | bytes 1572868
  63.1 9.3 %collective-permute-start.8 = (bf16[4,4,512,128]{3,2,1,0:T(8,128)(2,1)S(1)}, bf16[4,4,512,128]{3,2,1,0:T(8,128)(2,1)S(1)}, u32[]{:S(2)}, u32[]{:S(2)}) collective-permute-start(bf16[4,4,512,128]{3,2,1,0:T(8,128)(2,1)S(1)} %all-to-all-done.1.mine), channel_id=1, source_target_pairs={{0,1},{1,0},{2,3},{3,2},{4,5},{5,4},{6,7},{7,6},{8,9},{9,8},{10,11... | collective-permute-start | bytes 6291464 | tf_op jit(solution)/shard_map/ppermute | solution.py:485
  68.8 15.9 %collective-permute-start.7 = (bf16[4,512,512]{2,1,0:T(8,128)(2,1)}, bf16[4,512,512]{2,1,0:T(8,128)(2,1)S(1)}, u32[]{:S(2)}, u32[]{:S(2)}) collective-permute-start(bf16[4,512,512]{2,1,0:T(8,128)(2,1)} %project.1.refs_4_), channel_id=1, source_target_pairs={{0,1},{1,0},{2,3},{3,2},{4,5},{5,4},{6,7},{7,6},{8,9},{9,8},{10,11... | collective-permute-start | bytes 6291464 | tf_op jit(solution)/shard_map/ppermute | solution.py:485
  69.2 15.5 %collective-permute-start.6 = (bf16[512,512]{1,0:T(8,128)(2,1)S(1)}, bf16[512,512]{1,0:T(8,128)(2,1)S(1)}, u32[]{:S(2)}, u32[]{:S(2)}) collective-permute-start(bf16[512,512]{1,0:T(8,128)(2,1)S(1)} %copy-done.4), channel_id=1, source_target_pairs={{0,4},{1,5},{2,6},{3,7},{4,0},{5,1},{6,2},{7,3},{8,12},{9,13},{10,... | collective-permute-start | bytes 1572872 | tf_op jit(solution)/shard_map/ppermute | solution.py:477
  84.7 2.5 %copy-start.3 = (bf16[4,512,512]{2,1,0:T(8,128)(2,1)}, bf16[4,512,512]{2,1,0:T(8,128)(2,1)S(1)}, u32[]{:S(2)}) copy-start(bf16[4,512,512]{2,1,0:T(8,128)(2,1)S(1)} %collective-permute-done.7.other_ref) | copy-start | bytes 6291460
  87.2 14.3 %copy-start.1 = (bf16[4,512,512]{2,1,0:T(8,128)(2,1)}, bf16[4,512,512]{2,1,0:T(8,128)(2,1)S(1)}, u32[]{:S(2)}) copy-start(bf16[4,512,512]{2,1,0:T(8,128)(2,1)S(1)} %pad_maximum_fusion.mine) | copy-start | bytes 6291460
  87.2 19.5 %collective-permute-start.12 = (bf16[4,512,512]{2,1,0:T(8,128)(2,1)S(1)}, bf16[4,512,512]{2,1,0:T(8,128)(2,1)}, u32[]{:S(2)}, u32[]{:S(2)}) collective-permute-start(bf16[4,512,512]{2,1,0:T(8,128)(2,1)S(1)} %pad_maximum_fusion.mine), channel_id=1, source_target_pairs={{0,1},{1,0},{2,3},{3,2},{4,5},{5,4},{6,7},{7,6},{8,9},{9,8},{10,11... | collective-permute-start | bytes 6291464 | tf_op jit(solution)/shard_map/ppermute | solution.py:485
  87.3 52.2 %all-to-all-start.2 = ((bf16[8,512,128]{2,1,0:T(8,128)(2,1)}), bf16[8,512,128]{2,1,0:T(8,128)(2,1)S(1)}, u32[]{:S(2)}, u32[]{:S(2)}) async-start(bf16[8,512,128]{2,1,0:T(8,128)(2,1)} %outer.1), calls=%async_computation.2 | async-start | bytes 2097152 | tf_op jit(solution)/shard_map/all_to_all | solution.py:465
  101.5 16.6 %collective-permute-start.10 = (bf16[512,512]{1,0:T(8,128)(2,1)}, bf16[512,512]{1,0:T(8,128)(2,1)S(1)}, u32[]{:S(2)}, u32[]{:S(2)}) collective-permute-start(bf16[512,512]{1,0:T(8,128)(2,1)} %get-tuple-element.80), channel_id=1, source_target_pairs={{0,4},{1,5},{2,6},{3,7},{4,0},{5,1},{6,2},{7,3},{8,12},{9,13},{10,... | collective-permute-start | bytes 1572872 | tf_op jit(solution)/shard_map/ppermute | solution.py:477
  104.7 23.8 %collective-permute-start.11 = (bf16[512,512]{1,0:T(8,128)(2,1)}, bf16[512,512]{1,0:T(8,128)(2,1)S(1)}, u32[]{:S(2)}, u32[]{:S(2)}) collective-permute-start(bf16[512,512]{1,0:T(8,128)(2,1)} %get-tuple-element.81), channel_id=1, source_target_pairs={{0,6},{1,7},{2,0},{3,1},{4,2},{5,3},{6,4},{7,5},{8,14},{9,15},{10,... | collective-permute-start | bytes 1572872 | tf_op jit(solution)/shard_map/ppermute | solution.py:477
  105.9 22.6 %collective-permute-start.9 = (bf16[512,512]{1,0:T(8,128)(2,1)}, bf16[512,512]{1,0:T(8,128)(2,1)S(1)}, u32[]{:S(2)}, u32[]{:S(2)}) collective-permute-start(bf16[512,512]{1,0:T(8,128)(2,1)} %get-tuple-element.79), channel_id=1, source_target_pairs={{0,2},{1,3},{2,4},{3,5},{4,6},{5,7},{6,0},{7,1},{8,10},{9,11},{10,... | collective-permute-start | bytes 1572872 | tf_op jit(solution)/shard_map/ppermute | solution.py:477
  106.8 21.8 %copy-start.5 = (f32[512,512]{1,0:T(8,128)S(1)}, f32[512,512]{1,0:T(8,128)}, u32[]{:S(2)}) copy-start(f32[512,512]{1,0:T(8,128)} %get-tuple-element.78) | copy-start | bytes 3145732
  115.0 14.6 %collective-permute-start.13 = (bf16[192,512]{1,0:T(8,128)(2,1)}, bf16[192,512]{1,0:T(8,128)(2,1)S(1)}, u32[]{:S(2)}, u32[]{:S(2)}) collective-permute-start(bf16[192,512]{1,0:T(8,128)(2,1)} %get-tuple-element.91), channel_id=1, source_target_pairs={{8,0},{16,8},{24,16},{32,24},{40,32},{48,40},{56,48},{64,56},{72,6... | collective-permute-start | bytes 589832 | tf_op jit(solution)/shard_map/ppermute | solution.py:490
  (6 other events, 8.2 us)

commit v4 on v3

--- a/solution.py
+++ b/solution.py
@@ -18,6 +18,7 @@
 RIM = 16
 STEP = 64
 NZ, NX, NY = 8, 4, 4
+HALF = ROWS // 2
 F32, BF16 = jnp.float32, jnp.bfloat16
 
 
@@ -210,7 +211,7 @@
             out_ref[stream, start : start + STEP] = (total * live).astype(BF16)
 
 
-def params(mib=56):
+def params(mib=20):
     return pltpu.CompilerParams(vmem_limit_bytes=mib * 2**20)
 
 
@@ -248,7 +249,7 @@
         out_specs=[lane_spec(ROWS), pl.BlockSpec((LANES, ROWS), lambda i: (i, 0))] + [lane_spec(ROWS)] * 5,
         out_shape=forward_shapes() + [jax.ShapeDtypeStruct((ROWS, CH), BF16)],
         scratch_shapes=[pltpu.VMEM((3, RIM + ROWS, LANES), F32)],
-        compiler_params=params(),
+        compiler_params=params(56),
         cost_estimate=cost(1000, 1000),
         name="forward",
     )(info, streams, short, long_taps, fwd, inv, *after)
@@ -272,7 +273,7 @@
             pltpu.VMEM((3, TAIL + RIM, LANES), F32),
             pltpu.VMEM((3 * LONG, LANES), BF16),
         ],
-        compiler_params=params(),
+        compiler_params=params(56),
         cost_estimate=cost(1000, 1000),
         name="finish",
     )(info, streams, halo, short, long_taps, fwd, inv, q_side, k_side, v_side, gate, mix_in, turned, conv, *after)
@@ -293,7 +294,7 @@
             pltpu.VMEM((3, ROWS + RIM, LANES), F32),
             pltpu.VMEM((2 * LONG, LANES), BF16),
         ],
-        compiler_params=params(),
+        compiler_params=params(56),
         cost_estimate=cost(1000, 1000),
         name="backward",
     )(valid, d_conv, msg, d_q, k_side, v_side, short, long_taps, fwd, inv, *after)
@@ -335,15 +336,32 @@
 def project_add_kernel(info_ref, mix_ref, weight_ref, other_ref, *refs):
     total = jnp.dot(mix_ref[...], weight_ref[...], preferred_element_type=F32)
     total += other_ref[0].astype(F32)
-    for place, ref in enumerate(refs[-NY:]):
-
-        @pl.when(pl.program_id(0) == place)
-        def _(ref=ref):
-            ref[...] = total.astype(ref.dtype)
+    up_ref, down_ref, next_ref, last_ref, own_ref = refs[-5:]
+    top, bottom = total[:HALF].astype(BF16), total[HALF:].astype(BF16)
+
+    @pl.when(pl.program_id(0) == 0)
+    def _():
+        next_ref[...] = top
+        up_ref[HALF:] = bottom
+
+    @pl.when(pl.program_id(0) == 1)
+    def _():
+        up_ref[:HALF] = top
+        down_ref[HALF:] = bottom
+
+    @pl.when(pl.program_id(0) == 2)
+    def _():
+        down_ref[:HALF] = top
+        last_ref[...] = bottom
+
+    @pl.when(pl.program_id(0) == 3)
+    def _():
+        own_ref[...] = total
 
 
 def run_project_add(info, mix_in, weight, other, after=()):
     fixed = pl.BlockSpec((ROWS, CH), lambda i, order: (0, 0))
+    half = pl.BlockSpec((HALF, CH), lambda i, order: (0, 0))
     return pl.pallas_call(
         project_add_kernel,
         grid_spec=pltpu.PrefetchScalarGridSpec(
@@ -354,9 +372,10 @@
                 pl.BlockSpec((CH, CH), own_block),
                 pl.BlockSpec((1, ROWS, CH), lambda i, order: (i, 0, 0)),
             ] + [ANY] * len(after),
-            out_specs=[fixed] * NY,
+            out_specs=[fixed, fixed, half, half, fixed],
         ),
-        out_shape=[jax.ShapeDtypeStruct((ROWS, CH), BF16)] * (NY - 1) + [jax.ShapeDtypeStruct((ROWS, CH), F32)],
+        out_shape=[jax.ShapeDtypeStruct((rows, CH), BF16) for rows in (ROWS, ROWS, HALF, HALF)]
+        + [jax.ShapeDtypeStruct((ROWS, CH), F32)],
         compiler_params=params(),
         cost_estimate=cost(1000, 1000),
         name="project_add",
@@ -467,6 +486,10 @@
     )
 
 
+def add(one, other):
+    return (one.astype(F32) + other.astype(F32)).astype(BF16)
+
+
 def along_x(array, ahead):
     pairs = [(i, i // NX * NX + (i + ahead) % NX) for i in range(NZ * NX)]
     return lax.ppermute(array, "ctx", pairs)
@@ -502,36 +525,39 @@
     halo = neighbour(tail, 1)
     slab = exchange(quarters, "x")
     own = run_forward(info, streams, short, long_filter, forward_table, causal_table, (tail,))
-    slab, halo, below, above, *own = lax.optimization_barrier([slab, halo, below, above, *own])
+    slab, halo, below, above, held, *own = lax.optimization_barrier([slab, halo, below, above, cotangent, *own])
     slab_copies = copies(slab)
     mine = exchange(slab_copies, "y").reshape(NY, NX, ROWS, LANES)
     mix_in, turned, q_side, k_side, v_side, conv = run_finish(
         info, streams, halo, short, long_filter, forward_table, causal_table, own, (slab_copies,)
     )
     turned = [turned] + [along_x(turned, ahead) for ahead in (1, 2, 3)]
-    mine, cotangent, mix_in, *turned = lax.optimization_barrier([mine, cotangent, mix_in, *turned])
+    far = along_y(held, 2)
+    turned[1], mix_in = lax.optimization_barrier((turned[1], mix_in))
+    given = run_project(info, mix_in, out_weight)
+    taken = other_core(given)
+    mine, far, given, *turned = lax.optimization_barrier([mine, far, given, *turned])
     theirs = other_core(mine)
-    far = along_y(cotangent, 2)
-    given = run_project(info, mix_in, out_weight)
-    sums = run_outer(info, turned, mine, theirs, (given,))
-    taken = other_core(given)
-    far, taken, mix_in, sums = lax.optimization_barrier((far, taken, mix_in, sums))
-    one, two, three, own_out = run_project_add(info, mix_in, out_weight, taken)
-    sums = exchange(sums, "z")
     cots = jnp.stack([cotangent, below, above, far])
     cots_other = other_core(cots)
-    arrived = [along_y(one, 1), along_y(two, 2), along_y(three, 3)]
-    d_conv, d_q, msg = run_d_mix(info, out_weight, cots, cots_other, (q_side, k_side, v_side, conv))
+    partial = run_outer(info, turned, mine, theirs)
+    sums = exchange(partial, "z")
+    up, down, next_top, last_bottom, own_out = run_project_add(info, mix_in, out_weight, taken, (partial,))
+    from_below, from_above = along_y(up, 1), along_y(down, -1)
+    d_conv, d_q, msg = run_d_mix(
+        info, out_weight, cots, cots_other, (q_side, k_side, v_side, conv), (up,)
+    )
+    top = along_y(add(next_top, from_below[:HALF]), 1)
+    bottom = along_y(add(last_bottom, from_above[HALF:]), -1)
     msg = neighbour(msg, -1)
     d_streams = run_backward(
         info, d_conv, msg, d_q, k_side, v_side, short, long_filter, forward_table, anti_table
     )
-    sums, d_streams = lax.optimization_barrier((sums, d_streams))
+    sums, d_streams, own_out = lax.optimization_barrier((sums, d_streams, own_out))
     d_qkv = d_streams.transpose(1, 0, 2)
-    mixed = own_out
-    for array in arrived:
-        mixed = mixed + array.astype(F32)
-    mixed = mixed.astype(BF16)
+    top = own_out[:HALF] + top.astype(F32) + from_above[:HALF].astype(F32)
+    bottom = own_out[HALF:] + bottom.astype(F32) + from_below[HALF:].astype(F32)
+    mixed = jnp.concatenate([top, bottom], axis=0).astype(BF16)
     d_weight = jnp.sum(sums.astype(F32), axis=0) * (1.0 / jnp.sqrt(jnp.float32(ROWS * NZ * NX)))
     return mixed, d_qkv, d_weight
 

time: 143 us -> 146 us (1.021); the launches traced: 140 us -> 145 us
  local copies, waits for them, and re-layouts: 4.63 us -> 14.1 us
  Pallas kernels: 50.4 us -> 41.4 us
  other arithmetic: 4.28 us -> 7.02 us
  starting transfers between devices: 39 us -> 41.4 us
    ppermute x2, waiting for transfers between devices: 1.68 us -> 12.2 us  [neighbour(): lax.ppermute(array, 'ctx', [(i, i + by) for i in range(count) if 0 <= i +...]
    unnamed x26 -> x58, local copies, waits for them, and re-layouts: 2.87 us -> 12.3 us
    ppermute x3, waiting for transfers between devices: 23 us -> 13.9 us  [along_x(): return lax.ppermute(array, 'ctx', pairs)]
    ppermute x6 -> x7, waiting for transfers between devices: 16 us -> 9.96 us  [along_y(): return lax.ppermute(array, 'tp', pairs)]
    pallas_call x1, Pallas kernels: 8.24 us -> 3.97 us  [run_d_mix(): pl.pallas_call(d_mix_kernel, in_specs=[SMEM] + [VMEM] * 7 + [ANY] * len(a...]
    ppermute x3, waiting for transfers between devices: 0.01 us -> 3.78 us  [other_core(): return lax.ppermute(array, 'tp', [(i, i ^ 1) for i in range(2 * NY)])]
    pallas_call x1, Pallas kernels: 5.56 us -> 3.64 us  [run_project(): pl.pallas_call(project_kernel, grid_spec=pltpu.PrefetchScalarGridSpec(num...]
    ppermute x2, starting transfers between devices: 6.72 us -> 8.31 us  [neighbour(): lax.ppermute(array, 'ctx', [(i, i + by) for i in range(count) if 0 <= i +...]
  transfers between devices with their start and end apart: 17 -> 18, of which waited for: 6 -> 8; matrix products, arithmetic and copies ran while one was open for 1% -> 3% of each run, Pallas kernels for 36% -> 29%
where the time goes in v4:
time: 146 us; the launch traced here: 145 us
  starting transfers between devices  41.4 us (28%)
  Pallas kernels  41.4 us (28%)
  waiting for transfers between devices  39.8 us (27%)
  local copies, waits for them, and re-layouts  14.1 us (10%)
  other arithmetic  7.02 us (5%)
  between operations  1.54 us (1%)
    all_to_all x3, starting transfers between devices, exchange(): lax.all_to_all(array, 'tp' if axis == 'y' else 'ctx', 0, 0, axis_index_gr...  17 us
    ppermute x3, waiting for transfers between devices, along_x(): return lax.ppermute(array, 'ctx', pairs)  13.9 us
    unnamed x58, local copies, waits for them, and re-layouts  12.3 us
    ppermute x2, waiting for transfers between devices, neighbour(): lax.ppermute(array, 'ctx', [(i, i + by) for i in range(count) if 0 <= i +...  12.2 us
    ppermute x7, starting transfers between devices, along_y(): return lax.ppermute(array, 'tp', pairs)  11.8 us
    ppermute x7, waiting for transfers between devices, along_y(): return lax.ppermute(array, 'tp', pairs)  9.96 us
    pallas_call x1, Pallas kernels, run_backward(): pl.pallas_call(backward_kernel, grid=(CH // LANES,), in_specs=[SMEM, lane...  9.23 us
    ppermute x2, starting transfers between devices, neighbour(): lax.ppermute(array, 'ctx', [(i, i + by) for i in range(count) if 0 <= i +...  8.31 us
  transfers between devices with their start and end apart: 18, of which 8 were waited for; matrix products, arithmetic and copies ran while one was open for 3% of the time, Pallas kernels for 29%

profile of v4, /device:TPU:102, one launch (start us, length us, event | category | flops | bytes accessed | tf_op | source)
XLA Modules:
  0.0 145.3 jit_solution(4827531589287993134)
XLA Ops:
  8.6 4.8 %all-to-all-start = ((bf16[4,512,128]{2,1,0:T(8,128)(2,1)}), bf16[4,512,128]{2,1,0:T(8,128)(2,1)S(1)}, u32[]{:S(2)}, u32[]{:S(2)}) async-start(bf16[4,512,128]{2,1,0:T(8,128)(2,1)} %get-tuple-element.49), calls=%async_computation | async-start | bytes 1048576 | tf_op jit(solution)/shard_map/all_to_all | solution.py:484
  13.3 4.5 %collective-permute-start = (bf16[304,512]{1,0:T(8,128)(2,1)S(1)}, bf16[304,512]{1,0:T(8,128)(2,1)S(1)}, u32[]{:S(2)}, u32[]{:S(2)}) collective-permute-start(bf16[304,512]{1,0:T(8,128)(2,1)S(1)} %get-tuple-element.50.refs_0_), channel_id=1, source_target_pairs={{0,8},{8,16},{16,24},{24,32},{32,40},{40,48},{48,56},{56,64},{64,7... | collective-permute-start | bytes 933896 | tf_op jit(solution)/shard_map/ppermute | solution.py:513
  17.8 6.8 %forward.1 = (bf16[512,512]{1,0:T(8,128)(2,1)}, bf16[512,512]{1,0:T(8,128)(2,1)}, f32[512,512]{1,0:T(8,128)}, f32[512,512]{1,0:T(8,128)}, f32[512,512]{1,0:T(8,1...) custom-call(s32[4]{0:T(128)} %copy-done.22, bf16[3,512,512]{2,1,0:T(8,128)(2,1)} %bitcast.10, f32[3,7,512]{2,1,0:T(8,128)} %bitcast.18, ...), custom_call_target="tpu_custom_call" | custom-call | flops 1000 | bytes 1000 | tf_op jit(solution)/shard_map/forward/pallas_call | solution.py:242
  28.2 4.4 %all-to-all-start.1 = ((bf16[4,4,512,128]{3,2,1,0:T(8,128)(2,1)}), bf16[4,4,512,128]{3,2,1,0:T(8,128)(2,1)}, u32[]{:S(2)}, u32[]{:S(2)}) async-start(bf16[4,4,512,128]{3,2,1,0:T(8,128)(2,1)} %broadcast_in_dim.2.refs_3_), calls=%async_computation.1 | async-start | bytes 4194304 | tf_op jit(solution)/shard_map/all_to_all | solution.py:484
  32.7 5.8 %finish.1 = (bf16[512,512]{1,0:T(8,128)(2,1)}, bf16[512,512]{1,0:T(8,128)(2,1)}, f32[512,512]{1,0:T(8,128)}, f32[512,512]{1,0:T(8,128)}, f32[512,512]{1,0:T(8,128)}, /*index=5*/f32[512,512]{1,0:T(8,128)}) custom-call(s32[4]{0:T(128)} %copy-done.22, ...), custom_call_target="tpu_custom_call", output_to_operand_aliasing={{2}: (7, {}), {3}: (8, {}), {4}: (9, {}), {0}: (11, {}), {1... | custom-call | flops 1000 | bytes 1000 | tf_op jit(solution)/shard_map/finish/pallas_call | solution.py:262
  38.5 2.7 %collective-permute-start.4 = (bf16[512,512]{1,0:T(8,128)(2,1)}, bf16[512,512]{1,0:T(8,128)(2,1)S(1)}, u32[]{:S(2)}, u32[]{:S(2)}) collective-permute-start(bf16[512,512]{1,0:T(8,128)(2,1)} %get-tuple-element.73.refs_0_), channel_id=1, source_target_pairs={{0,8},{8,16},{16,24},{24,0},{32,40},{40,48},{48,56},{56,32},{64,72... | collective-permute-start | bytes 1572872 | tf_op jit(solution)/shard_map/ppermute | solution.py:495
  42.2 3.4 %collective-permute-start.3 = (bf16[512,512]{1,0:T(8,128)(2,1)S(1)}, bf16[512,512]{1,0:T(8,128)(2,1)S(1)}, u32[]{:S(2)}, u32[]{:S(2)}) collective-permute-start(bf16[512,512]{1,0:T(8,128)(2,1)S(1)} %copy-done.11), channel_id=1, source_target_pairs={{0,4},{1,5},{2,6},{3,7},{4,0},{5,1},{6,2},{7,3},{8,12},{9,13},{10,... | collective-permute-start | bytes 1572872 | tf_op jit(solution)/shard_map/ppermute | solution.py:500
  45.6 8.0 %collective-permute-done.4.refs_1_ = bf16[512,512]{1,0:T(8,128)(2,1)S(1)} collective-permute-done((bf16[512,512]{1,0:T(8,128)(2,1)}, bf16[512,512]{1,0:T(8,128)(2,1)S(1)}, u32[]{:S(2)}, u32[]{:S(2)}) %collective-permute-start.4) | collective-permute-done | bytes 524320 | tf_op jit(solution)/shard_map/ppermute | solution.py:495
  54.7 3.6 %project.1 = bf16[4,512,512]{2,1,0:T(8,128)(2,1)} custom-call(s32[4]{0:T(128)S(1)} %copy-done.23, bf16[512,512]{1,0:T(8,128)(2,1)S(1)} %copy-done.6, bf16[512,4096]{1,0:T(8,128)(2,1)S(1)} %copy-done), custom_call_target="tpu_custom_call" | custom-call | flops 1000 | bytes 1000 | tf_op jit(solution)/shard_map/project/pallas_call | solution.py:318
  59.1 5.8 %collective-permute-done.6.refs_3_ = bf16[512,512]{1,0:T(8,128)(2,1)S(1)} collective-permute-done((bf16[512,512]{1,0:T(8,128)(2,1)}, bf16[512,512]{1,0:T(8,128)(2,1)S(1)}, u32[]{:S(2)}, u32[]{:S(2)}) %collective-permute-start.6) | collective-permute-done | bytes 524320 | tf_op jit(solution)/shard_map/ppermute | solution.py:495
  65.8 3.0 %collective-permute-done.3 = bf16[512,512]{1,0:T(8,128)(2,1)S(1)} collective-permute-done((bf16[512,512]{1,0:T(8,128)(2,1)S(1)}, bf16[512,512]{1,0:T(8,128)(2,1)S(1)}, u32[]{:S(2)}, u32[]{:S(2)}) %collective-permute-start.3) | collective-permute-done | bytes 524320 | tf_op jit(solution)/shard_map/ppermute | solution.py:500
  71.5 3.8 %collective-permute-done.7.theirs = bf16[4,4,512,128]{3,2,1,0:T(8,128)(2,1)S(1)} collective-permute-done((bf16[4,4,512,128]{3,2,1,0:T(8,128)(2,1)}, bf16[4,4,512,128]{3,2,1,0:T(8,128)(2,1)S(1)}, u32[]{:S(2)}, u32[]{:S(2)}) %collective-permute-start.7) | collective-permute-done | bytes 2097184 | tf_op jit(solution)/shard_map/ppermute | solution.py:508
  75.3 5.1 %outer.1.refs_0_ = bf16[8,512,128]{2,1,0:T(8,128)(2,1)} custom-call(s32[4]{0:T(128)S(1)} %copy-done.23, bf16[4,4,512,128]{3,2,1,0:T(8,128)(2,1)} %all-to-all-done.1.mine, bf16[4,4,512,128]{3,2,1,0:T(8,128)(2,1)S(1)} %collective-permute-done.7.theirs, bf16[512,512]{1,0:T(8,128)(2,1)S(1)} %copy-done.12, bf16[512,512]{1,0:T(8,128)(2,1)S(1)} %collective-permute-done.4.refs_1_, ...), custom_call_target="tpu_custom_call" | custom-call | flops 1000 | bytes 1000 | tf_op jit(solution)/shard_map/outer/pallas_call | solution.py:427
  80.4 7.8 %all-to-all-start.2 = ((bf16[8,512,128]{2,1,0:T(8,128)(2,1)}), bf16[8,512,128]{2,1,0:T(8,128)(2,1)}, u32[]{:S(2)}, u32[]{:S(2)}) async-start(bf16[8,512,128]{2,1,0:T(8,128)(2,1)} %outer.1.refs_0_), calls=%async_computation.2 | async-start | bytes 2097152 | tf_op jit(solution)/shard_map/all_to_all | solution.py:484
  88.2 2.2 %copy-done.1 = bf16[512,4096]{1,0:T(8,128)(2,1)S(1)} copy-done((bf16[512,4096]{1,0:T(8,128)(2,1)S(1)}, bf16[512,4096]{1,0:T(8,128)(2,1)}, u32[]{:S(2)}) %copy-start.1) | copy-done | bytes 4194328
  90.4 5.5 %project_add.1 = (bf16[512,512]{1,0:T(8,128)(2,1)S(1)}, bf16[512,512]{1,0:T(8,128)(2,1)}, bf16[256,512]{1,0:T(8,128)(2,1)S(1)}, bf16[256,512]{1,0:T(8,128)(2,1)S(1)}, f32[512,512]{1,0:T(8,128)S(1)}) custom-call(s32[4]{0:T(128)S(1)} %copy-done.23, bf16[512,512]{1,0:T(8,128)(2,1)S(1)} %copy-done.7, bf16[512,4096]{1,0:T(8,128)(2,1)S(1)} %copy-done.1, ...), custom_call_target="tpu_custom_call" | custom-call | flops 1000 | bytes 1000 | tf_op jit(solution)/shard_map/project_add/pallas_call | solution.py:365
  96.8 1.9 %collective-permute-start.13 = (bf16[512,512]{1,0:T(8,128)(2,1)}, bf16[512,512]{1,0:T(8,128)(2,1)S(1)}, u32[]{:S(2)}, u32[]{:S(2)}) collective-permute-start(bf16[512,512]{1,0:T(8,128)(2,1)} %get-tuple-element.91), channel_id=1, source_target_pairs={{0,6},{1,7},{2,0},{3,1},{4,2},{5,3},{6,4},{7,5},{8,14},{9,15},{10,... | collective-permute-start | bytes 1572872 | tf_op jit(solution)/shard_map/ppermute | solution.py:500
  100.1 4.0 %d_mix.1 = (bf16[512,512]{1,0:T(8,128)(2,1)S(1)}, f32[512,512]{1,0:T(8,128)S(1)}, bf16[192,512]{1,0:T(8,128)(2,1)S(1)}) custom-call(s32[4]{0:T(128)S(1)} %copy-done.23, bf16[512,4096]{1,0:T(8,128)(2,1)S(1)} %copy-done.2, bf16[4,512,512]{2,1,0:T(8,128)(2,1)S(1)} %pad_maximum_fusion.mine, bf16[4,512,512]{2,1,0:T(8,128)(2,1)} %collective-permute-done.8.theirs, ...), custom_call_target="tpu_custom_call" | custom-call | flops 1000 | bytes 1000 | tf_op jit(solution)/shard_map/d_mix/pallas_call | solution.py:464
  105.8 3.8 %collective-permute-start.10 = (bf16[192,512]{1,0:T(8,128)(2,1)S(1)}, bf16[192,512]{1,0:T(8,128)(2,1)S(1)}, u32[]{:S(2)}, u32[]{:S(2)}) collective-permute-start(bf16[192,512]{1,0:T(8,128)(2,1)S(1)} %get-tuple-element.86), channel_id=1, source_target_pairs={{8,0},{16,8},{24,16},{32,24},{40,32},{48,40},{56,48},{64,56},{72,6... | collective-permute-start | bytes 589832 | tf_op jit(solution)/shard_map/ppermute | solution.py:513
  109.7 10.5 %collective-permute-done.10.msg_ref = bf16[192,512]{1,0:T(8,128)(2,1)S(1)} collective-permute-done((bf16[192,512]{1,0:T(8,128)(2,1)S(1)}, bf16[192,512]{1,0:T(8,128)(2,1)S(1)}, u32[]{:S(2)}, u32[]{:S(2)}) %collective-permute-start.10) | collective-permute-done | bytes 196640 | tf_op jit(solution)/shard_map/ppermute | solution.py:513
  120.9 9.2 %backward.1 = bf16[3,512,512]{2,1,0:T(8,128)(2,1)} custom-call(s32[4]{0:T(128)} %copy-done.22, bf16[512,512]{1,0:T(8,128)(2,1)} %copy-done.16, bf16[192,512]{1,0:T(8,128)(2,1)} %copy-done.28, f32[512,512]{1,0:T(8,128)} %copy-done.15, f32[512,512]{1,0:T(8,128)} %get-tuple-element.81.k_ref, f32[512,512]{1,0:T(8,128)} %get-tuple-element.82.v_ref, ...), custom_call_target="tpu_custom_call" | custom-call | flops 1000 | bytes 1000 | tf_op jit(solution)/shard_map/backward/pallas_call | solution.py:283
  130.2 2.9 %collective-permute-start.14 = (bf16[256,512]{1,0:T(8,128)(2,1)S(1)}, bf16[256,512]{1,0:T(8,128)(2,1)S(1)}, u32[]{:S(2)}, u32[]{:S(2)}) collective-permute-start(bf16[256,512]{1,0:T(8,128)(2,1)S(1)} %add_convert_fusion.1), channel_id=1, source_target_pairs={{0,6},{1,7},{2,0},{3,1},{4,2},{5,3},{6,4},{7,5},{8,14},{9,15},{10,... | collective-permute-start | bytes 786440 | tf_op jit(solution)/shard_map/ppermute | solution.py:500
  136.3 2.4 %collective-permute-done.14 = bf16[256,512]{1,0:T(8,128)(2,1)S(1)} collective-permute-done((bf16[256,512]{1,0:T(8,128)(2,1)S(1)}, bf16[256,512]{1,0:T(8,128)(2,1)S(1)}, u32[]{:S(2)}, u32[]{:S(2)}) %collective-permute-start.14) | collective-permute-done | bytes 262176 | tf_op jit(solution)/shard_map/ppermute | solution.py:500
  138.8 4.5 %collective-permute-done.12 = bf16[256,512]{1,0:T(8,128)(2,1)S(1)} collective-permute-done((bf16[256,512]{1,0:T(8,128)(2,1)S(1)}, bf16[256,512]{1,0:T(8,128)(2,1)S(1)}, u32[]{:S(2)}, u32[]{:S(2)}) %collective-permute-start.12) | collective-permute-done | bytes 262176 | tf_op jit(solution)/shard_map/ppermute | solution.py:500
  (87 shorter events, 27.2 us)
Async XLA Ops:
  0.6 25.8 %collective-permute-start.1 = (bf16[512,512]{1,0:T(8,128)(2,1)}, bf16[512,512]{1,0:T(8,128)(2,1)S(1)}, u32[]{:S(2)}, u32[]{:S(2)}) collective-permute-start(bf16[512,512]{1,0:T(8,128)(2,1)} %cot_ref.1), channel_id=1, source_target_pairs={{0,2},{1,3},{2,4},{3,5},{4,6},{5,7},{6,0},{7,1},{8,10},{9,11},{10,... | collective-permute-start | bytes 1572872 | tf_op jit(solution)/shard_map/ppermute | solution.py:500
  2.3 24.1 %collective-permute-start.2 = (bf16[512,512]{1,0:T(8,128)(2,1)}, bf16[512,512]{1,0:T(8,128)(2,1)S(1)}, u32[]{:S(2)}, u32[]{:S(2)}) collective-permute-start(bf16[512,512]{1,0:T(8,128)(2,1)} %cot_ref.1), channel_id=1, source_target_pairs={{0,6},{1,7},{2,0},{3,1},{4,2},{5,3},{6,4},{7,5},{8,14},{9,15},{10,... | collective-permute-start | bytes 1572872 | tf_op jit(solution)/shard_map/ppermute | solution.py:500
  4.7 13.1 %copy-start.22 = (s32[4]{0:T(128)}, s32[4]{0:T(128)S(1)}, u32[]{:S(2)}) copy-start(s32[4]{0:T(128)S(1)} %pad_add_fusion.info_ref.valid_ref.order_ref) | copy-start | bytes 52
  8.6 9.3 %copy-start.21 = (bf16[304,512]{1,0:T(8,128)(2,1)}, bf16[304,512]{1,0:T(8,128)(2,1)S(1)}, u32[]{:S(2)}) copy-start(bf16[304,512]{1,0:T(8,128)(2,1)S(1)} %get-tuple-element.50.refs_0_) | copy-start | bytes 933892
  8.6 17.8 %all-to-all-start = ((bf16[4,512,128]{2,1,0:T(8,128)(2,1)}), bf16[4,512,128]{2,1,0:T(8,128)(2,1)S(1)}, u32[]{:S(2)}, u32[]{:S(2)}) async-start(bf16[4,512,128]{2,1,0:T(8,128)(2,1)} %get-tuple-element.49), calls=%async_computation | async-start | bytes 1048576 | tf_op jit(solution)/shard_map/all_to_all | solution.py:484
  13.3 13.1 %collective-permute-start = (bf16[304,512]{1,0:T(8,128)(2,1)S(1)}, bf16[304,512]{1,0:T(8,128)(2,1)S(1)}, u32[]{:S(2)}, u32[]{:S(2)}) collective-permute-start(bf16[304,512]{1,0:T(8,128)(2,1)S(1)} %get-tuple-element.50.refs_0_), channel_id=1, source_target_pairs={{0,8},{8,16},{16,24},{24,32},{32,40},{40,48},{48,56},{56,64},{64,7... | collective-permute-start | bytes 933896 | tf_op jit(solution)/shard_map/ppermute | solution.py:513
  28.2 40.6 %all-to-all-start.1 = ((bf16[4,4,512,128]{3,2,1,0:T(8,128)(2,1)}), bf16[4,4,512,128]{3,2,1,0:T(8,128)(2,1)}, u32[]{:S(2)}, u32[]{:S(2)}) async-start(bf16[4,4,512,128]{3,2,1,0:T(8,128)(2,1)} %broadcast_in_dim.2.refs_3_), calls=%async_computation.1 | async-start | bytes 4194304 | tf_op jit(solution)/shard_map/all_to_all | solution.py:484
  32.6 9.5 %copy-start.11 = (bf16[512,512]{1,0:T(8,128)(2,1)S(1)}, bf16[512,512]{1,0:T(8,128)(2,1)}, u32[]{:S(2)}) copy-start(bf16[512,512]{1,0:T(8,128)(2,1)} %cot_ref.1) | copy-start | bytes 1572868
  32.7 21.0 %copy-start = (bf16[512,4096]{1,0:T(8,128)(2,1)S(1)}, bf16[512,4096]{1,0:T(8,128)(2,1)}, u32[]{:S(2)}) copy-start(bf16[512,4096]{1,0:T(8,128)(2,1)} %weight_ref.5) | copy-start | bytes 12582916
  32.7 21.0 %copy-start.23 = (s32[4]{0:T(128)S(1)}, s32[4]{0:T(128)}, u32[]{:S(2)}) copy-start(s32[4]{0:T(128)} %copy-done.22) | copy-start | bytes 52
  38.5 15.1 %collective-permute-start.4 = (bf16[512,512]{1,0:T(8,128)(2,1)}, bf16[512,512]{1,0:T(8,128)(2,1)S(1)}, u32[]{:S(2)}, u32[]{:S(2)}) collective-permute-start(bf16[512,512]{1,0:T(8,128)(2,1)} %get-tuple-element.73.refs_0_), channel_id=1, source_target_pairs={{0,8},{8,16},{16,24},{24,0},{32,40},{40,48},{48,56},{56,32},{64,72... | collective-permute-start | bytes 1572872 | tf_op jit(solution)/shard_map/ppermute | solution.py:495
  41.2 17.1 %collective-permute-start.5 = (bf16[512,512]{1,0:T(8,128)(2,1)}, bf16[512,512]{1,0:T(8,128)(2,1)S(1)}, u32[]{:S(2)}, u32[]{:S(2)}) collective-permute-start(bf16[512,512]{1,0:T(8,128)(2,1)} %get-tuple-element.73.refs_0_), channel_id=1, source_target_pairs={{0,16},{8,24},{16,0},{24,8},{32,48},{40,56},{48,32},{56,40},{64,80... | collective-permute-start | bytes 1572872 | tf_op jit(solution)/shard_map/ppermute | solution.py:495
  41.2 23.7 %collective-permute-start.6 = (bf16[512,512]{1,0:T(8,128)(2,1)}, bf16[512,512]{1,0:T(8,128)(2,1)S(1)}, u32[]{:S(2)}, u32[]{:S(2)}) collective-permute-start(bf16[512,512]{1,0:T(8,128)(2,1)} %get-tuple-element.73.refs_0_), channel_id=1, source_target_pairs={{0,24},{8,0},{16,8},{24,16},{32,56},{40,32},{48,40},{56,48},{64,88... | collective-permute-start | bytes 1572872 | tf_op jit(solution)/shard_map/ppermute | solution.py:495
  42.2 26.7 %collective-permute-start.3 = (bf16[512,512]{1,0:T(8,128)(2,1)S(1)}, bf16[512,512]{1,0:T(8,128)(2,1)S(1)}, u32[]{:S(2)}, u32[]{:S(2)}) collective-permute-start(bf16[512,512]{1,0:T(8,128)(2,1)S(1)} %copy-done.11), channel_id=1, source_target_pairs={{0,4},{1,5},{2,6},{3,7},{4,0},{5,1},{6,2},{7,3},{8,12},{9,13},{10,... | collective-permute-start | bytes 1572872 | tf_op jit(solution)/shard_map/ppermute | solution.py:500
  68.8 6.5 %collective-permute-start.7 = (bf16[4,4,512,128]{3,2,1,0:T(8,128)(2,1)}, bf16[4,4,512,128]{3,2,1,0:T(8,128)(2,1)S(1)}, u32[]{:S(2)}, u32[]{:S(2)}) collective-permute-start(bf16[4,4,512,128]{3,2,1,0:T(8,128)(2,1)} %all-to-all-done.1.mine), channel_id=1, source_target_pairs={{0,1},{1,0},{2,3},{3,2},{4,5},{5,4},{6,7},{7,6},{8,9},{9,8},{10,11... | collective-permute-start | bytes 6291464 | tf_op jit(solution)/shard_map/ppermute | solution.py:508
  68.8 19.3 %collective-permute-start.9 = (bf16[4,512,512]{2,1,0:T(8,128)(2,1)}, bf16[4,512,512]{2,1,0:T(8,128)(2,1)}, u32[]{:S(2)}, u32[]{:S(2)}) collective-permute-start(bf16[4,512,512]{2,1,0:T(8,128)(2,1)} %project.1), channel_id=1, source_target_pairs={{0,1},{1,0},{2,3},{3,2},{4,5},{5,4},{6,7},{7,6},{8,9},{9,8},{10,11... | collective-permute-start | bytes 6291464 | tf_op jit(solution)/shard_map/ppermute | solution.py:508
  71.4 27.4 %collective-permute-start.8 = (bf16[4,512,512]{2,1,0:T(8,128)(2,1)S(1)}, bf16[4,512,512]{2,1,0:T(8,128)(2,1)}, u32[]{:S(2)}, u32[]{:S(2)}) collective-permute-start(bf16[4,512,512]{2,1,0:T(8,128)(2,1)S(1)} %pad_maximum_fusion.mine), channel_id=1, source_target_pairs={{0,1},{1,0},{2,3},{3,2},{4,5},{5,4},{6,7},{7,6},{8,9},{9,8},{10,11... | collective-permute-start | bytes 6291464 | tf_op jit(solution)/shard_map/ppermute | solution.py:508
  80.4 53.8 %all-to-all-start.2 = ((bf16[8,512,128]{2,1,0:T(8,128)(2,1)}), bf16[8,512,128]{2,1,0:T(8,128)(2,1)}, u32[]{:S(2)}, u32[]{:S(2)}) async-start(bf16[8,512,128]{2,1,0:T(8,128)(2,1)} %outer.1.refs_0_), calls=%async_computation.2 | async-start | bytes 2097152 | tf_op jit(solution)/shard_map/all_to_all | solution.py:484
  96.8 33.3 %collective-permute-start.13 = (bf16[512,512]{1,0:T(8,128)(2,1)}, bf16[512,512]{1,0:T(8,128)(2,1)S(1)}, u32[]{:S(2)}, u32[]{:S(2)}) collective-permute-start(bf16[512,512]{1,0:T(8,128)(2,1)} %get-tuple-element.91), channel_id=1, source_target_pairs={{0,6},{1,7},{2,0},{3,1},{4,2},{5,3},{6,4},{7,5},{8,14},{9,15},{10,... | collective-permute-start | bytes 1572872 | tf_op jit(solution)/shard_map/ppermute | solution.py:500
  98.7 34.4 %collective-permute-start.11 = (bf16[512,512]{1,0:T(8,128)(2,1)S(1)}, bf16[512,512]{1,0:T(8,128)(2,1)}, u32[]{:S(2)}, u32[]{:S(2)}) collective-permute-start(bf16[512,512]{1,0:T(8,128)(2,1)S(1)} %get-tuple-element.84.refs_0_), channel_id=1, source_target_pairs={{0,2},{1,3},{2,4},{3,5},{4,6},{5,7},{6,0},{7,1},{8,10},{9,11},{10,... | collective-permute-start | bytes 1572872 | tf_op jit(solution)/shard_map/ppermute | solution.py:500
  105.8 14.3 %collective-permute-start.10 = (bf16[192,512]{1,0:T(8,128)(2,1)S(1)}, bf16[192,512]{1,0:T(8,128)(2,1)S(1)}, u32[]{:S(2)}, u32[]{:S(2)}) collective-permute-start(bf16[192,512]{1,0:T(8,128)(2,1)S(1)} %get-tuple-element.86), channel_id=1, source_target_pairs={{8,0},{16,8},{24,16},{32,24},{40,32},{48,40},{56,48},{64,56},{72,6... | collective-permute-start | bytes 589832 | tf_op jit(solution)/shard_map/ppermute | solution.py:513
  130.1 13.2 %copy-start.14 = (f32[512,512]{1,0:T(8,128)S(1)}, f32[512,512]{1,0:T(8,128)}, u32[]{:S(2)}) copy-start(f32[512,512]{1,0:T(8,128)} %copy-done.13) | copy-start | bytes 3145732
  130.2 8.6 %collective-permute-start.14 = (bf16[256,512]{1,0:T(8,128)(2,1)S(1)}, bf16[256,512]{1,0:T(8,128)(2,1)S(1)}, u32[]{:S(2)}, u32[]{:S(2)}) collective-permute-start(bf16[256,512]{1,0:T(8,128)(2,1)S(1)} %add_convert_fusion.1), channel_id=1, source_target_pairs={{0,6},{1,7},{2,0},{3,1},{4,2},{5,3},{6,4},{7,5},{8,14},{9,15},{10,... | collective-permute-start | bytes 786440 | tf_op jit(solution)/shard_map/ppermute | solution.py:500
  134.1 9.1 %collective-permute-start.12 = (bf16[256,512]{1,0:T(8,128)(2,1)S(1)}, bf16[256,512]{1,0:T(8,128)(2,1)S(1)}, u32[]{:S(2)}, u32[]{:S(2)}) collective-permute-start(bf16[256,512]{1,0:T(8,128)(2,1)S(1)} %add_convert_fusion.3), channel_id=1, source_target_pairs={{0,2},{1,3},{2,4},{3,5},{4,6},{5,7},{6,0},{7,1},{8,10},{9,11},{10,... | collective-permute-start | bytes 786440 | tf_op jit(solution)/shard_map/ppermute | solution.py:500
  (23 other events, 76.8 us)

commit v5 on v4

--- a/solution.py
+++ b/solution.py
@@ -163,52 +163,72 @@
         turned_ref[:, start : start + LONG] = mix_in.T.astype(BF16)
 
 
-def backward_kernel(
-    valid_ref, dconv_ref, msg_ref, dq_ref, k_ref, v_ref, short_ref, long_ref, fwd_ref, inv_ref,
-    *refs,
-):
-    out_ref, ext_ref, gate_ref = refs[-3:]
-    valid = valid_ref[0]
-    fwd = fwd_ref[...]
-    inv = inv_ref[...]
-    gate_ref[0:TAIL] = msg_ref[0:TAIL]
-    gate_ref[TAIL : 2 * LONG] = jnp.zeros((2 * LONG - TAIL, LANES), BF16)
-    cos_h, sin_h, alt_h = filter_spectrum(fwd, long_ref[...])
-    sign = signs(2 * LONG)
-    blocks = ROWS // LONG
-    ext_ref[0, 0:ROWS] = dq_ref[...]
-    ext_ref[0, ROWS : ROWS + RIM] = msg_ref[TAIL : TAIL + RIM].astype(F32)
-    now = spectrum(fwd, dconv_ref[0:LONG])
-    for block in range(blocks + 1):
-        start = block * LONG
-        if block + 1 < blocks:
-            after = spectrum(fwd, dconv_ref[start + LONG : start + 2 * LONG])
-        else:
-            rim = (block + 1 - blocks) * LONG
-            after = spectrum(fwd, gate_ref[rim : rim + LONG])
-        window = now + sign * after
-        now = after
-        cos_x, sin_x = window[:LONG], window[LONG:]
-        product = jnp.concatenate(
-            [cos_x * cos_h + sin_x * sin_h, sin_x * alt_h - cos_x * sin_h], axis=0
-        )
-        gated = back(inv, product)
-        if block < blocks:
-            ext_ref[1, start : start + LONG] = gated * v_ref[start : start + LONG]
-            ext_ref[2, start : start + LONG] = gated * k_ref[start : start + LONG]
-        else:
-            rim = gated[:RIM]
-            v_rim = msg_ref[TAIL + RIM : TAIL + 2 * RIM].astype(F32)
-            k_rim = msg_ref[TAIL + 2 * RIM : TAIL + 3 * RIM].astype(F32)
-            ext_ref[1, ROWS : ROWS + RIM] = rim * v_rim
-            ext_ref[2, ROWS : ROWS + RIM] = rim * k_rim
-    for start in range(0, ROWS, STEP):
-        live = live_rows(valid, start, STEP)
+def correlate(now, after, sign, inv, cos_h, sin_h, alt_h):
+    window = now + sign * after
+    cos_x, sin_x = window[:LONG], window[LONG:]
+    product = jnp.concatenate(
+        [cos_x * cos_h + sin_x * sin_h, sin_x * alt_h - cos_x * sin_h], axis=0
+    )
+    return back(inv, product)
+
+
+def filter_back(valid, first, short_ref, ext_ref, out_ref):
+    for start in range(0, HALF, STEP):
+        live = live_rows(valid, first + start, STEP)
         for stream in range(3):
             total = short_ref[stream, 0:1] * ext_ref[stream, start : start + STEP]
             for tap in range(1, SHORT):
                 total += short_ref[stream, tap : tap + 1] * ext_ref[stream, start + tap : start + tap + STEP]
             out_ref[stream, start : start + STEP] = (total * live).astype(BF16)
+
+
+def backward_kernel(
+    valid_ref, dconv_ref, dq_ref, k_ref, v_ref, short_ref, long_ref, fwd_ref, inv_ref, *refs
+):
+    out_ref, ext_ref = refs[-2:]
+    fwd = fwd_ref[...]
+    inv = inv_ref[...]
+    taps = filter_spectrum(fwd, long_ref[...])
+    sign = signs(2 * LONG)
+    ext_ref[0, 0 : HALF + RIM] = dq_ref[0 : HALF + RIM]
+    now = spectrum(fwd, dconv_ref[0:LONG])
+    for start in range(0, HALF + LONG, LONG):
+        after = spectrum(fwd, dconv_ref[start + LONG : start + 2 * LONG])
+        gated = correlate(now, after, sign, inv, *taps)
+        now = after
+        rows = LONG if start < HALF else RIM
+        ext_ref[1, start : start + rows] = gated[:rows] * v_ref[start : start + rows]
+        ext_ref[2, start : start + rows] = gated[:rows] * k_ref[start : start + rows]
+    filter_back(valid_ref[0], 0, short_ref, ext_ref, out_ref)
+
+
+def backward_end_kernel(
+    valid_ref, dconv_ref, msg_ref, dq_ref, k_ref, v_ref, short_ref, long_ref, fwd_ref, inv_ref, *refs
+):
+    out_ref, ext_ref, gate_ref = refs[-3:]
+    fwd = fwd_ref[...]
+    inv = inv_ref[...]
+    taps = filter_spectrum(fwd, long_ref[...])
+    sign = signs(2 * LONG)
+    gate_ref[0:HALF] = dconv_ref[...]
+    gate_ref[HALF : HALF + TAIL] = msg_ref[0:TAIL]
+    gate_ref[HALF + TAIL : HALF + 2 * LONG] = jnp.zeros((2 * LONG - TAIL, LANES), BF16)
+    ext_ref[0, 0:HALF] = dq_ref[...]
+    ext_ref[0, HALF : HALF + RIM] = msg_ref[TAIL : TAIL + RIM].astype(F32)
+    now = spectrum(fwd, gate_ref[0:LONG])
+    for start in range(0, HALF + LONG, LONG):
+        after = spectrum(fwd, gate_ref[start + LONG : start + 2 * LONG])
+        gated = correlate(now, after, sign, inv, *taps)
+        now = after
+        if start < HALF:
+            ext_ref[1, start : start + LONG] = gated * v_ref[start : start + LONG]
+            ext_ref[2, start : start + LONG] = gated * k_ref[start : start + LONG]
+        else:
+            v_rim = msg_ref[TAIL + RIM : TAIL + 2 * RIM].astype(F32)
+            k_rim = msg_ref[TAIL + 2 * RIM : TAIL + 3 * RIM].astype(F32)
+            ext_ref[1, HALF : HALF + RIM] = gated[:RIM] * v_rim
+            ext_ref[2, HALF : HALF + RIM] = gated[:RIM] * k_rim
+    filter_back(valid_ref[0], HALF, short_ref, ext_ref, out_ref)
 
 
 def params(mib=20):
@@ -279,25 +299,45 @@
     )(info, streams, halo, short, long_taps, fwd, inv, q_side, k_side, v_side, gate, mix_in, turned, conv, *after)
 
 
-def run_backward(valid, d_conv, msg, d_q, k_side, v_side, short, long_taps, fwd, inv, after=()):
+def run_backward(info, d_conv, d_q, k_side, v_side, short, long_taps, fwd, inv, after=()):
     return pl.pallas_call(
         backward_kernel,
         grid=(CH // LANES,),
         in_specs=[
-            SMEM, lane_spec(ROWS), lane_spec(TAIL + 3 * RIM), lane_spec(ROWS), lane_spec(ROWS),
-            lane_spec(ROWS), lane_spec(3, SHORT), lane_spec(LONG),
+            SMEM, lane_spec(ROWS), lane_spec(ROWS), lane_spec(ROWS), lane_spec(ROWS),
+            lane_spec(3, SHORT), lane_spec(LONG),
             whole(2 * LONG, 2 * LONG), whole(2 * LONG, 2 * LONG),
         ] + [ANY] * len(after),
-        out_specs=lane_spec(3, ROWS),
+        out_specs=lane_spec(3, HALF),
         out_shape=jax.ShapeDtypeStruct((3, ROWS, CH), BF16),
+        scratch_shapes=[pltpu.VMEM((3, HALF + RIM, LANES), F32)],
+        compiler_params=params(56),
+        cost_estimate=cost(1000, 1000),
+        name="backward",
+    )(info, d_conv, d_q, k_side, v_side, short, long_taps, fwd, inv, *after)
+
+
+def run_backward_end(info, d_conv, msg, d_q, k_side, v_side, short, long_taps, fwd, inv, out, after=()):
+    low = pl.BlockSpec((HALF, LANES), lambda i: (1, i))
+    return pl.pallas_call(
+        backward_end_kernel,
+        grid=(CH // LANES,),
+        in_specs=[
+            SMEM, low, lane_spec(TAIL + 3 * RIM), low, low, low,
+            lane_spec(3, SHORT), lane_spec(LONG),
+            whole(2 * LONG, 2 * LONG), whole(2 * LONG, 2 * LONG), ANY,
+        ] + [ANY] * len(after),
+        out_specs=pl.BlockSpec((3, HALF, LANES), lambda i: (0, 1, i)),
+        out_shape=jax.ShapeDtypeStruct((3, ROWS, CH), BF16),
+        input_output_aliases={10: 0},
         scratch_shapes=[
-            pltpu.VMEM((3, ROWS + RIM, LANES), F32),
-            pltpu.VMEM((2 * LONG, LANES), BF16),
+            pltpu.VMEM((3, HALF + RIM, LANES), F32),
+            pltpu.VMEM((HALF + 2 * LONG, LANES), BF16),
         ],
         compiler_params=params(56),
         cost_estimate=cost(1000, 1000),
-        name="backward",
-    )(valid, d_conv, msg, d_q, k_side, v_side, short, long_taps, fwd, inv, *after)
+        name="backward_end",
+    )(info, d_conv, msg, d_q, k_side, v_side, short, long_taps, fwd, inv, out, *after)
 
 
 def project_kernel(order_ref, mix_ref, weight_ref, *refs):
@@ -520,12 +560,11 @@
     streams = qkv.transpose(1, 0, 2)
     short = short_filter.transpose(1, 0, 2)
 
-    below, above = along_y(cotangent, 1), along_y(cotangent, -1)
     tail, quarters = run_prepare(info, streams, cotangent)
     halo = neighbour(tail, 1)
     slab = exchange(quarters, "x")
     own = run_forward(info, streams, short, long_filter, forward_table, causal_table, (tail,))
-    slab, halo, below, above, held, *own = lax.optimization_barrier([slab, halo, below, above, cotangent, *own])
+    slab, halo, held, *own = lax.optimization_barrier([slab, halo, cotangent, *own])
     slab_copies = copies(slab)
     mine = exchange(slab_copies, "y").reshape(NY, NX, ROWS, LANES)
     mix_in, turned, q_side, k_side, v_side, conv = run_finish(
@@ -536,23 +575,26 @@
     turned[1], mix_in = lax.optimization_barrier((turned[1], mix_in))
     given = run_project(info, mix_in, out_weight)
     taken = other_core(given)
-    mine, far, given, *turned = lax.optimization_barrier([mine, far, given, *turned])
+    mine, far, given, held, *turned = lax.optimization_barrier([mine, far, given, held, *turned])
+    below, above = along_y(held, 1), along_y(held, -1)
     theirs = other_core(mine)
+    partial = run_outer(info, turned, mine, theirs)
+    below, above, far, partial = lax.optimization_barrier((below, above, far, partial))
     cots = jnp.stack([cotangent, below, above, far])
     cots_other = other_core(cots)
-    partial = run_outer(info, turned, mine, theirs)
     sums = exchange(partial, "z")
     up, down, next_top, last_bottom, own_out = run_project_add(info, mix_in, out_weight, taken, (partial,))
     from_below, from_above = along_y(up, 1), along_y(down, -1)
     d_conv, d_q, msg = run_d_mix(
         info, out_weight, cots, cots_other, (q_side, k_side, v_side, conv), (up,)
     )
-    top = along_y(add(next_top, from_below[:HALF]), 1)
-    bottom = along_y(add(last_bottom, from_above[HALF:]), -1)
+    from_below, from_above, msg = lax.optimization_barrier((from_below, from_above, msg))
+    next_top, last_bottom = add(next_top, from_below[:HALF]), add(last_bottom, from_above[HALF:])
+    top, bottom = along_y(next_top, 1), along_y(last_bottom, -1)
     msg = neighbour(msg, -1)
-    d_streams = run_backward(
-        info, d_conv, msg, d_q, k_side, v_side, short, long_filter, forward_table, anti_table
-    )
+    sides = (d_q, k_side, v_side, short, long_filter, forward_table, anti_table)
+    begun = run_backward(info, d_conv, *sides)
+    d_streams = run_backward_end(info, d_conv, msg, *sides, begun, (next_top, last_bottom))
     sums, d_streams, own_out = lax.optimization_barrier((sums, d_streams, own_out))
     d_qkv = d_streams.transpose(1, 0, 2)
     top = own_out[:HALF] + top.astype(F32) + from_above[:HALF].astype(F32)

time: 146 us -> 142 us (0.973)
  the two profiles are of different devices: /device:TPU:102 before, /device:TPU:26 now
where the time goes in v5:
time: 142 us; the launch traced here: 141 us
  Pallas kernels  42.3 us (30%)
  starting transfers between devices  41.6 us (29%)
  waiting for transfers between devices  32.3 us (23%)
  local copies, waits for them, and re-layouts  18.1 us (13%)
  other arithmetic  4.76 us (3%)
  between operations  1.59 us (1%)
    all_to_all x3, starting transfers between devices, exchange(): lax.all_to_all(array, 'tp' if axis == 'y' else 'ctx', 0, 0, axis_index_gr...  17.7 us
    ppermute x3, waiting for transfers between devices, along_x(): return lax.ppermute(array, 'ctx', pairs)  16.8 us
    unnamed x66, local copies, waits for them, and re-layouts  16.3 us
    ppermute x7, waiting for transfers between devices, along_y(): return lax.ppermute(array, 'tp', pairs)  10.7 us
    ppermute x2, starting transfers between devices, neighbour(): lax.ppermute(array, 'ctx', [(i, i + by) for i in range(count) if 0 <= i +...  9.33 us
    ppermute x7, starting transfers between devices, along_y(): return lax.ppermute(array, 'tp', pairs)  9.06 us
    pallas_call x1, Pallas kernels, run_forward(): pl.pallas_call(forward_kernel, grid=(CH // LANES,), in_specs=[SMEM, lane_...  6.82 us
    pallas_call x1, Pallas kernels, run_backward(): pl.pallas_call(backward_kernel, grid=(CH // LANES,), in_specs=[SMEM, lane...  6.66 us
  transfers between devices with their start and end apart: 18, of which 7 were waited for; matrix products, arithmetic and copies ran while one was open for 3% of the time, Pallas kernels for 29%

profile of v5, /device:TPU:26, one launch (start us, length us, event | category | flops | bytes accessed | tf_op | source)
XLA Modules:
  0.0 140.6 jit_solution(12457954150261344325)
XLA Ops:
  5.2 4.8 %all-to-all-start = ((bf16[4,512,128]{2,1,0:T(8,128)(2,1)}), bf16[4,512,128]{2,1,0:T(8,128)(2,1)S(1)}, u32[]{:S(2)}, u32[]{:S(2)}) async-start(bf16[4,512,128]{2,1,0:T(8,128)(2,1)} %get-tuple-element.55), calls=%async_computation | async-start | bytes 1048576 | tf_op jit(solution)/shard_map/all_to_all | solution.py:524
  10.1 3.4 %collective-permute-start = (bf16[304,512]{1,0:T(8,128)(2,1)S(1)}, bf16[304,512]{1,0:T(8,128)(2,1)S(1)}, u32[]{:S(2)}, u32[]{:S(2)}) collective-permute-start(bf16[304,512]{1,0:T(8,128)(2,1)S(1)} %get-tuple-element.56.refs_0_), channel_id=1, source_target_pairs={{0,8},{8,16},{16,24},{24,32},{32,40},{40,48},{48,56},{56,64},{64,7... | collective-permute-start | bytes 933896 | tf_op jit(solution)/shard_map/ppermute | solution.py:553
  13.5 6.8 %forward.1 = (bf16[512,512]{1,0:T(8,128)(2,1)}, bf16[512,512]{1,0:T(8,128)(2,1)}, f32[512,512]{1,0:T(8,128)}, f32[512,512]{1,0:T(8,128)}, f32[512,512]{1,0:T(8,1...) custom-call(s32[4]{0:T(128)} %copy-done.25, bf16[3,512,512]{2,1,0:T(8,128)(2,1)} %bitcast.10, f32[3,7,512]{2,1,0:T(8,128)} %bitcast.15, ...), custom_call_target="tpu_custom_call" | custom-call | flops 1000 | bytes 1000 | tf_op jit(solution)/shard_map/forward/pallas_call | solution.py:262
  20.3 2.7 %collective-permute-done.halo_ref = bf16[304,512]{1,0:T(8,128)(2,1)S(1)} collective-permute-done((bf16[304,512]{1,0:T(8,128)(2,1)S(1)}, bf16[304,512]{1,0:T(8,128)(2,1)S(1)}, u32[]{:S(2)}, u32[]{:S(2)}) %collective-permute-start) | collective-permute-done | bytes 311328 | tf_op jit(solution)/shard_map/ppermute | solution.py:553
  23.0 1.8 %broadcast_in_dim.2.refs_3_ = bf16[4,4,512,128]{3,2,1,0:T(8,128)(2,1)} broadcast(bf16[4,512,128]{2,1,0:T(8,128)(2,1)S(1)} %all-to-all-done), dimensions={1,2,3} | broadcast | bytes 2621440 | tf_op jit(solution)/shard_map/broadcast_in_dim | solution.py:544
  24.7 4.7 %all-to-all-start.1 = ((bf16[4,4,512,128]{3,2,1,0:T(8,128)(2,1)}), bf16[4,4,512,128]{3,2,1,0:T(8,128)(2,1)S(1)}, u32[]{:S(2)}, u32[]{:S(2)}) async-start(bf16[4,4,512,128]{3,2,1,0:T(8,128)(2,1)} %broadcast_in_dim.2.refs_3_), calls=%async_computation.1 | async-start | bytes 4194304 | tf_op jit(solution)/shard_map/all_to_all | solution.py:524
  29.4 5.8 %finish.1 = (bf16[512,512]{1,0:T(8,128)(2,1)}, bf16[512,512]{1,0:T(8,128)(2,1)}, f32[512,512]{1,0:T(8,128)}, f32[512,512]{1,0:T(8,128)}, f32[512,512]{1,0:T(8,128)}, /*index=5*/f32[512,512]{1,0:T(8,128)}) custom-call(s32[4]{0:T(128)} %copy-done.25, ...), custom_call_target="tpu_custom_call", output_to_operand_aliasing={{2}: (7, {}), {3}: (8, {}), {4}: (9, {}), {0}: (11, {}), {1... | custom-call | flops 1000 | bytes 1000 | tf_op jit(solution)/shard_map/finish/pallas_call | solution.py:282
  35.2 1.8 %collective-permute-start.2 = (bf16[512,512]{1,0:T(8,128)(2,1)}, bf16[512,512]{1,0:T(8,128)(2,1)S(1)}, u32[]{:S(2)}, u32[]{:S(2)}) collective-permute-start(bf16[512,512]{1,0:T(8,128)(2,1)} %get-tuple-element.81.refs_0_), channel_id=1, source_target_pairs={{0,8},{8,16},{16,24},{24,0},{32,40},{40,48},{48,56},{56,32},{64,72... | collective-permute-start | bytes 1572872 | tf_op jit(solution)/shard_map/ppermute | solution.py:535
  38.0 2.5 %collective-permute-start.4 = (bf16[512,512]{1,0:T(8,128)(2,1)}, bf16[512,512]{1,0:T(8,128)(2,1)S(1)}, u32[]{:S(2)}, u32[]{:S(2)}) collective-permute-start(bf16[512,512]{1,0:T(8,128)(2,1)} %get-tuple-element.81.refs_0_), channel_id=1, source_target_pairs={{0,24},{8,0},{16,8},{24,16},{32,56},{40,32},{48,40},{56,48},{64,88... | collective-permute-start | bytes 1572872 | tf_op jit(solution)/shard_map/ppermute | solution.py:535
  42.0 16.8 %collective-permute-done.2.refs_1_ = bf16[512,512]{1,0:T(8,128)(2,1)S(1)} collective-permute-done((bf16[512,512]{1,0:T(8,128)(2,1)}, bf16[512,512]{1,0:T(8,128)(2,1)S(1)}, u32[]{:S(2)}, u32[]{:S(2)}) %collective-permute-start.2) | collective-permute-done | bytes 524320 | tf_op jit(solution)/shard_map/ppermute | solution.py:535
  60.7 2.6 %project.1 = bf16[4,512,512]{2,1,0:T(8,128)(2,1)S(1)} custom-call(s32[4]{0:T(128)S(1)} %copy-done.26, bf16[512,512]{1,0:T(8,128)(2,1)S(1)} %copy-done.6, bf16[512,4096]{1,0:T(8,128)(2,1)S(1)} %copy-done), custom_call_target="tpu_custom_call" | custom-call | flops 1000 | bytes 1000 | tf_op jit(solution)/shard_map/project/pallas_call | solution.py:358
  66.7 1.7 %collective-permute-start.6 = (bf16[512,512]{1,0:T(8,128)(2,1)S(1)}, bf16[512,512]{1,0:T(8,128)(2,1)S(1)}, u32[]{:S(2)}, u32[]{:S(2)}) collective-permute-start(bf16[512,512]{1,0:T(8,128)(2,1)S(1)} %copy-done.14), channel_id=1, source_target_pairs={{0,6},{1,7},{2,0},{3,1},{4,2},{5,3},{6,4},{7,5},{8,14},{9,15},{10,... | collective-permute-start | bytes 1572872 | tf_op jit(solution)/shard_map/ppermute | solution.py:540
  68.4 2.0 %collective-permute-done.7.theirs = bf16[4,4,512,128]{3,2,1,0:T(8,128)(2,1)S(1)} collective-permute-done((bf16[4,4,512,128]{3,2,1,0:T(8,128)(2,1)S(1)}, bf16[4,4,512,128]{3,2,1,0:T(8,128)(2,1)S(1)}, u32[]{:S(2)}, u32[]{:S(2)}) %collective-permute-start.7) | collective-permute-done | bytes 2097184 | tf_op jit(solution)/shard_map/ppermute | solution.py:548
  73.6 4.0 %outer.1.refs_0_ = bf16[8,512,128]{2,1,0:T(8,128)(2,1)} custom-call(s32[4]{0:T(128)S(1)} %copy-done.26, bf16[4,4,512,128]{3,2,1,0:T(8,128)(2,1)S(1)} %all-to-all-done.1.mine, bf16[4,4,512,128]{3,2,1,0:T(8,128)(2,1)S(1)} %collective-permute-done.7.theirs, bf16[512,512]{1,0:T(8,128)(2,1)S(1)} %copy-done.15, bf16[512,512]{1,0:T(8,128)(2,1)S(1)} %copy-done.19, ...), custom_call_target="tpu_custom_call" | custom-call | flops 1000 | bytes 1000 | tf_op jit(solution)/shard_map/outer/pallas_call | solution.py:467
  77.5 3.1 %collective-permute-done.5 = bf16[512,512]{1,0:T(8,128)(2,1)S(1)} collective-permute-done((bf16[512,512]{1,0:T(8,128)(2,1)S(1)}, bf16[512,512]{1,0:T(8,128)(2,1)S(1)}, u32[]{:S(2)}, u32[]{:S(2)}) %collective-permute-start.5) | collective-permute-done | bytes 524320 | tf_op jit(solution)/shard_map/ppermute | solution.py:540
  83.3 8.2 %all-to-all-start.2 = ((bf16[8,512,128]{2,1,0:T(8,128)(2,1)}), bf16[8,512,128]{2,1,0:T(8,128)(2,1)}, u32[]{:S(2)}, u32[]{:S(2)}) async-start(bf16[8,512,128]{2,1,0:T(8,128)(2,1)} %outer.1.refs_0_), calls=%async_computation.2 | async-start | bytes 2097152 | tf_op jit(solution)/shard_map/all_to_all | solution.py:524
  91.5 2.2 %copy-done.1 = bf16[512,4096]{1,0:T(8,128)(2,1)S(1)} copy-done((bf16[512,4096]{1,0:T(8,128)(2,1)S(1)}, bf16[512,4096]{1,0:T(8,128)(2,1)}, u32[]{:S(2)}) %copy-start.1) | copy-done | bytes 4194328
  93.7 4.7 %project_add.1 = (bf16[512,512]{1,0:T(8,128)(2,1)S(1)}, bf16[512,512]{1,0:T(8,128)(2,1)S(1)}, bf16[256,512]{1,0:T(8,128)(2,1)S(1)}, bf16[256,512]{1,0:T(8,128)(2,1)S(1)}, f32[512,512]{1,0:T(8,128)S(1)}) custom-call(s32[4]{0:T(128)S(1)} %copy-done.26, bf16[512,512]{1,0:T(8,128)(2,1)S(1)} %copy-done.7, bf16[512,4096]{1,0:T(8,128)(2,1)S(1)} %copy-done.1, ...), custom_call_target="tpu_custom_call" | custom-call | flops 1000 | bytes 1000 | tf_op jit(solution)/shard_map/project_add/pallas_call | solution.py:405
  101.8 4.0 %d_mix.1 = (bf16[512,512]{1,0:T(8,128)(2,1)S(1)}, f32[512,512]{1,0:T(8,128)S(1)}, bf16[192,512]{1,0:T(8,128)(2,1)S(1)}) custom-call(s32[4]{0:T(128)S(1)} %copy-done.26, bf16[512,4096]{1,0:T(8,128)(2,1)S(1)} %copy-done.2, bf16[4,512,512]{2,1,0:T(8,128)(2,1)S(1)} %pad_maximum_fusion.mine, bf16[4,512,512]{2,1,0:T(8,128)(2,1)} %collective-permute-done.8.theirs, ...), custom_call_target="tpu_custom_call" | custom-call | flops 1000 | bytes 1000 | tf_op jit(solution)/shard_map/d_mix/pallas_call | solution.py:504
  107.6 4.9 %collective-permute-done.10 = bf16[512,512]{1,0:T(8,128)(2,1)S(1)} collective-permute-done((bf16[512,512]{1,0:T(8,128)(2,1)S(1)}, bf16[512,512]{1,0:T(8,128)(2,1)S(1)}, u32[]{:S(2)}, u32[]{:S(2)}) %collective-permute-start.10) | collective-permute-done | bytes 524320 | tf_op jit(solution)/shard_map/ppermute | solution.py:540
  113.9 6.0 %collective-permute-start.12 = (bf16[192,512]{1,0:T(8,128)(2,1)S(1)}, bf16[192,512]{1,0:T(8,128)(2,1)S(1)}, u32[]{:S(2)}, u32[]{:S(2)}) collective-permute-start(bf16[192,512]{1,0:T(8,128)(2,1)S(1)} %get-tuple-element.97), channel_id=1, source_target_pairs={{8,0},{16,8},{24,16},{32,24},{40,32},{48,40},{56,48},{64,56},{72,6... | collective-permute-start | bytes 589832 | tf_op jit(solution)/shard_map/ppermute | solution.py:553
  120.4 3.0 %collective-permute-start.13 = (bf16[256,512]{1,0:T(8,128)(2,1)S(1)}, bf16[256,512]{1,0:T(8,128)(2,1)S(1)}, u32[]{:S(2)}, u32[]{:S(2)}) collective-permute-start(bf16[256,512]{1,0:T(8,128)(2,1)S(1)} %add_convert_fusion.3.refs_1_), channel_id=1, source_target_pairs={{0,2},{1,3},{2,4},{3,5},{4,6},{5,7},{6,0},{7,1},{8,10},{9,11},{10,... | collective-permute-start | bytes 786440 | tf_op jit(solution)/shard_map/ppermute | solution.py:540
  123.4 6.7 %backward.1.refs_0_ = bf16[3,512,512]{2,1,0:T(8,128)(2,1)} custom-call(s32[4]{0:T(128)} %copy-done.25, bf16[512,512]{1,0:T(8,128)(2,1)} %copy-done.11, f32[512,512]{1,0:T(8,128)} %copy-done.10, f32[512,512]{1,0:T(8,128)} %get-tuple-element.90.k_ref, f32[512,512]{1,0:T(8,128)} %get-tuple-element.91.v_ref, f32[3,7,512]{2,1,0:T(8,128)} %bitcast.17, ...), custom_call_target="tpu_custom_call" | custom-call | flops 1000 | bytes 1000 | tf_op jit(solution)/shard_map/backward/pallas_call | solution.py:303
  130.8 6.5 %backward_end.1 = bf16[3,512,512]{2,1,0:T(8,128)(2,1)} custom-call(s32[4]{0:T(128)} %copy-done.25, bf16[512,512]{1,0:T(8,128)(2,1)} %copy-done.11, bf16[192,512]{1,0:T(8,128)(2,1)} %copy-done.32, f32[512,512]{1,0:T(8,128)} %copy-done.10, f32[512,512]{1,0:T(8,128)} %get-tuple-element.90.k_ref, ...), custom_call_target="tpu_custom_call", output_to_operand_aliasing={{}: (10, {})} | custom-call | flops 1000 | bytes 1000 | tf_op jit(solution)/shard_map/backward_end/pallas_call | solution.py:322
  (96 shorter events, 28.5 us)
Async XLA Ops:
  1.4 12.1 %copy-start.25 = (s32[4]{0:T(128)}, s32[4]{0:T(128)S(1)}, u32[]{:S(2)}) copy-start(s32[4]{0:T(128)S(1)} %pad_add_fusion.info_ref.valid_ref.order_ref) | copy-start | bytes 52
  5.2 17.7 %all-to-all-start = ((bf16[4,512,128]{2,1,0:T(8,128)(2,1)}), bf16[4,512,128]{2,1,0:T(8,128)(2,1)S(1)}, u32[]{:S(2)}, u32[]{:S(2)}) async-start(bf16[4,512,128]{2,1,0:T(8,128)(2,1)} %get-tuple-element.55), calls=%async_computation | async-start | bytes 1048576 | tf_op jit(solution)/shard_map/all_to_all | solution.py:524
  10.1 12.9 %collective-permute-start = (bf16[304,512]{1,0:T(8,128)(2,1)S(1)}, bf16[304,512]{1,0:T(8,128)(2,1)S(1)}, u32[]{:S(2)}, u32[]{:S(2)}) collective-permute-start(bf16[304,512]{1,0:T(8,128)(2,1)S(1)} %get-tuple-element.56.refs_0_), channel_id=1, source_target_pairs={{0,8},{8,16},{16,24},{24,32},{32,40},{40,48},{48,56},{56,64},{64,7... | collective-permute-start | bytes 933896 | tf_op jit(solution)/shard_map/ppermute | solution.py:553
  24.7 41.5 %all-to-all-start.1 = ((bf16[4,4,512,128]{3,2,1,0:T(8,128)(2,1)}), bf16[4,4,512,128]{3,2,1,0:T(8,128)(2,1)S(1)}, u32[]{:S(2)}, u32[]{:S(2)}) async-start(bf16[4,4,512,128]{3,2,1,0:T(8,128)(2,1)} %broadcast_in_dim.2.refs_3_), calls=%async_computation.1 | async-start | bytes 4194304 | tf_op jit(solution)/shard_map/all_to_all | solution.py:524
  29.4 11.1 %copy-start.14 = (bf16[512,512]{1,0:T(8,128)(2,1)S(1)}, bf16[512,512]{1,0:T(8,128)(2,1)}, u32[]{:S(2)}) copy-start(bf16[512,512]{1,0:T(8,128)(2,1)} %cot_ref.1) | copy-start | bytes 1572868
  29.4 30.2 %copy-start = (bf16[512,4096]{1,0:T(8,128)(2,1)S(1)}, bf16[512,4096]{1,0:T(8,128)(2,1)}, u32[]{:S(2)}) copy-start(bf16[512,4096]{1,0:T(8,128)(2,1)} %weight_ref.5) | copy-start | bytes 12582916
  29.4 30.2 %copy-start.26 = (s32[4]{0:T(128)S(1)}, s32[4]{0:T(128)}, u32[]{:S(2)}) copy-start(s32[4]{0:T(128)} %copy-done.25) | copy-start | bytes 52
  35.2 23.6 %collective-permute-start.2 = (bf16[512,512]{1,0:T(8,128)(2,1)}, bf16[512,512]{1,0:T(8,128)(2,1)S(1)}, u32[]{:S(2)}, u32[]{:S(2)}) collective-permute-start(bf16[512,512]{1,0:T(8,128)(2,1)} %get-tuple-element.81.refs_0_), channel_id=1, source_target_pairs={{0,8},{8,16},{16,24},{24,0},{32,40},{40,48},{48,56},{56,32},{64,72... | collective-permute-start | bytes 1572872 | tf_op jit(solution)/shard_map/ppermute | solution.py:535
  37.0 27.6 %collective-permute-start.3 = (bf16[512,512]{1,0:T(8,128)(2,1)}, bf16[512,512]{1,0:T(8,128)(2,1)S(1)}, u32[]{:S(2)}, u32[]{:S(2)}) collective-permute-start(bf16[512,512]{1,0:T(8,128)(2,1)} %get-tuple-element.81.refs_0_), channel_id=1, source_target_pairs={{0,16},{8,24},{16,0},{24,8},{32,48},{40,56},{48,32},{56,40},{64,80... | collective-permute-start | bytes 1572872 | tf_op jit(solution)/shard_map/ppermute | solution.py:535
  38.0 27.5 %collective-permute-start.4 = (bf16[512,512]{1,0:T(8,128)(2,1)}, bf16[512,512]{1,0:T(8,128)(2,1)S(1)}, u32[]{:S(2)}, u32[]{:S(2)}) collective-permute-start(bf16[512,512]{1,0:T(8,128)(2,1)} %get-tuple-element.81.refs_0_), channel_id=1, source_target_pairs={{0,24},{8,0},{16,8},{24,16},{32,56},{40,32},{48,40},{56,48},{64,88... | collective-permute-start | bytes 1572872 | tf_op jit(solution)/shard_map/ppermute | solution.py:535
  40.6 25.7 %collective-permute-start.1 = (bf16[512,512]{1,0:T(8,128)(2,1)S(1)}, bf16[512,512]{1,0:T(8,128)(2,1)}, u32[]{:S(2)}, u32[]{:S(2)}) collective-permute-start(bf16[512,512]{1,0:T(8,128)(2,1)S(1)} %copy-done.14), channel_id=1, source_target_pairs={{0,4},{1,5},{2,6},{3,7},{4,0},{5,1},{6,2},{7,3},{8,12},{9,13},{10,... | collective-permute-start | bytes 1572872 | tf_op jit(solution)/shard_map/ppermute | solution.py:540
  60.7 9.8 %copy-start.15 = (bf16[512,512]{1,0:T(8,128)(2,1)S(1)}, bf16[512,512]{1,0:T(8,128)(2,1)}, u32[]{:S(2)}) copy-start(bf16[512,512]{1,0:T(8,128)(2,1)} %get-tuple-element.81.refs_0_) | copy-start | bytes 1572868
  66.3 4.2 %collective-permute-start.7 = (bf16[4,4,512,128]{3,2,1,0:T(8,128)(2,1)S(1)}, bf16[4,4,512,128]{3,2,1,0:T(8,128)(2,1)S(1)}, u32[]{:S(2)}, u32[]{:S(2)}) collective-permute-start(bf16[4,4,512,128]{3,2,1,0:T(8,128)(2,1)S(1)} %all-to-all-done.1.mine), channel_id=1, source_target_pairs={{0,1},{1,0},{2,3},{3,2},{4,5},{5,4},{6,7},{7,6},{8,9},{9,8},{10,11... | collective-permute-start | bytes 6291464 | tf_op jit(solution)/shard_map/ppermute | solution.py:548
  66.3 14.3 %collective-permute-start.5 = (bf16[512,512]{1,0:T(8,128)(2,1)S(1)}, bf16[512,512]{1,0:T(8,128)(2,1)S(1)}, u32[]{:S(2)}, u32[]{:S(2)}) collective-permute-start(bf16[512,512]{1,0:T(8,128)(2,1)S(1)} %copy-done.14), channel_id=1, source_target_pairs={{0,2},{1,3},{2,4},{3,5},{4,6},{5,7},{6,0},{7,1},{8,10},{9,11},{10,... | collective-permute-start | bytes 1572872 | tf_op jit(solution)/shard_map/ppermute | solution.py:540
  66.7 15.2 %collective-permute-start.6 = (bf16[512,512]{1,0:T(8,128)(2,1)S(1)}, bf16[512,512]{1,0:T(8,128)(2,1)S(1)}, u32[]{:S(2)}, u32[]{:S(2)}) collective-permute-start(bf16[512,512]{1,0:T(8,128)(2,1)S(1)} %copy-done.14), channel_id=1, source_target_pairs={{0,6},{1,7},{2,0},{3,1},{4,2},{5,3},{6,4},{7,5},{8,14},{9,15},{10,... | collective-permute-start | bytes 1572872 | tf_op jit(solution)/shard_map/ppermute | solution.py:540
  68.4 23.1 %collective-permute-start.9 = (bf16[4,512,512]{2,1,0:T(8,128)(2,1)}, bf16[4,512,512]{2,1,0:T(8,128)(2,1)}, u32[]{:S(2)}, u32[]{:S(2)}) collective-permute-start(bf16[4,512,512]{2,1,0:T(8,128)(2,1)} %copy-done.12), channel_id=1, source_target_pairs={{0,1},{1,0},{2,3},{3,2},{4,5},{5,4},{6,7},{7,6},{8,9},{9,8},{10,11... | collective-permute-start | bytes 6291464 | tf_op jit(solution)/shard_map/ppermute | solution.py:548
  83.2 17.4 %collective-permute-start.8 = (bf16[4,512,512]{2,1,0:T(8,128)(2,1)S(1)}, bf16[4,512,512]{2,1,0:T(8,128)(2,1)}, u32[]{:S(2)}, u32[]{:S(2)}) collective-permute-start(bf16[4,512,512]{2,1,0:T(8,128)(2,1)S(1)} %pad_maximum_fusion.mine), channel_id=1, source_target_pairs={{0,1},{1,0},{2,3},{3,2},{4,5},{5,4},{6,7},{7,6},{8,9},{9,8},{10,11... | collective-permute-start | bytes 6291464 | tf_op jit(solution)/shard_map/ppermute | solution.py:548
  83.3 54.0 %all-to-all-start.2 = ((bf16[8,512,128]{2,1,0:T(8,128)(2,1)}), bf16[8,512,128]{2,1,0:T(8,128)(2,1)}, u32[]{:S(2)}, u32[]{:S(2)}) async-start(bf16[8,512,128]{2,1,0:T(8,128)(2,1)} %outer.1.refs_0_), calls=%async_computation.2 | async-start | bytes 2097152 | tf_op jit(solution)/shard_map/all_to_all | solution.py:524
  98.4 14.0 %collective-permute-start.10 = (bf16[512,512]{1,0:T(8,128)(2,1)S(1)}, bf16[512,512]{1,0:T(8,128)(2,1)S(1)}, u32[]{:S(2)}, u32[]{:S(2)}) collective-permute-start(bf16[512,512]{1,0:T(8,128)(2,1)S(1)} %get-tuple-element.93.refs_0_), channel_id=1, source_target_pairs={{0,2},{1,3},{2,4},{3,5},{4,6},{5,7},{6,0},{7,1},{8,10},{9,11},{10,... | collective-permute-start | bytes 1572872 | tf_op jit(solution)/shard_map/ppermute | solution.py:540
  99.0 14.9 %collective-permute-start.11 = (bf16[512,512]{1,0:T(8,128)(2,1)S(1)}, bf16[512,512]{1,0:T(8,128)(2,1)S(1)}, u32[]{:S(2)}, u32[]{:S(2)}) collective-permute-start(bf16[512,512]{1,0:T(8,128)(2,1)S(1)} %get-tuple-element.95), channel_id=1, source_target_pairs={{0,6},{1,7},{2,0},{3,1},{4,2},{5,3},{6,4},{7,5},{8,14},{9,15},{10,... | collective-permute-start | bytes 1572872 | tf_op jit(solution)/shard_map/ppermute | solution.py:540
  113.9 16.2 %collective-permute-start.12 = (bf16[192,512]{1,0:T(8,128)(2,1)S(1)}, bf16[192,512]{1,0:T(8,128)(2,1)S(1)}, u32[]{:S(2)}, u32[]{:S(2)}) collective-permute-start(bf16[192,512]{1,0:T(8,128)(2,1)S(1)} %get-tuple-element.97), channel_id=1, source_target_pairs={{8,0},{16,8},{24,16},{32,24},{40,32},{48,40},{56,48},{64,56},{72,6... | collective-permute-start | bytes 589832 | tf_op jit(solution)/shard_map/ppermute | solution.py:553
  119.9 10.2 %copy-start.27 = (bf16[256,512]{1,0:T(8,128)(2,1)}, bf16[256,512]{1,0:T(8,128)(2,1)S(1)}, u32[]{:S(2)}) copy-start(bf16[256,512]{1,0:T(8,128)(2,1)S(1)} %add_convert_fusion.2.refs_2_) | copy-start | bytes 786436
  120.0 19.5 %collective-permute-start.14 = (bf16[256,512]{1,0:T(8,128)(2,1)S(1)}, bf16[256,512]{1,0:T(8,128)(2,1)S(1)}, u32[]{:S(2)}, u32[]{:S(2)}) collective-permute-start(bf16[256,512]{1,0:T(8,128)(2,1)S(1)} %add_convert_fusion.2.refs_2_), channel_id=1, source_target_pairs={{0,6},{1,7},{2,0},{3,1},{4,2},{5,3},{6,4},{7,5},{8,14},{9,15},{10,... | collective-permute-start | bytes 786440 | tf_op jit(solution)/shard_map/ppermute | solution.py:540
  120.4 19.1 %collective-permute-start.13 = (bf16[256,512]{1,0:T(8,128)(2,1)S(1)}, bf16[256,512]{1,0:T(8,128)(2,1)S(1)}, u32[]{:S(2)}, u32[]{:S(2)}) collective-permute-start(bf16[256,512]{1,0:T(8,128)(2,1)S(1)} %add_convert_fusion.3.refs_1_), channel_id=1, source_target_pairs={{0,2},{1,3},{2,4},{3,5},{4,6},{5,7},{6,0},{7,1},{8,10},{9,11},{10,... | collective-permute-start | bytes 786440 | tf_op jit(solution)/shard_map/ppermute | solution.py:540
  (27 other events, 97.1 us)

commit v6 on v4

--- a/solution.py
+++ b/solution.py
@@ -403,7 +403,7 @@
             jax.ShapeDtypeStruct((RIM + 2 * TAIL, CH), BF16),
             jax.ShapeDtypeStruct((NX, ROWS, LANES), BF16),
         ],
-        compiler_params=params(),
+        compiler_params=params(56),
         cost_estimate=cost(1000, 1000),
         name="prepare",
     )(info, streams, cotangent)
@@ -419,6 +419,7 @@
             both = jnp.concatenate([mine[y, x], theirs[y, x]], axis=1)
             part = jnp.dot(turned[behind][...], both, preferred_element_type=F32)
             total = part if total is None else total + part
+        total = total * (1.0 / np.sqrt(float(ROWS * NZ * NX)))
         out_ref[2 * y + core] = total[:, :LANES].astype(BF16)
         out_ref[2 * y + 1 - core] = total[:, LANES:].astype(BF16)
 
@@ -520,12 +521,11 @@
     streams = qkv.transpose(1, 0, 2)
     short = short_filter.transpose(1, 0, 2)
 
-    below, above = along_y(cotangent, 1), along_y(cotangent, -1)
     tail, quarters = run_prepare(info, streams, cotangent)
     halo = neighbour(tail, 1)
     slab = exchange(quarters, "x")
     own = run_forward(info, streams, short, long_filter, forward_table, causal_table, (tail,))
-    slab, halo, below, above, held, *own = lax.optimization_barrier([slab, halo, below, above, cotangent, *own])
+    slab, held, *_ = lax.optimization_barrier([slab, cotangent, halo, *own])
     slab_copies = copies(slab)
     mine = exchange(slab_copies, "y").reshape(NY, NX, ROWS, LANES)
     mix_in, turned, q_side, k_side, v_side, conv = run_finish(
@@ -533,32 +533,36 @@
     )
     turned = [turned] + [along_x(turned, ahead) for ahead in (1, 2, 3)]
     far = along_y(held, 2)
-    turned[1], mix_in = lax.optimization_barrier((turned[1], mix_in))
-    given = run_project(info, mix_in, out_weight)
+    given = run_project(info, mix_in, out_weight, (turned[1],))
     taken = other_core(given)
-    mine, far, given, *turned = lax.optimization_barrier([mine, far, given, *turned])
-    theirs = other_core(mine)
-    cots = jnp.stack([cotangent, below, above, far])
+    held, _ = lax.optimization_barrier((held, turned[1]))
+    below, above = along_y(held, 1), along_y(held, -1)
+    ready, *_ = lax.optimization_barrier([mine, far, given, *turned])
+    theirs = other_core(ready)
+    partial = run_outer(info, turned, mine, theirs)
+    held, _ = lax.optimization_barrier((cotangent, partial))
+    cots = jnp.stack([held, below, above, far])
     cots_other = other_core(cots)
-    partial = run_outer(info, turned, mine, theirs)
     sums = exchange(partial, "z")
     up, down, next_top, last_bottom, own_out = run_project_add(info, mix_in, out_weight, taken, (partial,))
     from_below, from_above = along_y(up, 1), along_y(down, -1)
     d_conv, d_q, msg = run_d_mix(
         info, out_weight, cots, cots_other, (q_side, k_side, v_side, conv), (up,)
     )
-    top = along_y(add(next_top, from_below[:HALF]), 1)
-    bottom = along_y(add(last_bottom, from_above[HALF:]), -1)
+    from_below, from_above, _ = lax.optimization_barrier((from_below, from_above, msg))
+    next_top, last_bottom = add(next_top, from_below[:HALF]), add(last_bottom, from_above[HALF:])
+    top, bottom = along_y(next_top, 1), along_y(last_bottom, -1)
     msg = neighbour(msg, -1)
     d_streams = run_backward(
-        info, d_conv, msg, d_q, k_side, v_side, short, long_filter, forward_table, anti_table
+        info, d_conv, msg, d_q, k_side, v_side, short, long_filter, forward_table, anti_table,
+        (next_top, last_bottom),
     )
-    sums, d_streams, own_out = lax.optimization_barrier((sums, d_streams, own_out))
+    sums, own_out, _ = lax.optimization_barrier((sums, own_out, d_streams))
     d_qkv = d_streams.transpose(1, 0, 2)
     top = own_out[:HALF] + top.astype(F32) + from_above[:HALF].astype(F32)
     bottom = own_out[HALF:] + bottom.astype(F32) + from_below[HALF:].astype(F32)
     mixed = jnp.concatenate([top, bottom], axis=0).astype(BF16)
-    d_weight = jnp.sum(sums.astype(F32), axis=0) * (1.0 / jnp.sqrt(jnp.float32(ROWS * NZ * NX)))
+    d_weight = jnp.sum(sums.astype(F32), axis=0)
     return mixed, d_qkv, d_weight
 
 

time: 146 us -> 141 us (0.966)
  Pallas kernels: 41.4 us -> 39.3 us
  other arithmetic: 7.02 us -> 5.22 us
    ppermute x3, waiting for transfers between devices: 13.9 us -> 16.3 us  [along_x(): return lax.ppermute(array, 'ctx', pairs)]
    ppermute x2, waiting for transfers between devices: 12.2 us -> 9.83 us  [neighbour(): lax.ppermute(array, 'ctx', [(i, i + by) for i in range(count) if 0 <= i +...]
    ppermute x3, waiting for transfers between devices: 3.78 us -> 2.13 us  [other_core(): return lax.ppermute(array, 'tp', [(i, i ^ 1) for i in range(2 * NY)])]
    unnamed x58 -> x52, local copies, waits for them, and re-layouts: 12.3 us -> 12 us
  transfers between devices with their start and end apart: 18 -> 18, of which waited for: 8 -> 8; matrix products, arithmetic and copies ran while one was open for 3% -> 3% of each run, Pallas kernels for 29% -> 27%
where the time goes in v6:
time: 141 us; the launch traced here: 140 us
  starting transfers between devices  40.7 us (29%)
  Pallas kernels  39.3 us (28%)
  waiting for transfers between devices  39.1 us (28%)
  local copies, waits for them, and re-layouts  13.8 us (10%)
  other arithmetic  5.22 us (4%)
  between operations  1.52 us (1%)
    all_to_all x3, starting transfers between devices, exchange(): lax.all_to_all(array, 'tp' if axis == 'y' else 'ctx', 0, 0, axis_index_gr...  17 us
    ppermute x3, waiting for transfers between devices, along_x(): return lax.ppermute(array, 'ctx', pairs)  16.3 us
    ppermute x7, starting transfers between devices, along_y(): return lax.ppermute(array, 'tp', pairs)  12.2 us
    unnamed x52, local copies, waits for them, and re-layouts  12 us
    ppermute x7, waiting for transfers between devices, along_y(): return lax.ppermute(array, 'tp', pairs)  10.9 us
    ppermute x2, waiting for transfers between devices, neighbour(): lax.ppermute(array, 'ctx', [(i, i + by) for i in range(count) if 0 <= i +...  9.83 us
    pallas_call x1, Pallas kernels, run_backward(): pl.pallas_call(backward_kernel, grid=(CH // LANES,), in_specs=[SMEM, lane...  9.32 us
    ppermute x2, starting transfers between devices, neighbour(): lax.ppermute(array, 'ctx', [(i, i + by) for i in range(count) if 0 <= i +...  7.86 us
  transfers between devices with their start and end apart: 18, of which 8 were waited for; matrix products, arithmetic and copies ran while one was open for 3% of the time, Pallas kernels for 27%

profile of v6, /device:TPU:102, one launch (start us, length us, event | category | flops | bytes accessed | tf_op | source)
XLA Modules:
  0.0 139.6 jit_solution(12973441861935381823)
XLA Ops:
  1.9 2.3 %prepare.1 = (bf16[304,512]{1,0:T(8,128)(2,1)}, bf16[4,512,128]{2,1,0:T(8,128)(2,1)}) custom-call(s32[4]{0:T(128)} %pad_add_fusion.info_ref.valid_ref.order_ref, bf16[3,512,512]{2,1,0:T(8,128)(2,1)} %bitcast.10, bf16[512,512]{1,0:T(8,128)(2,1)} %cot_ref.1), custom_call_target="tpu_custom_call" | custom-call | flops 1000 | bytes 1000 | tf_op jit(solution)/shard_map/prepare/pallas_call | solution.py:397
  4.2 4.8 %all-to-all-start = ((bf16[4,512,128]{2,1,0:T(8,128)(2,1)}), bf16[4,512,128]{2,1,0:T(8,128)(2,1)S(1)}, u32[]{:S(2)}, u32[]{:S(2)}) async-start(bf16[4,512,128]{2,1,0:T(8,128)(2,1)} %get-tuple-element.35), calls=%async_computation | async-start | bytes 1048576 | tf_op jit(solution)/shard_map/all_to_all | solution.py:485
  9.0 4.5 %collective-permute-start = (bf16[304,512]{1,0:T(8,128)(2,1)}, bf16[304,512]{1,0:T(8,128)(2,1)S(1)}, u32[]{:S(2)}, u32[]{:S(2)}) collective-permute-start(bf16[304,512]{1,0:T(8,128)(2,1)} %get-tuple-element.36.refs_0_), channel_id=1, source_target_pairs={{0,8},{8,16},{16,24},{24,32},{32,40},{40,48},{48,56},{56,64},{64,7... | collective-permute-start | bytes 933896 | tf_op jit(solution)/shard_map/ppermute | solution.py:514
  13.5 6.8 %forward.1 = (bf16[512,512]{1,0:T(8,128)(2,1)}, bf16[512,512]{1,0:T(8,128)(2,1)}, f32[512,512]{1,0:T(8,128)}, f32[512,512]{1,0:T(8,128)}, f32[512,512]{1,0:T(8,1...) custom-call(s32[4]{0:T(128)} %pad_add_fusion.info_ref.valid_ref.order_ref, bf16[3,512,512]{2,1,0:T(8,128)(2,1)} %bitcast.11, ...), custom_call_target="tpu_custom_call" | custom-call | flops 1000 | bytes 1000 | tf_op jit(solution)/shard_map/forward/pallas_call | solution.py:242
  20.3 2.2 %collective-permute-done.halo_ref = bf16[304,512]{1,0:T(8,128)(2,1)S(1)} collective-permute-done((bf16[304,512]{1,0:T(8,128)(2,1)}, bf16[304,512]{1,0:T(8,128)(2,1)S(1)}, u32[]{:S(2)}, u32[]{:S(2)}) %collective-permute-start) | collective-permute-done | bytes 311328 | tf_op jit(solution)/shard_map/ppermute | solution.py:514
  24.2 4.5 %all-to-all-start.1 = ((bf16[4,4,512,128]{3,2,1,0:T(8,128)(2,1)}), bf16[4,4,512,128]{3,2,1,0:T(8,128)(2,1)S(1)}, u32[]{:S(2)}, u32[]{:S(2)}) async-start(bf16[4,4,512,128]{3,2,1,0:T(8,128)(2,1)} %broadcast_in_dim.2.refs_3_), calls=%async_computation.1 | async-start | bytes 4194304 | tf_op jit(solution)/shard_map/all_to_all | solution.py:485
  28.7 5.8 %finish.1 = (bf16[512,512]{1,0:T(8,128)(2,1)}, bf16[512,512]{1,0:T(8,128)(2,1)}, f32[512,512]{1,0:T(8,128)}, f32[512,512]{1,0:T(8,128)}, f32[512,512]{1,0:T(8,128)}, /*index=5*/f32[512,512]{1,0:T(8,128)}) custom-call(s32[4]{0:T(128)} %pad_add_fusion.info_ref.valid_ref.order_ref, ...), custom_call_target="tpu_custom_call", output_to_operand_aliasing={{2}: (7, {}), {3}: (8, {}), {4}: (9, {}), {0}: (11, {}), {1... | custom-call | flops 1000 | bytes 1000 | tf_op jit(solution)/shard_map/finish/pallas_call | solution.py:262
  34.5 2.5 %collective-permute-start.2 = (bf16[512,512]{1,0:T(8,128)(2,1)}, bf16[512,512]{1,0:T(8,128)(2,1)S(1)}, u32[]{:S(2)}, u32[]{:S(2)}) collective-permute-start(bf16[512,512]{1,0:T(8,128)(2,1)} %get-tuple-element.47.refs_0_), channel_id=1, source_target_pairs={{0,8},{8,16},{16,24},{24,0},{32,40},{40,48},{48,56},{56,32},{64,72... | collective-permute-start | bytes 1572872 | tf_op jit(solution)/shard_map/ppermute | solution.py:496
  36.9 3.5 %collective-permute-start.1 = (bf16[512,512]{1,0:T(8,128)(2,1)}, bf16[512,512]{1,0:T(8,128)(2,1)S(1)}, u32[]{:S(2)}, u32[]{:S(2)}) collective-permute-start(bf16[512,512]{1,0:T(8,128)(2,1)} %cot_ref.1), channel_id=1, source_target_pairs={{0,4},{1,5},{2,6},{3,7},{4,0},{5,1},{6,2},{7,3},{8,12},{9,13},{10,... | collective-permute-start | bytes 1572872 | tf_op jit(solution)/shard_map/ppermute | solution.py:501
  41.4 16.3 %collective-permute-done.2.refs_0_.refs_1_ = bf16[512,512]{1,0:T(8,128)(2,1)S(1)} collective-permute-done((bf16[512,512]{1,0:T(8,128)(2,1)}, bf16[512,512]{1,0:T(8,128)(2,1)S(1)}, u32[]{:S(2)}, u32[]{:S(2)}) %collective-permute-start.2) | collective-permute-done | bytes 524320 | tf_op jit(solution)/shard_map/ppermute | solution.py:496
  58.8 2.6 %project.1 = bf16[4,512,512]{2,1,0:T(8,128)(2,1)S(1)} custom-call(s32[4]{0:T(128)S(1)} %copy-done.19, bf16[512,512]{1,0:T(8,128)(2,1)S(1)} %copy-done.5, bf16[512,4096]{1,0:T(8,128)(2,1)S(1)} %copy-done, bf16[512,512]{1,0:T(8,128)(2,1)S(1)} %collective-permute-done.2.refs_0_.refs_1_), custom_call_target="tpu_custom_call" | custom-call | flops 1000 | bytes 1000 | tf_op jit(solution)/shard_map/project/pallas_call | solution.py:318
  62.6 2.4 %collective-permute-done.1 = bf16[512,512]{1,0:T(8,128)(2,1)S(1)} collective-permute-done((bf16[512,512]{1,0:T(8,128)(2,1)}, bf16[512,512]{1,0:T(8,128)(2,1)S(1)}, u32[]{:S(2)}, u32[]{:S(2)}) %collective-permute-start.1) | collective-permute-done | bytes 524320 | tf_op jit(solution)/shard_map/ppermute | solution.py:501
  69.6 2.1 %collective-permute-done.5.theirs = bf16[4,4,512,128]{3,2,1,0:T(8,128)(2,1)S(1)} collective-permute-done((bf16[4,4,512,128]{3,2,1,0:T(8,128)(2,1)S(1)}, bf16[4,4,512,128]{3,2,1,0:T(8,128)(2,1)S(1)}, u32[]{:S(2)}, u32[]{:S(2)}) %collective-permute-start.5) | collective-permute-done | bytes 2097184 | tf_op jit(solution)/shard_map/ppermute | solution.py:509
  73.8 3.9 %outer.1.refs_0_ = bf16[8,512,128]{2,1,0:T(8,128)(2,1)} custom-call(s32[4]{0:T(128)S(1)} %copy-done.19, bf16[4,4,512,128]{3,2,1,0:T(8,128)(2,1)S(1)} %all-to-all-done.1.mine, bf16[4,4,512,128]{3,2,1,0:T(8,128)(2,1)S(1)} %collective-permute-done.5.theirs, bf16[512,512]{1,0:T(8,128)(2,1)S(1)} %copy-done.10, ...), custom_call_target="tpu_custom_call" | custom-call | flops 1000 | bytes 1000 | tf_op jit(solution)/shard_map/outer/pallas_call | solution.py:428
  77.7 4.4 %collective-permute-done.8 = bf16[512,512]{1,0:T(8,128)(2,1)S(1)} collective-permute-done((bf16[512,512]{1,0:T(8,128)(2,1)}, bf16[512,512]{1,0:T(8,128)(2,1)S(1)}, u32[]{:S(2)}, u32[]{:S(2)}) %collective-permute-start.8) | collective-permute-done | bytes 524320 | tf_op jit(solution)/shard_map/ppermute | solution.py:501
  85.6 7.8 %all-to-all-start.2 = ((bf16[8,512,128]{2,1,0:T(8,128)(2,1)}), bf16[8,512,128]{2,1,0:T(8,128)(2,1)}, u32[]{:S(2)}, u32[]{:S(2)}) async-start(bf16[8,512,128]{2,1,0:T(8,128)(2,1)} %outer.1.refs_0_), calls=%async_computation.2 | async-start | bytes 2097152 | tf_op jit(solution)/shard_map/all_to_all | solution.py:485
  93.5 2.2 %copy-done.1 = bf16[512,4096]{1,0:T(8,128)(2,1)S(1)} copy-done((bf16[512,4096]{1,0:T(8,128)(2,1)S(1)}, bf16[512,4096]{1,0:T(8,128)(2,1)}, u32[]{:S(2)}) %copy-start.1) | copy-done | bytes 4194328
  95.6 4.7 %project_add.1 = (bf16[512,512]{1,0:T(8,128)(2,1)S(1)}, bf16[512,512]{1,0:T(8,128)(2,1)S(1)}, bf16[256,512]{1,0:T(8,128)(2,1)S(1)}, bf16[256,512]{1,0:T(8,128)(2,1)S(1)}, f32[512,512]{1,0:T(8,128)S(1)}) custom-call(s32[4]{0:T(128)S(1)} %copy-done.19, bf16[512,512]{1,0:T(8,128)(2,1)S(1)} %copy-done.6, bf16[512,4096]{1,0:T(8,128)(2,1)S(1)} %copy-done.1, ...), custom_call_target="tpu_custom_call" | custom-call | flops 1000 | bytes 1000 | tf_op jit(solution)/shard_map/project_add/pallas_call | solution.py:365
  100.4 3.2 %collective-permute-start.12 = (bf16[512,512]{1,0:T(8,128)(2,1)S(1)}, bf16[512,512]{1,0:T(8,128)(2,1)S(1)}, u32[]{:S(2)}, u32[]{:S(2)}) collective-permute-start(bf16[512,512]{1,0:T(8,128)(2,1)S(1)} %get-tuple-element.61), channel_id=1, source_target_pairs={{0,6},{1,7},{2,0},{3,1},{4,2},{5,3},{6,4},{7,5},{8,14},{9,15},{10,... | collective-permute-start | bytes 1572872 | tf_op jit(solution)/shard_map/ppermute | solution.py:501
  104.9 4.0 %d_mix.1 = (bf16[512,512]{1,0:T(8,128)(2,1)S(1)}, f32[512,512]{1,0:T(8,128)S(1)}, bf16[192,512]{1,0:T(8,128)(2,1)S(1)}) custom-call(s32[4]{0:T(128)S(1)} %copy-done.19, bf16[512,4096]{1,0:T(8,128)(2,1)S(1)} %copy-done.2, bf16[4,512,512]{2,1,0:T(8,128)(2,1)S(1)} %pad_maximum_fusion.mine, bf16[4,512,512]{2,1,0:T(8,128)(2,1)} %collective-permute-done.9.theirs, ...), custom_call_target="tpu_custom_call" | custom-call | flops 1000 | bytes 1000 | tf_op jit(solution)/shard_map/d_mix/pallas_call | solution.py:465
  109.9 3.4 %collective-permute-start.10 = (bf16[192,512]{1,0:T(8,128)(2,1)S(1)}, bf16[192,512]{1,0:T(8,128)(2,1)S(1)}, u32[]{:S(2)}, u32[]{:S(2)}) collective-permute-start(bf16[192,512]{1,0:T(8,128)(2,1)S(1)} %get-tuple-element.58), channel_id=1, source_target_pairs={{8,0},{16,8},{24,16},{32,24},{40,32},{48,40},{56,48},{64,56},{72,6... | collective-permute-start | bytes 589832 | tf_op jit(solution)/shard_map/ppermute | solution.py:514
  115.5 3.3 %collective-permute-start.14 = (bf16[256,512]{1,0:T(8,128)(2,1)S(1)}, bf16[256,512]{1,0:T(8,128)(2,1)S(1)}, u32[]{:S(2)}, u32[]{:S(2)}) collective-permute-start(bf16[256,512]{1,0:T(8,128)(2,1)S(1)} %add_convert_fusion.2.refs_1_), channel_id=1, source_target_pairs={{0,6},{1,7},{2,0},{3,1},{4,2},{5,3},{6,4},{7,5},{8,14},{9,15},{10,... | collective-permute-start | bytes 786440 | tf_op jit(solution)/shard_map/ppermute | solution.py:501
  118.8 7.6 %collective-permute-done.10.msg_ref = bf16[192,512]{1,0:T(8,128)(2,1)S(1)} collective-permute-done((bf16[192,512]{1,0:T(8,128)(2,1)S(1)}, bf16[192,512]{1,0:T(8,128)(2,1)S(1)}, u32[]{:S(2)}, u32[]{:S(2)}) %collective-permute-start.10) | collective-permute-done | bytes 196640 | tf_op jit(solution)/shard_map/ppermute | solution.py:514
  127.1 9.3 %backward.1 = bf16[3,512,512]{2,1,0:T(8,128)(2,1)} custom-call(s32[4]{0:T(128)} %pad_add_fusion.info_ref.valid_ref.order_ref, bf16[512,512]{1,0:T(8,128)(2,1)} %copy-done.14, bf16[192,512]{1,0:T(8,128)(2,1)} %copy-done.25, f32[512,512]{1,0:T(8,128)} %copy-done.11, f32[512,512]{1,0:T(8,128)} %get-tuple-element.53.k_ref, f32[512,512]{1,0:T(8,128)} %get-tuple-element.54.v_ref, ...), custom_call_target="tpu_custom_call" | custom-call | flops 1000 | bytes 1000 | tf_op jit(solution)/shard_map/backward/pallas_call | solution.py:283
  (80 shorter events, 24.1 us)
Async XLA Ops:
  4.2 18.3 %all-to-all-start = ((bf16[4,512,128]{2,1,0:T(8,128)(2,1)}), bf16[4,512,128]{2,1,0:T(8,128)(2,1)S(1)}, u32[]{:S(2)}, u32[]{:S(2)}) async-start(bf16[4,512,128]{2,1,0:T(8,128)(2,1)} %get-tuple-element.35), calls=%async_computation | async-start | bytes 1048576 | tf_op jit(solution)/shard_map/all_to_all | solution.py:485
  9.0 13.5 %collective-permute-start = (bf16[304,512]{1,0:T(8,128)(2,1)}, bf16[304,512]{1,0:T(8,128)(2,1)S(1)}, u32[]{:S(2)}, u32[]{:S(2)}) collective-permute-start(bf16[304,512]{1,0:T(8,128)(2,1)} %get-tuple-element.36.refs_0_), channel_id=1, source_target_pairs={{0,8},{8,16},{16,24},{24,32},{32,40},{40,48},{48,56},{56,64},{64,7... | collective-permute-start | bytes 933896 | tf_op jit(solution)/shard_map/ppermute | solution.py:514
  24.2 43.3 %all-to-all-start.1 = ((bf16[4,4,512,128]{3,2,1,0:T(8,128)(2,1)}), bf16[4,4,512,128]{3,2,1,0:T(8,128)(2,1)S(1)}, u32[]{:S(2)}, u32[]{:S(2)}) async-start(bf16[4,4,512,128]{3,2,1,0:T(8,128)(2,1)} %broadcast_in_dim.2.refs_3_), calls=%async_computation.1 | async-start | bytes 4194304 | tf_op jit(solution)/shard_map/all_to_all | solution.py:485
  28.7 29.0 %copy-start = (bf16[512,4096]{1,0:T(8,128)(2,1)S(1)}, bf16[512,4096]{1,0:T(8,128)(2,1)}, u32[]{:S(2)}) copy-start(bf16[512,4096]{1,0:T(8,128)(2,1)} %weight_ref.5) | copy-start | bytes 12582916
  28.7 29.0 %copy-start.19 = (s32[4]{0:T(128)S(1)}, s32[4]{0:T(128)}, u32[]{:S(2)}) copy-start(s32[4]{0:T(128)} %pad_add_fusion.info_ref.valid_ref.order_ref) | copy-start | bytes 52
  34.5 23.2 %collective-permute-start.2 = (bf16[512,512]{1,0:T(8,128)(2,1)}, bf16[512,512]{1,0:T(8,128)(2,1)S(1)}, u32[]{:S(2)}, u32[]{:S(2)}) collective-permute-start(bf16[512,512]{1,0:T(8,128)(2,1)} %get-tuple-element.47.refs_0_), channel_id=1, source_target_pairs={{0,8},{8,16},{16,24},{24,0},{32,40},{40,48},{48,56},{56,32},{64,72... | collective-permute-start | bytes 1572872 | tf_op jit(solution)/shard_map/ppermute | solution.py:496
  36.9 28.1 %collective-permute-start.1 = (bf16[512,512]{1,0:T(8,128)(2,1)}, bf16[512,512]{1,0:T(8,128)(2,1)S(1)}, u32[]{:S(2)}, u32[]{:S(2)}) collective-permute-start(bf16[512,512]{1,0:T(8,128)(2,1)} %cot_ref.1), channel_id=1, source_target_pairs={{0,4},{1,5},{2,6},{3,7},{4,0},{5,1},{6,2},{7,3},{8,12},{9,13},{10,... | collective-permute-start | bytes 1572872 | tf_op jit(solution)/shard_map/ppermute | solution.py:501
  40.5 24.6 %collective-permute-start.3 = (bf16[512,512]{1,0:T(8,128)(2,1)}, bf16[512,512]{1,0:T(8,128)(2,1)S(1)}, u32[]{:S(2)}, u32[]{:S(2)}) collective-permute-start(bf16[512,512]{1,0:T(8,128)(2,1)} %get-tuple-element.47.refs_0_), channel_id=1, source_target_pairs={{0,16},{8,24},{16,0},{24,8},{32,48},{40,56},{48,32},{56,40},{64,80... | collective-permute-start | bytes 1572872 | tf_op jit(solution)/shard_map/ppermute | solution.py:496
  40.7 26.0 %collective-permute-start.4 = (bf16[512,512]{1,0:T(8,128)(2,1)}, bf16[512,512]{1,0:T(8,128)(2,1)S(1)}, u32[]{:S(2)}, u32[]{:S(2)}) collective-permute-start(bf16[512,512]{1,0:T(8,128)(2,1)} %get-tuple-element.47.refs_0_), channel_id=1, source_target_pairs={{0,24},{8,0},{16,8},{24,16},{32,56},{40,32},{48,40},{56,48},{64,88... | collective-permute-start | bytes 1572872 | tf_op jit(solution)/shard_map/ppermute | solution.py:496
  58.7 13.0 %copy-start.10 = (bf16[512,512]{1,0:T(8,128)(2,1)S(1)}, bf16[512,512]{1,0:T(8,128)(2,1)}, u32[]{:S(2)}) copy-start(bf16[512,512]{1,0:T(8,128)(2,1)} %get-tuple-element.47.refs_0_) | copy-start | bytes 1572868
  67.6 4.2 %collective-permute-start.5 = (bf16[4,4,512,128]{3,2,1,0:T(8,128)(2,1)S(1)}, bf16[4,4,512,128]{3,2,1,0:T(8,128)(2,1)S(1)}, u32[]{:S(2)}, u32[]{:S(2)}) collective-permute-start(bf16[4,4,512,128]{3,2,1,0:T(8,128)(2,1)S(1)} %all-to-all-done.1.mine), channel_id=1, source_target_pairs={{0,1},{1,0},{2,3},{3,2},{4,5},{5,4},{6,7},{7,6},{8,9},{9,8},{10,11... | collective-permute-start | bytes 6291464 | tf_op jit(solution)/shard_map/ppermute | solution.py:509
  67.6 14.5 %collective-permute-start.8 = (bf16[512,512]{1,0:T(8,128)(2,1)}, bf16[512,512]{1,0:T(8,128)(2,1)S(1)}, u32[]{:S(2)}, u32[]{:S(2)}) collective-permute-start(bf16[512,512]{1,0:T(8,128)(2,1)} %cot_ref.1), channel_id=1, source_target_pairs={{0,6},{1,7},{2,0},{3,1},{4,2},{5,3},{6,4},{7,5},{8,14},{9,15},{10,... | collective-permute-start | bytes 1572872 | tf_op jit(solution)/shard_map/ppermute | solution.py:501
  68.7 15.5 %collective-permute-start.7 = (bf16[512,512]{1,0:T(8,128)(2,1)}, bf16[512,512]{1,0:T(8,128)(2,1)S(1)}, u32[]{:S(2)}, u32[]{:S(2)}) collective-permute-start(bf16[512,512]{1,0:T(8,128)(2,1)} %cot_ref.1), channel_id=1, source_target_pairs={{0,2},{1,3},{2,4},{3,5},{4,6},{5,7},{6,0},{7,1},{8,10},{9,11},{10,... | collective-permute-start | bytes 1572872 | tf_op jit(solution)/shard_map/ppermute | solution.py:501
  69.6 23.8 %collective-permute-start.6 = (bf16[4,512,512]{2,1,0:T(8,128)(2,1)}, bf16[4,512,512]{2,1,0:T(8,128)(2,1)}, u32[]{:S(2)}, u32[]{:S(2)}) collective-permute-start(bf16[4,512,512]{2,1,0:T(8,128)(2,1)} %copy-done.9), channel_id=1, source_target_pairs={{0,1},{1,0},{2,3},{3,2},{4,5},{5,4},{6,7},{7,6},{8,9},{9,8},{10,11... | collective-permute-start | bytes 6291464 | tf_op jit(solution)/shard_map/ppermute | solution.py:509
  85.5 18.1 %collective-permute-start.9 = (bf16[4,512,512]{2,1,0:T(8,128)(2,1)S(1)}, bf16[4,512,512]{2,1,0:T(8,128)(2,1)}, u32[]{:S(2)}, u32[]{:S(2)}) collective-permute-start(bf16[4,512,512]{2,1,0:T(8,128)(2,1)S(1)} %pad_maximum_fusion.mine), channel_id=1, source_target_pairs={{0,1},{1,0},{2,3},{3,2},{4,5},{5,4},{6,7},{7,6},{8,9},{9,8},{10,11... | collective-permute-start | bytes 6291464 | tf_op jit(solution)/shard_map/ppermute | solution.py:509
  85.6 50.8 %all-to-all-start.2 = ((bf16[8,512,128]{2,1,0:T(8,128)(2,1)}), bf16[8,512,128]{2,1,0:T(8,128)(2,1)}, u32[]{:S(2)}, u32[]{:S(2)}) async-start(bf16[8,512,128]{2,1,0:T(8,128)(2,1)} %outer.1.refs_0_), calls=%async_computation.2 | async-start | bytes 2097152 | tf_op jit(solution)/shard_map/all_to_all | solution.py:485
  100.3 14.9 %collective-permute-start.11 = (bf16[512,512]{1,0:T(8,128)(2,1)S(1)}, bf16[512,512]{1,0:T(8,128)(2,1)S(1)}, u32[]{:S(2)}, u32[]{:S(2)}) collective-permute-start(bf16[512,512]{1,0:T(8,128)(2,1)S(1)} %get-tuple-element.56.refs_0_), channel_id=1, source_target_pairs={{0,2},{1,3},{2,4},{3,5},{4,6},{5,7},{6,0},{7,1},{8,10},{9,11},{10,... | collective-permute-start | bytes 1572872 | tf_op jit(solution)/shard_map/ppermute | solution.py:501
  100.4 14.8 %collective-permute-start.12 = (bf16[512,512]{1,0:T(8,128)(2,1)S(1)}, bf16[512,512]{1,0:T(8,128)(2,1)S(1)}, u32[]{:S(2)}, u32[]{:S(2)}) collective-permute-start(bf16[512,512]{1,0:T(8,128)(2,1)S(1)} %get-tuple-element.61), channel_id=1, source_target_pairs={{0,6},{1,7},{2,0},{3,1},{4,2},{5,3},{6,4},{7,5},{8,14},{9,15},{10,... | collective-permute-start | bytes 1572872 | tf_op jit(solution)/shard_map/ppermute | solution.py:501
  109.9 16.6 %copy-start.14 = (bf16[512,512]{1,0:T(8,128)(2,1)}, bf16[512,512]{1,0:T(8,128)(2,1)S(1)}, u32[]{:S(2)}) copy-start(bf16[512,512]{1,0:T(8,128)(2,1)S(1)} %get-tuple-element.57.dconv_ref) | copy-start | bytes 1572868
  109.9 16.6 %collective-permute-start.10 = (bf16[192,512]{1,0:T(8,128)(2,1)S(1)}, bf16[192,512]{1,0:T(8,128)(2,1)S(1)}, u32[]{:S(2)}, u32[]{:S(2)}) collective-permute-start(bf16[192,512]{1,0:T(8,128)(2,1)S(1)} %get-tuple-element.58), channel_id=1, source_target_pairs={{8,0},{16,8},{24,16},{32,24},{40,32},{48,40},{56,48},{64,56},{72,6... | collective-permute-start | bytes 589832 | tf_op jit(solution)/shard_map/ppermute | solution.py:514
  115.3 11.1 %copy-start.20 = (bf16[256,512]{1,0:T(8,128)(2,1)}, bf16[256,512]{1,0:T(8,128)(2,1)S(1)}, u32[]{:S(2)}) copy-start(bf16[256,512]{1,0:T(8,128)(2,1)S(1)} %add_convert_fusion.3.refs_0_) | copy-start | bytes 786436
  115.3 23.2 %collective-permute-start.13 = (bf16[256,512]{1,0:T(8,128)(2,1)S(1)}, bf16[256,512]{1,0:T(8,128)(2,1)S(1)}, u32[]{:S(2)}, u32[]{:S(2)}) collective-permute-start(bf16[256,512]{1,0:T(8,128)(2,1)S(1)} %add_convert_fusion.3.refs_0_), channel_id=1, source_target_pairs={{0,2},{1,3},{2,4},{3,5},{4,6},{5,7},{6,0},{7,1},{8,10},{9,11},{10,... | collective-permute-start | bytes 786440 | tf_op jit(solution)/shard_map/ppermute | solution.py:501
  115.5 23.0 %collective-permute-start.14 = (bf16[256,512]{1,0:T(8,128)(2,1)S(1)}, bf16[256,512]{1,0:T(8,128)(2,1)S(1)}, u32[]{:S(2)}, u32[]{:S(2)}) collective-permute-start(bf16[256,512]{1,0:T(8,128)(2,1)S(1)} %add_convert_fusion.2.refs_1_), channel_id=1, source_target_pairs={{0,6},{1,7},{2,0},{3,1},{4,2},{5,3},{6,4},{7,5},{8,14},{9,15},{10,... | collective-permute-start | bytes 786440 | tf_op jit(solution)/shard_map/ppermute | solution.py:501
  127.1 11.4 %copy-start.13 = (f32[512,512]{1,0:T(8,128)S(1)}, f32[512,512]{1,0:T(8,128)}, u32[]{:S(2)}) copy-start(f32[512,512]{1,0:T(8,128)} %copy-done.12) | copy-start | bytes 3145732
  (20 other events, 83.8 us)

commit v7 on v5

--- a/solution.py
+++ b/solution.py
@@ -443,7 +443,7 @@
             jax.ShapeDtypeStruct((RIM + 2 * TAIL, CH), BF16),
             jax.ShapeDtypeStruct((NX, ROWS, LANES), BF16),
         ],
-        compiler_params=params(),
+        compiler_params=params(56),
         cost_estimate=cost(1000, 1000),
         name="prepare",
     )(info, streams, cotangent)
@@ -459,6 +459,7 @@
             both = jnp.concatenate([mine[y, x], theirs[y, x]], axis=1)
             part = jnp.dot(turned[behind][...], both, preferred_element_type=F32)
             total = part if total is None else total + part
+        total = total * (1.0 / np.sqrt(float(ROWS * NZ * NX)))
         out_ref[2 * y + core] = total[:, :LANES].astype(BF16)
         out_ref[2 * y + 1 - core] = total[:, LANES:].astype(BF16)
 
@@ -564,7 +565,7 @@
     halo = neighbour(tail, 1)
     slab = exchange(quarters, "x")
     own = run_forward(info, streams, short, long_filter, forward_table, causal_table, (tail,))
-    slab, halo, held, *own = lax.optimization_barrier([slab, halo, cotangent, *own])
+    slab, held, *_ = lax.optimization_barrier([slab, cotangent, halo, *own])
     slab_copies = copies(slab)
     mine = exchange(slab_copies, "y").reshape(NY, NX, ROWS, LANES)
     mix_in, turned, q_side, k_side, v_side, conv = run_finish(
@@ -572,35 +573,34 @@
     )
     turned = [turned] + [along_x(turned, ahead) for ahead in (1, 2, 3)]
     far = along_y(held, 2)
-    turned[1], mix_in = lax.optimization_barrier((turned[1], mix_in))
-    given = run_project(info, mix_in, out_weight)
+    given = run_project(info, mix_in, out_weight, (turned[1],))
     taken = other_core(given)
-    mine, far, given, held, *turned = lax.optimization_barrier([mine, far, given, held, *turned])
+    ready, held, *_ = lax.optimization_barrier([mine, held, far, given, *turned])
     below, above = along_y(held, 1), along_y(held, -1)
-    theirs = other_core(mine)
+    theirs = other_core(ready)
     partial = run_outer(info, turned, mine, theirs)
-    below, above, far, partial = lax.optimization_barrier((below, above, far, partial))
-    cots = jnp.stack([cotangent, below, above, far])
-    cots_other = other_core(cots)
     sums = exchange(partial, "z")
     up, down, next_top, last_bottom, own_out = run_project_add(info, mix_in, out_weight, taken, (partial,))
     from_below, from_above = along_y(up, 1), along_y(down, -1)
+    held, _ = lax.optimization_barrier((cotangent, up))
+    cots = jnp.stack([held, below, above, far])
+    cots_other = other_core(cots)
     d_conv, d_q, msg = run_d_mix(
         info, out_weight, cots, cots_other, (q_side, k_side, v_side, conv), (up,)
     )
-    from_below, from_above, msg = lax.optimization_barrier((from_below, from_above, msg))
+    from_below, from_above, _ = lax.optimization_barrier((from_below, from_above, msg))
     next_top, last_bottom = add(next_top, from_below[:HALF]), add(last_bottom, from_above[HALF:])
     top, bottom = along_y(next_top, 1), along_y(last_bottom, -1)
     msg = neighbour(msg, -1)
     sides = (d_q, k_side, v_side, short, long_filter, forward_table, anti_table)
     begun = run_backward(info, d_conv, *sides)
     d_streams = run_backward_end(info, d_conv, msg, *sides, begun, (next_top, last_bottom))
-    sums, d_streams, own_out = lax.optimization_barrier((sums, d_streams, own_out))
+    sums, own_out, _ = lax.optimization_barrier((sums, own_out, d_streams))
     d_qkv = d_streams.transpose(1, 0, 2)
     top = own_out[:HALF] + top.astype(F32) + from_above[:HALF].astype(F32)
     bottom = own_out[HALF:] + bottom.astype(F32) + from_below[HALF:].astype(F32)
     mixed = jnp.concatenate([top, bottom], axis=0).astype(BF16)
-    d_weight = jnp.sum(sums.astype(F32), axis=0) * (1.0 / jnp.sqrt(jnp.float32(ROWS * NZ * NX)))
+    d_weight = jnp.sum(sums.astype(F32), axis=0)
     return mixed, d_qkv, d_weight
 
 

time: 142 us -> 140 us (0.986)
  the two profiles are of different devices: /device:TPU:26 before, /device:TPU:102 now
where the time goes in v7:
time: 140 us; the launch traced here: 138 us
  Pallas kernels  42.1 us (30%)
  starting transfers between devices  41.3 us (30%)
  waiting for transfers between devices  27.7 us (20%)
  local copies, waits for them, and re-layouts  18.2 us (13%)
  other arithmetic  7.23 us (5%)
  between operations  1.59 us (1%)
    all_to_all x3, starting transfers between devices, exchange(): lax.all_to_all(array, 'tp' if axis == 'y' else 'ctx', 0, 0, axis_index_gr...  17.5 us
    unnamed x70, local copies, waits for them, and re-layouts  16.4 us
    ppermute x3, waiting for transfers between devices, along_x(): return lax.ppermute(array, 'ctx', pairs)  16.3 us
    ppermute x7, starting transfers between devices, along_y(): return lax.ppermute(array, 'tp', pairs)  12.2 us
    ppermute x2, waiting for transfers between devices, neighbour(): lax.ppermute(array, 'ctx', [(i, i + by) for i in range(count) if 0 <= i +...  8.93 us
    ppermute x2, starting transfers between devices, neighbour(): lax.ppermute(array, 'ctx', [(i, i + by) for i in range(count) if 0 <= i +...  7.46 us
    pallas_call x1, Pallas kernels, run_forward(): pl.pallas_call(forward_kernel, grid=(CH // LANES,), in_specs=[SMEM, lane_...  6.91 us
    pallas_call x1, Pallas kernels, run_backward(): pl.pallas_call(backward_kernel, grid=(CH // LANES,), in_specs=[SMEM, lane...  6.67 us
  transfers between devices with their start and end apart: 18, of which 5 were waited for; matrix products, arithmetic and copies ran while one was open for 2% of the time, Pallas kernels for 29%

profile of v7, /device:TPU:102, one launch (start us, length us, event | category | flops | bytes accessed | tf_op | source)
XLA Modules:
  0.0 138.2 jit_solution(8082993073996521438)
XLA Ops:
  1.8 2.3 %prepare.1 = (bf16[304,512]{1,0:T(8,128)(2,1)}, bf16[4,512,128]{2,1,0:T(8,128)(2,1)}) custom-call(s32[4]{0:T(128)} %pad_add_fusion.info_ref.valid_ref.order_ref, bf16[3,512,512]{2,1,0:T(8,128)(2,1)} %bitcast.10, bf16[512,512]{1,0:T(8,128)(2,1)} %cot_ref.1), custom_call_target="tpu_custom_call" | custom-call | flops 1000 | bytes 1000 | tf_op jit(solution)/shard_map/prepare/pallas_call | solution.py:437
  4.1 4.8 %all-to-all-start = ((bf16[4,512,128]{2,1,0:T(8,128)(2,1)}), bf16[4,512,128]{2,1,0:T(8,128)(2,1)S(1)}, u32[]{:S(2)}, u32[]{:S(2)}) async-start(bf16[4,512,128]{2,1,0:T(8,128)(2,1)} %get-tuple-element.35), calls=%async_computation | async-start | bytes 1048576 | tf_op jit(solution)/shard_map/all_to_all | solution.py:525
  8.9 4.5 %collective-permute-start = (bf16[304,512]{1,0:T(8,128)(2,1)}, bf16[304,512]{1,0:T(8,128)(2,1)S(1)}, u32[]{:S(2)}, u32[]{:S(2)}) collective-permute-start(bf16[304,512]{1,0:T(8,128)(2,1)} %get-tuple-element.36.refs_0_), channel_id=1, source_target_pairs={{0,8},{8,16},{16,24},{24,32},{32,40},{40,48},{48,56},{56,64},{64,7... | collective-permute-start | bytes 933896 | tf_op jit(solution)/shard_map/ppermute | solution.py:554
  13.4 6.9 %forward.1 = (bf16[512,512]{1,0:T(8,128)(2,1)}, bf16[512,512]{1,0:T(8,128)(2,1)}, f32[512,512]{1,0:T(8,128)}, f32[512,512]{1,0:T(8,128)}, f32[512,512]{1,0:T(8,1...) custom-call(s32[4]{0:T(128)} %pad_add_fusion.info_ref.valid_ref.order_ref, bf16[3,512,512]{2,1,0:T(8,128)(2,1)} %bitcast.11, ...), custom_call_target="tpu_custom_call" | custom-call | flops 1000 | bytes 1000 | tf_op jit(solution)/shard_map/forward/pallas_call | solution.py:262
  20.3 2.1 %collective-permute-done.halo_ref = bf16[304,512]{1,0:T(8,128)(2,1)S(1)} collective-permute-done((bf16[304,512]{1,0:T(8,128)(2,1)}, bf16[304,512]{1,0:T(8,128)(2,1)S(1)}, u32[]{:S(2)}, u32[]{:S(2)}) %collective-permute-start) | collective-permute-done | bytes 311328 | tf_op jit(solution)/shard_map/ppermute | solution.py:554
  24.2 4.5 %all-to-all-start.1 = ((bf16[4,4,512,128]{3,2,1,0:T(8,128)(2,1)}), bf16[4,4,512,128]{3,2,1,0:T(8,128)(2,1)S(1)}, u32[]{:S(2)}, u32[]{:S(2)}) async-start(bf16[4,4,512,128]{3,2,1,0:T(8,128)(2,1)} %broadcast_in_dim.2.refs_3_), calls=%async_computation.1 | async-start | bytes 4194304 | tf_op jit(solution)/shard_map/all_to_all | solution.py:525
  28.6 5.8 %finish.1 = (bf16[512,512]{1,0:T(8,128)(2,1)}, bf16[512,512]{1,0:T(8,128)(2,1)}, f32[512,512]{1,0:T(8,128)}, f32[512,512]{1,0:T(8,128)}, f32[512,512]{1,0:T(8,128)}, /*index=5*/f32[512,512]{1,0:T(8,128)}) custom-call(s32[4]{0:T(128)} %pad_add_fusion.info_ref.valid_ref.order_ref, ...), custom_call_target="tpu_custom_call", output_to_operand_aliasing={{2}: (7, {}), {3}: (8, {}), {4}: (9, {}), {0}: (11, {}), {1... | custom-call | flops 1000 | bytes 1000 | tf_op jit(solution)/shard_map/finish/pallas_call | solution.py:282
  34.4 2.5 %collective-permute-start.2 = (bf16[512,512]{1,0:T(8,128)(2,1)}, bf16[512,512]{1,0:T(8,128)(2,1)S(1)}, u32[]{:S(2)}, u32[]{:S(2)}) collective-permute-start(bf16[512,512]{1,0:T(8,128)(2,1)} %get-tuple-element.47.refs_0_), channel_id=1, source_target_pairs={{0,8},{8,16},{16,24},{24,0},{32,40},{40,48},{48,56},{56,32},{64,72... | collective-permute-start | bytes 1572872 | tf_op jit(solution)/shard_map/ppermute | solution.py:536
  37.9 3.5 %collective-permute-start.1 = (bf16[512,512]{1,0:T(8,128)(2,1)}, bf16[512,512]{1,0:T(8,128)(2,1)}, u32[]{:S(2)}, u32[]{:S(2)}) collective-permute-start(bf16[512,512]{1,0:T(8,128)(2,1)} %cot_ref.1), channel_id=1, source_target_pairs={{0,4},{1,5},{2,6},{3,7},{4,0},{5,1},{6,2},{7,3},{8,12},{9,13},{10,... | collective-permute-start | bytes 1572872 | tf_op jit(solution)/shard_map/ppermute | solution.py:541
  41.4 16.3 %collective-permute-done.2.refs_0_.refs_1_ = bf16[512,512]{1,0:T(8,128)(2,1)S(1)} collective-permute-done((bf16[512,512]{1,0:T(8,128)(2,1)}, bf16[512,512]{1,0:T(8,128)(2,1)S(1)}, u32[]{:S(2)}, u32[]{:S(2)}) %collective-permute-start.2) | collective-permute-done | bytes 524320 | tf_op jit(solution)/shard_map/ppermute | solution.py:536
  58.7 2.6 %project.1 = bf16[4,512,512]{2,1,0:T(8,128)(2,1)S(1)} custom-call(s32[4]{0:T(128)S(1)} %copy-done.25, bf16[512,512]{1,0:T(8,128)(2,1)S(1)} %copy-done.5, bf16[512,4096]{1,0:T(8,128)(2,1)S(1)} %copy-done, bf16[512,512]{1,0:T(8,128)(2,1)S(1)} %collective-permute-done.2.refs_0_.refs_1_), custom_call_target="tpu_custom_call" | custom-call | flops 1000 | bytes 1000 | tf_op jit(solution)/shard_map/project/pallas_call | solution.py:358
  68.9 2.4 %collective-permute-done.5.theirs = bf16[4,4,512,128]{3,2,1,0:T(8,128)(2,1)S(1)} collective-permute-done((bf16[4,4,512,128]{3,2,1,0:T(8,128)(2,1)S(1)}, bf16[4,4,512,128]{3,2,1,0:T(8,128)(2,1)S(1)}, u32[]{:S(2)}, u32[]{:S(2)}) %collective-permute-start.5) | collective-permute-done | bytes 2097184 | tf_op jit(solution)/shard_map/ppermute | solution.py:549
  74.4 3.9 %outer.1.refs_0_ = bf16[8,512,128]{2,1,0:T(8,128)(2,1)} custom-call(s32[4]{0:T(128)S(1)} %copy-done.25, bf16[4,4,512,128]{3,2,1,0:T(8,128)(2,1)S(1)} %all-to-all-done.1.mine, bf16[4,4,512,128]{3,2,1,0:T(8,128)(2,1)S(1)} %collective-permute-done.5.theirs, bf16[512,512]{1,0:T(8,128)(2,1)S(1)} %copy-done.12, bf16[512,512]{1,0:T(8,128)(2,1)S(1)} %copy-done.14, ...), custom_call_target="tpu_custom_call" | custom-call | flops 1000 | bytes 1000 | tf_op jit(solution)/shard_map/outer/pallas_call | solution.py:468
  78.4 2.8 %project_add.1 = (bf16[512,512]{1,0:T(8,128)(2,1)S(1)}, bf16[512,512]{1,0:T(8,128)(2,1)S(1)}, bf16[256,512]{1,0:T(8,128)(2,1)S(1)}, bf16[256,512]{1,0:T(8,128)(2,1)S(1)}, f32[512,512]{1,0:T(8,128)S(1)}) custom-call(s32[4]{0:T(128)S(1)} %copy-done.25, bf16[512,512]{1,0:T(8,128)(2,1)S(1)} %copy-done.6, bf16[512,4096]{1,0:T(8,128)(2,1)S(1)} %copy-done.1, ...), custom_call_target="tpu_custom_call" | custom-call | flops 1000 | bytes 1000 | tf_op jit(solution)/shard_map/project_add/pallas_call | solution.py:405
  82.7 3.4 %pad_maximum_fusion.mine = bf16[4,512,512]{2,1,0:T(8,128)(2,1)} fusion(bf16[1,512,512]{2,1,0:T(8,128)(2,1)} %bitcast.8, bf16[1,512,512]{2,1,0:T(8,128)(2,1)S(1)} %bitcast.19, bf16[1,512,512]{2,1,0:T(8,128)(2,1)S(1)} %bitcast.18, bf16[1,512,512]{2,1,0:T(8,128)(2,1)} %bitcast.5), kind=kLoop, calls=%fused_computation | loop fusion | flops 3145728 | bytes 4194304 | tf_op jit(solution)/shard_map/stack | solution.py:586
  86.4 8.3 %all-to-all-start.2 = ((bf16[8,512,128]{2,1,0:T(8,128)(2,1)}), bf16[8,512,128]{2,1,0:T(8,128)(2,1)}, u32[]{:S(2)}, u32[]{:S(2)}) async-start(bf16[8,512,128]{2,1,0:T(8,128)(2,1)} %outer.1.refs_0_), calls=%async_computation.2 | async-start | bytes 2097152 | tf_op jit(solution)/shard_map/all_to_all | solution.py:525
  97.9 2.2 %copy-done.2 = bf16[512,4096]{1,0:T(8,128)(2,1)S(1)} copy-done((bf16[512,4096]{1,0:T(8,128)(2,1)S(1)}, bf16[512,4096]{1,0:T(8,128)(2,1)}, u32[]{:S(2)}) %copy-start.2) | copy-done | bytes 4194328
  102.4 4.7 %d_mix.1 = (bf16[512,512]{1,0:T(8,128)(2,1)S(1)}, f32[512,512]{1,0:T(8,128)S(1)}, bf16[192,512]{1,0:T(8,128)(2,1)S(1)}) custom-call(s32[4]{0:T(128)S(1)} %copy-done.25, bf16[512,4096]{1,0:T(8,128)(2,1)S(1)} %copy-done.2, bf16[4,512,512]{2,1,0:T(8,128)(2,1)} %pad_maximum_fusion.mine, bf16[4,512,512]{2,1,0:T(8,128)(2,1)} %collective-permute-done.9.theirs, ...), custom_call_target="tpu_custom_call" | custom-call | flops 1000 | bytes 1000 | tf_op jit(solution)/shard_map/d_mix/pallas_call | solution.py:505
  108.9 3.0 %collective-permute-start.10 = (bf16[192,512]{1,0:T(8,128)(2,1)S(1)}, bf16[192,512]{1,0:T(8,128)(2,1)S(1)}, u32[]{:S(2)}, u32[]{:S(2)}) collective-permute-start(bf16[192,512]{1,0:T(8,128)(2,1)S(1)} %get-tuple-element.58), channel_id=1, source_target_pairs={{8,0},{16,8},{24,16},{32,24},{40,32},{48,40},{56,48},{64,56},{72,6... | collective-permute-start | bytes 589832 | tf_op jit(solution)/shard_map/ppermute | solution.py:554
  112.0 1.8 %collective-permute-start.14 = (bf16[256,512]{1,0:T(8,128)(2,1)S(1)}, bf16[256,512]{1,0:T(8,128)(2,1)S(1)}, u32[]{:S(2)}, u32[]{:S(2)}) collective-permute-start(bf16[256,512]{1,0:T(8,128)(2,1)S(1)} %add_convert_fusion.2.refs_2_), channel_id=1, source_target_pairs={{0,6},{1,7},{2,0},{3,1},{4,2},{5,3},{6,4},{7,5},{8,14},{9,15},{10,... | collective-permute-start | bytes 786440 | tf_op jit(solution)/shard_map/ppermute | solution.py:541
  114.3 6.7 %backward.1.refs_0_ = bf16[3,512,512]{2,1,0:T(8,128)(2,1)} custom-call(s32[4]{0:T(128)} %pad_add_fusion.info_ref.valid_ref.order_ref, bf16[512,512]{1,0:T(8,128)(2,1)} %copy-done.10, f32[512,512]{1,0:T(8,128)} %copy-done.9, f32[512,512]{1,0:T(8,128)} %get-tuple-element.54.k_ref, f32[512,512]{1,0:T(8,128)} %get-tuple-element.55.v_ref, f32[3,7,512]{2,1,0:T(8,128)} %bitcast.16, ...), custom_call_target="tpu_custom_call" | custom-call | flops 1000 | bytes 1000 | tf_op jit(solution)/shard_map/backward/pallas_call | solution.py:303
  121.0 6.8 %collective-permute-done.10.msg_ref = bf16[192,512]{1,0:T(8,128)(2,1)S(1)} collective-permute-done((bf16[192,512]{1,0:T(8,128)(2,1)S(1)}, bf16[192,512]{1,0:T(8,128)(2,1)S(1)}, u32[]{:S(2)}, u32[]{:S(2)}) %collective-permute-start.10) | collective-permute-done | bytes 196640 | tf_op jit(solution)/shard_map/ppermute | solution.py:554
  128.5 6.5 %backward_end.1 = bf16[3,512,512]{2,1,0:T(8,128)(2,1)} custom-call(s32[4]{0:T(128)} %pad_add_fusion.info_ref.valid_ref.order_ref, bf16[512,512]{1,0:T(8,128)(2,1)} %copy-done.10, bf16[192,512]{1,0:T(8,128)(2,1)} %copy-done.34, f32[512,512]{1,0:T(8,128)} %copy-done.9, f32[512,512]{1,0:T(8,128)} %get-tuple-element.54.k_ref, ...), custom_call_target="tpu_custom_call", output_to_operand_aliasing={{}: (10, {})} | custom-call | flops 1000 | bytes 1000 | tf_op jit(solution)/shard_map/backward_end/pallas_call | solution.py:322
  135.0 2.1 %convert_reduce_fusion = f32[512,128]{1,0:T(8,128)} fusion(bf16[8,512,128]{2,1,0:T(8,128)(2,1)} %all-to-all-done.2), kind=kLoop, calls=%fused_computation.1 | loop fusion | flops 983040 | bytes 1310720 | tf_op jit(solution)/shard_map/reduce_sum | solution.py:603
  (99 shorter events, 26.4 us)
Async XLA Ops:
  4.1 18.3 %all-to-all-start = ((bf16[4,512,128]{2,1,0:T(8,128)(2,1)}), bf16[4,512,128]{2,1,0:T(8,128)(2,1)S(1)}, u32[]{:S(2)}, u32[]{:S(2)}) async-start(bf16[4,512,128]{2,1,0:T(8,128)(2,1)} %get-tuple-element.35), calls=%async_computation | async-start | bytes 1048576 | tf_op jit(solution)/shard_map/all_to_all | solution.py:525
  8.9 13.5 %collective-permute-start = (bf16[304,512]{1,0:T(8,128)(2,1)}, bf16[304,512]{1,0:T(8,128)(2,1)S(1)}, u32[]{:S(2)}, u32[]{:S(2)}) collective-permute-start(bf16[304,512]{1,0:T(8,128)(2,1)} %get-tuple-element.36.refs_0_), channel_id=1, source_target_pairs={{0,8},{8,16},{16,24},{24,32},{32,40},{40,48},{48,56},{56,64},{64,7... | collective-permute-start | bytes 933896 | tf_op jit(solution)/shard_map/ppermute | solution.py:554
  24.2 40.9 %all-to-all-start.1 = ((bf16[4,4,512,128]{3,2,1,0:T(8,128)(2,1)}), bf16[4,4,512,128]{3,2,1,0:T(8,128)(2,1)S(1)}, u32[]{:S(2)}, u32[]{:S(2)}) async-start(bf16[4,4,512,128]{3,2,1,0:T(8,128)(2,1)} %broadcast_in_dim.2.refs_3_), calls=%async_computation.1 | async-start | bytes 4194304 | tf_op jit(solution)/shard_map/all_to_all | solution.py:525
  28.6 29.0 %copy-start = (bf16[512,4096]{1,0:T(8,128)(2,1)S(1)}, bf16[512,4096]{1,0:T(8,128)(2,1)}, u32[]{:S(2)}) copy-start(bf16[512,4096]{1,0:T(8,128)(2,1)} %weight_ref.5) | copy-start | bytes 12582916
  28.6 29.0 %copy-start.25 = (s32[4]{0:T(128)S(1)}, s32[4]{0:T(128)}, u32[]{:S(2)}) copy-start(s32[4]{0:T(128)} %pad_add_fusion.info_ref.valid_ref.order_ref) | copy-start | bytes 52
  34.4 23.2 %collective-permute-start.2 = (bf16[512,512]{1,0:T(8,128)(2,1)}, bf16[512,512]{1,0:T(8,128)(2,1)S(1)}, u32[]{:S(2)}, u32[]{:S(2)}) collective-permute-start(bf16[512,512]{1,0:T(8,128)(2,1)} %get-tuple-element.47.refs_0_), channel_id=1, source_target_pairs={{0,8},{8,16},{16,24},{24,0},{32,40},{40,48},{48,56},{56,32},{64,72... | collective-permute-start | bytes 1572872 | tf_op jit(solution)/shard_map/ppermute | solution.py:536
  36.9 26.5 %collective-permute-start.3 = (bf16[512,512]{1,0:T(8,128)(2,1)}, bf16[512,512]{1,0:T(8,128)(2,1)S(1)}, u32[]{:S(2)}, u32[]{:S(2)}) collective-permute-start(bf16[512,512]{1,0:T(8,128)(2,1)} %get-tuple-element.47.refs_0_), channel_id=1, source_target_pairs={{0,16},{8,24},{16,0},{24,8},{32,48},{40,56},{48,32},{56,40},{64,80... | collective-permute-start | bytes 1572872 | tf_op jit(solution)/shard_map/ppermute | solution.py:536
  37.1 27.1 %collective-permute-start.4 = (bf16[512,512]{1,0:T(8,128)(2,1)}, bf16[512,512]{1,0:T(8,128)(2,1)S(1)}, u32[]{:S(2)}, u32[]{:S(2)}) collective-permute-start(bf16[512,512]{1,0:T(8,128)(2,1)} %get-tuple-element.47.refs_0_), channel_id=1, source_target_pairs={{0,24},{8,0},{16,8},{24,16},{32,56},{40,32},{48,40},{56,48},{64,88... | collective-permute-start | bytes 1572872 | tf_op jit(solution)/shard_map/ppermute | solution.py:536
  37.9 27.2 %collective-permute-start.1 = (bf16[512,512]{1,0:T(8,128)(2,1)}, bf16[512,512]{1,0:T(8,128)(2,1)}, u32[]{:S(2)}, u32[]{:S(2)}) collective-permute-start(bf16[512,512]{1,0:T(8,128)(2,1)} %cot_ref.1), channel_id=1, source_target_pairs={{0,4},{1,5},{2,6},{3,7},{4,0},{5,1},{6,2},{7,3},{8,12},{9,13},{10,... | collective-permute-start | bytes 1572872 | tf_op jit(solution)/shard_map/ppermute | solution.py:541
  65.1 6.2 %collective-permute-start.5 = (bf16[4,4,512,128]{3,2,1,0:T(8,128)(2,1)S(1)}, bf16[4,4,512,128]{3,2,1,0:T(8,128)(2,1)S(1)}, u32[]{:S(2)}, u32[]{:S(2)}) collective-permute-start(bf16[4,4,512,128]{3,2,1,0:T(8,128)(2,1)S(1)} %all-to-all-done.1.mine), channel_id=1, source_target_pairs={{0,1},{1,0},{2,3},{3,2},{4,5},{5,4},{6,7},{7,6},{8,9},{9,8},{10,11... | collective-permute-start | bytes 6291464 | tf_op jit(solution)/shard_map/ppermute | solution.py:549
  65.2 13.2 %collective-permute-start.6 = (bf16[4,512,512]{2,1,0:T(8,128)(2,1)}, bf16[4,512,512]{2,1,0:T(8,128)(2,1)S(1)}, u32[]{:S(2)}, u32[]{:S(2)}) collective-permute-start(bf16[4,512,512]{2,1,0:T(8,128)(2,1)} %copy-done.11), channel_id=1, source_target_pairs={{0,1},{1,0},{2,3},{3,2},{4,5},{5,4},{6,7},{7,6},{8,9},{9,8},{10,11... | collective-permute-start | bytes 6291464 | tf_op jit(solution)/shard_map/ppermute | solution.py:549
  65.7 17.1 %collective-permute-start.7 = (bf16[512,512]{1,0:T(8,128)(2,1)}, bf16[512,512]{1,0:T(8,128)(2,1)S(1)}, u32[]{:S(2)}, u32[]{:S(2)}) collective-permute-start(bf16[512,512]{1,0:T(8,128)(2,1)} %cot_ref.1), channel_id=1, source_target_pairs={{0,2},{1,3},{2,4},{3,5},{4,6},{5,7},{6,0},{7,1},{8,10},{9,11},{10,... | collective-permute-start | bytes 1572872 | tf_op jit(solution)/shard_map/ppermute | solution.py:541
  67.4 15.3 %collective-permute-start.8 = (bf16[512,512]{1,0:T(8,128)(2,1)}, bf16[512,512]{1,0:T(8,128)(2,1)S(1)}, u32[]{:S(2)}, u32[]{:S(2)}) collective-permute-start(bf16[512,512]{1,0:T(8,128)(2,1)} %cot_ref.1), channel_id=1, source_target_pairs={{0,6},{1,7},{2,0},{3,1},{4,2},{5,3},{6,4},{7,5},{8,14},{9,15},{10,... | collective-permute-start | bytes 1572872 | tf_op jit(solution)/shard_map/ppermute | solution.py:541
  82.7 15.2 %copy-start.7 = (f32[512,512]{1,0:T(8,128)S(1)}, f32[512,512]{1,0:T(8,128)}, u32[]{:S(2)}) copy-start(f32[512,512]{1,0:T(8,128)} %get-tuple-element.53.q_ref) | copy-start | bytes 3145732
  86.2 11.7 %collective-permute-start.9 = (bf16[4,512,512]{2,1,0:T(8,128)(2,1)}, bf16[4,512,512]{2,1,0:T(8,128)(2,1)}, u32[]{:S(2)}, u32[]{:S(2)}) collective-permute-start(bf16[4,512,512]{2,1,0:T(8,128)(2,1)} %pad_maximum_fusion.mine), channel_id=1, source_target_pairs={{0,1},{1,0},{2,3},{3,2},{4,5},{5,4},{6,7},{7,6},{8,9},{9,8},{10,11... | collective-permute-start | bytes 6291464 | tf_op jit(solution)/shard_map/ppermute | solution.py:549
  86.4 48.6 %all-to-all-start.2 = ((bf16[8,512,128]{2,1,0:T(8,128)(2,1)}), bf16[8,512,128]{2,1,0:T(8,128)(2,1)}, u32[]{:S(2)}, u32[]{:S(2)}) async-start(bf16[8,512,128]{2,1,0:T(8,128)(2,1)} %outer.1.refs_0_), calls=%async_computation.2 | async-start | bytes 2097152 | tf_op jit(solution)/shard_map/all_to_all | solution.py:525
  94.6 17.2 %collective-permute-start.11 = (bf16[512,512]{1,0:T(8,128)(2,1)}, bf16[512,512]{1,0:T(8,128)(2,1)S(1)}, u32[]{:S(2)}, u32[]{:S(2)}) collective-permute-start(bf16[512,512]{1,0:T(8,128)(2,1)} %copy-done.17), channel_id=1, source_target_pairs={{0,2},{1,3},{2,4},{3,5},{4,6},{5,7},{6,0},{7,1},{8,10},{9,11},{10,... | collective-permute-start | bytes 1572872 | tf_op jit(solution)/shard_map/ppermute | solution.py:541
  96.4 15.5 %collective-permute-start.12 = (bf16[512,512]{1,0:T(8,128)(2,1)}, bf16[512,512]{1,0:T(8,128)(2,1)S(1)}, u32[]{:S(2)}, u32[]{:S(2)}) collective-permute-start(bf16[512,512]{1,0:T(8,128)(2,1)} %copy-done.26), channel_id=1, source_target_pairs={{0,6},{1,7},{2,0},{3,1},{4,2},{5,3},{6,4},{7,5},{8,14},{9,15},{10,... | collective-permute-start | bytes 1572872 | tf_op jit(solution)/shard_map/ppermute | solution.py:541
  108.9 19.0 %collective-permute-start.10 = (bf16[192,512]{1,0:T(8,128)(2,1)S(1)}, bf16[192,512]{1,0:T(8,128)(2,1)S(1)}, u32[]{:S(2)}, u32[]{:S(2)}) collective-permute-start(bf16[192,512]{1,0:T(8,128)(2,1)S(1)} %get-tuple-element.58), channel_id=1, source_target_pairs={{8,0},{16,8},{24,16},{32,24},{40,32},{48,40},{56,48},{64,56},{72,6... | collective-permute-start | bytes 589832 | tf_op jit(solution)/shard_map/ppermute | solution.py:554
  112.0 25.1 %collective-permute-start.14 = (bf16[256,512]{1,0:T(8,128)(2,1)S(1)}, bf16[256,512]{1,0:T(8,128)(2,1)S(1)}, u32[]{:S(2)}, u32[]{:S(2)}) collective-permute-start(bf16[256,512]{1,0:T(8,128)(2,1)S(1)} %add_convert_fusion.2.refs_2_), channel_id=1, source_target_pairs={{0,6},{1,7},{2,0},{3,1},{4,2},{5,3},{6,4},{7,5},{8,14},{9,15},{10,... | collective-permute-start | bytes 786440 | tf_op jit(solution)/shard_map/ppermute | solution.py:541
  113.9 23.2 %collective-permute-start.13 = (bf16[256,512]{1,0:T(8,128)(2,1)S(1)}, bf16[256,512]{1,0:T(8,128)(2,1)S(1)}, u32[]{:S(2)}, u32[]{:S(2)}) collective-permute-start(bf16[256,512]{1,0:T(8,128)(2,1)S(1)} %add_convert_fusion.3.refs_1_), channel_id=1, source_target_pairs={{0,2},{1,3},{2,4},{3,5},{4,6},{5,7},{6,0},{7,1},{8,10},{9,11},{10,... | collective-permute-start | bytes 786440 | tf_op jit(solution)/shard_map/ppermute | solution.py:541
  121.0 16.1 %copy-start.16 = (f32[512,512]{1,0:T(8,128)S(1)}, f32[512,512]{1,0:T(8,128)}, u32[]{:S(2)}) copy-start(f32[512,512]{1,0:T(8,128)} %copy-done.15) | copy-start | bytes 3145732
  121.0 16.1 %copy-start.30 = (bf16[512,512]{1,0:T(8,128)(2,1)S(1)}, bf16[512,512]{1,0:T(8,128)(2,1)}, u32[]{:S(2)}) copy-start(bf16[512,512]{1,0:T(8,128)(2,1)} %copy-done.29) | copy-start | bytes 1572868
  121.0 16.1 %copy-start.32 = (bf16[512,512]{1,0:T(8,128)(2,1)S(1)}, bf16[512,512]{1,0:T(8,128)(2,1)}, u32[]{:S(2)}) copy-start(bf16[512,512]{1,0:T(8,128)(2,1)} %copy-done.31) | copy-start | bytes 1572868
  (29 other events, 119.3 us)

commit v8 on v7

--- a/solution.py
+++ b/solution.py
@@ -103,8 +103,8 @@
     for start in range(0, ROWS, STEP):
         k_side = filtered(short_ref, ext_ref, 1, RIM + start, STEP)
         v_side = filtered(short_ref, ext_ref, 2, RIM + start, STEP)
-        k_ref[start : start + STEP] = k_side
-        v_ref[start : start + STEP] = v_side
+        k_ref[start : start + STEP] = k_side.astype(BF16)
+        v_ref[start : start + STEP] = v_side.astype(BF16)
         q_ref[start : start + STEP] = filtered(short_ref, ext_ref, 0, RIM + start, STEP)
         gate_ref[start : start + STEP] = (k_side * v_side).astype(BF16)
     fwd = fwd_ref[...]
@@ -116,7 +116,7 @@
         now = spectrum(fwd, gate_ref[start : start + LONG])
         conv = convolve(before, now, sign, inv, *taps)
         before = now
-        conv_ref[start : start + LONG] = conv
+        conv_ref[start : start + LONG] = conv.astype(BF16)
         mix_in = live_rows(valid, start, LONG) * q_ref[start : start + LONG] * conv
         mix_ref[start : start + LONG] = mix_in.astype(BF16)
         turned_ref[:, start : start + LONG] = mix_in.T.astype(BF16)
@@ -141,8 +141,8 @@
     k_rim = filtered(short_ref, ext_ref, 1, TAIL, RIM)
     v_rim = filtered(short_ref, ext_ref, 2, TAIL, RIM)
     q_ref[...] = q_rim
-    k_ref[...] = k_rim
-    v_ref[...] = v_rim
+    k_ref[...] = k_rim.astype(BF16)
+    v_ref[...] = v_rim.astype(BF16)
     gate_ref[LONG : LONG + RIM] = (k_rim * v_rim).astype(BF16)
     gate_ref[LONG + RIM : 3 * LONG] = gate_in[RIM:]
     fwd = fwd_ref[...]
@@ -154,7 +154,7 @@
         now = spectrum(fwd, gate_ref[LONG + start : 2 * LONG + start])
         conv = convolve(before, now, sign, inv, *taps)
         before = now
-        conv_ref[start : start + LONG] = conv
+        conv_ref[start : start + LONG] = conv.astype(BF16)
         q_side = q_in[start : start + LONG]
         if start == 0:
             q_side = jnp.concatenate([q_rim, q_side[RIM:]], axis=0)
@@ -190,15 +190,15 @@
     inv = inv_ref[...]
     taps = filter_spectrum(fwd, long_ref[...])
     sign = signs(2 * LONG)
-    ext_ref[0, 0 : HALF + RIM] = dq_ref[0 : HALF + RIM]
+    ext_ref[0, 0 : HALF + RIM] = dq_ref[0 : HALF + RIM].astype(F32)
     now = spectrum(fwd, dconv_ref[0:LONG])
     for start in range(0, HALF + LONG, LONG):
         after = spectrum(fwd, dconv_ref[start + LONG : start + 2 * LONG])
         gated = correlate(now, after, sign, inv, *taps)
         now = after
         rows = LONG if start < HALF else RIM
-        ext_ref[1, start : start + rows] = gated[:rows] * v_ref[start : start + rows]
-        ext_ref[2, start : start + rows] = gated[:rows] * k_ref[start : start + rows]
+        ext_ref[1, start : start + rows] = gated[:rows] * v_ref[start : start + rows].astype(F32)
+        ext_ref[2, start : start + rows] = gated[:rows] * k_ref[start : start + rows].astype(F32)
     filter_back(valid_ref[0], 0, short_ref, ext_ref, out_ref)
 
 
@@ -213,7 +213,7 @@
     gate_ref[0:HALF] = dconv_ref[...]
     gate_ref[HALF : HALF + TAIL] = msg_ref[0:TAIL]
     gate_ref[HALF + TAIL : HALF + 2 * LONG] = jnp.zeros((2 * LONG - TAIL, LANES), BF16)
-    ext_ref[0, 0:HALF] = dq_ref[...]
+    ext_ref[0, 0:HALF] = dq_ref[...].astype(F32)
     ext_ref[0, HALF : HALF + RIM] = msg_ref[TAIL : TAIL + RIM].astype(F32)
     now = spectrum(fwd, gate_ref[0:LONG])
     for start in range(0, HALF + LONG, LONG):
@@ -221,8 +221,8 @@
         gated = correlate(now, after, sign, inv, *taps)
         now = after
         if start < HALF:
-            ext_ref[1, start : start + LONG] = gated * v_ref[start : start + LONG]
-            ext_ref[2, start : start + LONG] = gated * k_ref[start : start + LONG]
+            ext_ref[1, start : start + LONG] = gated * v_ref[start : start + LONG].astype(F32)
+            ext_ref[2, start : start + LONG] = gated * k_ref[start : start + LONG].astype(F32)
         else:
             v_rim = msg_ref[TAIL + RIM : TAIL + 2 * RIM].astype(F32)
             k_rim = msg_ref[TAIL + 2 * RIM : TAIL + 3 * RIM].astype(F32)
@@ -255,7 +255,7 @@
 def forward_shapes():
     side = jax.ShapeDtypeStruct((ROWS, CH), F32)
     square = jax.ShapeDtypeStruct((ROWS, CH), BF16)
-    return [square, square, side, side, side, side]
+    return [square, square, side, square, square, square]
 
 
 def run_forward(info, streams, short, long_taps, fwd, inv, after=()):
@@ -492,13 +492,13 @@
     row = lax.broadcasted_iota(jnp.int32, (ROWS, CH), 0)
     d_mix = jnp.where(row < info_ref[0], total, 0.0)
     d_conv = (d_mix * q_ref[...]).astype(BF16)
-    d_q = d_mix * conv_ref[...]
+    d_q = (d_mix * conv_ref[...].astype(F32)).astype(BF16)
     dconv_ref[...] = d_conv
     dq_ref[...] = d_q
     msg_ref[0:TAIL] = d_conv[:TAIL]
-    msg_ref[TAIL : TAIL + RIM] = d_q[:RIM].astype(BF16)
-    msg_ref[TAIL + RIM : TAIL + 2 * RIM] = v_ref[0:RIM].astype(BF16)
-    msg_ref[TAIL + 2 * RIM : TAIL + 3 * RIM] = k_ref[0:RIM].astype(BF16)
+    msg_ref[TAIL : TAIL + RIM] = d_q[:RIM]
+    msg_ref[TAIL + RIM : TAIL + 2 * RIM] = v_ref[...]
+    msg_ref[TAIL + 2 * RIM : TAIL + 3 * RIM] = k_ref[...]
 
 
 def run_d_mix(info, weight, mine, theirs, sides, after=()):
@@ -507,7 +507,7 @@
         in_specs=[SMEM] + [VMEM] * 7 + [ANY] * len(after),
         out_specs=[VMEM] * 3,
         out_shape=[
-            jax.ShapeDtypeStruct((ROWS, CH), BF16), jax.ShapeDtypeStruct((ROWS, CH), F32),
+            jax.ShapeDtypeStruct((ROWS, CH), BF16), jax.ShapeDtypeStruct((ROWS, CH), BF16),
             jax.ShapeDtypeStruct((TAIL + 3 * RIM, CH), BF16),
         ],
         compiler_params=params(),
@@ -586,7 +586,7 @@
     cots = jnp.stack([held, below, above, far])
     cots_other = other_core(cots)
     d_conv, d_q, msg = run_d_mix(
-        info, out_weight, cots, cots_other, (q_side, k_side, v_side, conv), (up,)
+        info, out_weight, cots, cots_other, (q_side, k_side[:RIM], v_side[:RIM], conv), (up,)
     )
     from_below, from_above, _ = lax.optimization_barrier((from_below, from_above, msg))
     next_top, last_bottom = add(next_top, from_below[:HALF]), add(last_bottom, from_above[HALF:])

time: 140 us -> 138 us (0.986)
    slice x0 -> x2, local copies, waits for them, and re-layouts: none -> 1.44 us  [the longest x1 0.72 us: local(): k_side[:RIM]]
    unnamed x70 -> x66, local copies, waits for them, and re-layouts: 16.4 us -> 16.2 us
  transfers between devices with their start and end apart: 18 -> 18, of which waited for: 5 -> 5; matrix products, arithmetic and copies ran while one was open for 2% -> 3% of each run, Pallas kernels for 29% -> 28%
where the time goes in v8:
time: 138 us; the launch traced here: 137 us
  Pallas kernels  41.2 us (30%)
  starting transfers between devices  41.2 us (30%)
  waiting for transfers between devices  27.6 us (20%)
  local copies, waits for them, and re-layouts  19.4 us (14%)
  other arithmetic  5.89 us (4%)
  between operations  1.57 us (1%)
    all_to_all x3, starting transfers between devices, exchange(): lax.all_to_all(array, 'tp' if axis == 'y' else 'ctx', 0, 0, axis_index_gr...  17.4 us
    ppermute x3, waiting for transfers between devices, along_x(): return lax.ppermute(array, 'ctx', pairs)  16.3 us
    unnamed x66, local copies, waits for them, and re-layouts  16.2 us
    ppermute x7, starting transfers between devices, along_y(): return lax.ppermute(array, 'tp', pairs)  12.2 us
    ppermute x2, waiting for transfers between devices, neighbour(): lax.ppermute(array, 'ctx', [(i, i + by) for i in range(count) if 0 <= i +...  8.65 us
    ppermute x2, starting transfers between devices, neighbour(): lax.ppermute(array, 'ctx', [(i, i + by) for i in range(count) if 0 <= i +...  7.49 us
    pallas_call x1, Pallas kernels, run_forward(): pl.pallas_call(forward_kernel, grid=(CH // LANES,), in_specs=[SMEM, lane_...  6.68 us
    pallas_call x1, Pallas kernels, run_backward(): pl.pallas_call(backward_kernel, grid=(CH // LANES,), in_specs=[SMEM, lane...  6.6 us
  transfers between devices with their start and end apart: 18, of which 5 were waited for; matrix products, arithmetic and copies ran while one was open for 3% of the time, Pallas kernels for 28%

profile of v8, /device:TPU:102, one launch (start us, length us, event | category | flops | bytes accessed | tf_op | source)
XLA Modules:
  0.0 136.8 jit_solution(4706749282804219177)
XLA Ops:
  1.9 2.3 %prepare.1 = (bf16[304,512]{1,0:T(8,128)(2,1)}, bf16[4,512,128]{2,1,0:T(8,128)(2,1)}) custom-call(s32[4]{0:T(128)} %pad_add_fusion.info_ref.valid_ref.order_ref, bf16[3,512,512]{2,1,0:T(8,128)(2,1)} %bitcast.10, bf16[512,512]{1,0:T(8,128)(2,1)} %cot_ref.1), custom_call_target="tpu_custom_call" | custom-call | flops 1000 | bytes 1000 | tf_op jit(solution)/shard_map/prepare/pallas_call | solution.py:437
  4.2 4.8 %all-to-all-start = ((bf16[4,512,128]{2,1,0:T(8,128)(2,1)}), bf16[4,512,128]{2,1,0:T(8,128)(2,1)S(1)}, u32[]{:S(2)}, u32[]{:S(2)}) async-start(bf16[4,512,128]{2,1,0:T(8,128)(2,1)} %get-tuple-element.35), calls=%async_computation | async-start | bytes 1048576 | tf_op jit(solution)/shard_map/all_to_all | solution.py:525
  8.9 4.5 %collective-permute-start = (bf16[304,512]{1,0:T(8,128)(2,1)}, bf16[304,512]{1,0:T(8,128)(2,1)S(1)}, u32[]{:S(2)}, u32[]{:S(2)}) collective-permute-start(bf16[304,512]{1,0:T(8,128)(2,1)} %get-tuple-element.36.refs_0_), channel_id=1, source_target_pairs={{0,8},{8,16},{16,24},{24,32},{32,40},{40,48},{48,56},{56,64},{64,7... | collective-permute-start | bytes 933896 | tf_op jit(solution)/shard_map/ppermute | solution.py:554
  13.4 6.7 %forward.1 = (bf16[512,512]{1,0:T(8,128)(2,1)}, bf16[512,512]{1,0:T(8,128)(2,1)}, f32[512,512]{1,0:T(8,128)}, bf16[512,512]{1,0:T(8,128)(2,1)}, bf16[512,512]{1,...) custom-call(s32[4]{0:T(128)} %pad_add_fusion.info_ref.valid_ref.order_ref, ...), custom_call_target="tpu_custom_call" | custom-call | flops 1000 | bytes 1000 | tf_op jit(solution)/shard_map/forward/pallas_call | solution.py:262
  20.1 2.3 %collective-permute-done.halo_ref = bf16[304,512]{1,0:T(8,128)(2,1)S(1)} collective-permute-done((bf16[304,512]{1,0:T(8,128)(2,1)}, bf16[304,512]{1,0:T(8,128)(2,1)S(1)}, u32[]{:S(2)}, u32[]{:S(2)}) %collective-permute-start) | collective-permute-done | bytes 311328 | tf_op jit(solution)/shard_map/ppermute | solution.py:554
  24.2 4.5 %all-to-all-start.1 = ((bf16[4,4,512,128]{3,2,1,0:T(8,128)(2,1)}), bf16[4,4,512,128]{3,2,1,0:T(8,128)(2,1)S(1)}, u32[]{:S(2)}, u32[]{:S(2)}) async-start(bf16[4,4,512,128]{3,2,1,0:T(8,128)(2,1)} %broadcast_in_dim.2.refs_3_), calls=%async_computation.1 | async-start | bytes 4194304 | tf_op jit(solution)/shard_map/all_to_all | solution.py:525
  28.6 5.7 %finish.1 = (bf16[512,512]{1,0:T(8,128)(2,1)}, bf16[512,512]{1,0:T(8,128)(2,1)}, f32[512,512]{1,0:T(8,128)}, bf16[512,512]{1,0:T(8,128)(2,1)}, bf16[512,512]{1,0:T(8,128)(2,1)}, /*index=5*/bf16[512,512]{1,0:T(8,128)(2,1)}) custom-call(s32[4]{0:T(128)} %pad_add_fusion.info_ref.valid_ref.orde, ...), custom_call_target="tpu_custom_call", output_to_operand_aliasing={{2}: (7, {}), {3}: (8, {}), {4}: (9, {}), {0}: (11, {}), {1... | custom-call | flops 1000 | bytes 1000 | tf_op jit(solution)/shard_map/finish/pallas_call | solution.py:282
  34.4 2.5 %collective-permute-start.2 = (bf16[512,512]{1,0:T(8,128)(2,1)}, bf16[512,512]{1,0:T(8,128)(2,1)S(1)}, u32[]{:S(2)}, u32[]{:S(2)}) collective-permute-start(bf16[512,512]{1,0:T(8,128)(2,1)} %get-tuple-element.47.refs_0_), channel_id=1, source_target_pairs={{0,8},{8,16},{16,24},{24,0},{32,40},{40,48},{48,56},{56,32},{64,72... | collective-permute-start | bytes 1572872 | tf_op jit(solution)/shard_map/ppermute | solution.py:536
  37.8 3.5 %collective-permute-start.1 = (bf16[512,512]{1,0:T(8,128)(2,1)}, bf16[512,512]{1,0:T(8,128)(2,1)}, u32[]{:S(2)}, u32[]{:S(2)}) collective-permute-start(bf16[512,512]{1,0:T(8,128)(2,1)} %cot_ref.1), channel_id=1, source_target_pairs={{0,4},{1,5},{2,6},{3,7},{4,0},{5,1},{6,2},{7,3},{8,12},{9,13},{10,... | collective-permute-start | bytes 1572872 | tf_op jit(solution)/shard_map/ppermute | solution.py:541
  41.3 16.3 %collective-permute-done.2.refs_0_.refs_1_ = bf16[512,512]{1,0:T(8,128)(2,1)S(1)} collective-permute-done((bf16[512,512]{1,0:T(8,128)(2,1)}, bf16[512,512]{1,0:T(8,128)(2,1)S(1)}, u32[]{:S(2)}, u32[]{:S(2)}) %collective-permute-start.2) | collective-permute-done | bytes 524320 | tf_op jit(solution)/shard_map/ppermute | solution.py:536
  58.6 2.6 %project.1 = bf16[4,512,512]{2,1,0:T(8,128)(2,1)S(1)} custom-call(s32[4]{0:T(128)S(1)} %copy-done.23, bf16[512,512]{1,0:T(8,128)(2,1)S(1)} %copy-done.3, bf16[512,4096]{1,0:T(8,128)(2,1)S(1)} %copy-done, bf16[512,512]{1,0:T(8,128)(2,1)S(1)} %collective-permute-done.2.refs_0_.refs_1_), custom_call_target="tpu_custom_call" | custom-call | flops 1000 | bytes 1000 | tf_op jit(solution)/shard_map/project/pallas_call | solution.py:358
  68.9 2.5 %collective-permute-done.5.theirs = bf16[4,4,512,128]{3,2,1,0:T(8,128)(2,1)S(1)} collective-permute-done((bf16[4,4,512,128]{3,2,1,0:T(8,128)(2,1)S(1)}, bf16[4,4,512,128]{3,2,1,0:T(8,128)(2,1)S(1)}, u32[]{:S(2)}, u32[]{:S(2)}) %collective-permute-start.5) | collective-permute-done | bytes 2097184 | tf_op jit(solution)/shard_map/ppermute | solution.py:549
  74.5 3.9 %outer.1.refs_0_ = bf16[8,512,128]{2,1,0:T(8,128)(2,1)} custom-call(s32[4]{0:T(128)S(1)} %copy-done.23, bf16[4,4,512,128]{3,2,1,0:T(8,128)(2,1)S(1)} %all-to-all-done.1.mine, bf16[4,4,512,128]{3,2,1,0:T(8,128)(2,1)S(1)} %collective-permute-done.5.theirs, bf16[512,512]{1,0:T(8,128)(2,1)S(1)} %copy-done.9, bf16[512,512]{1,0:T(8,128)(2,1)S(1)} %copy-done.11, ...), custom_call_target="tpu_custom_call" | custom-call | flops 1000 | bytes 1000 | tf_op jit(solution)/shard_map/outer/pallas_call | solution.py:468
  78.5 2.8 %project_add.1 = (bf16[512,512]{1,0:T(8,128)(2,1)S(1)}, bf16[512,512]{1,0:T(8,128)(2,1)S(1)}, bf16[256,512]{1,0:T(8,128)(2,1)S(1)}, bf16[256,512]{1,0:T(8,128)(2,1)S(1)}, f32[512,512]{1,0:T(8,128)S(1)}) custom-call(s32[4]{0:T(128)S(1)} %copy-done.23, bf16[512,512]{1,0:T(8,128)(2,1)S(1)} %copy-done.4, bf16[512,4096]{1,0:T(8,128)(2,1)S(1)} %copy-done.1, ...), custom_call_target="tpu_custom_call" | custom-call | flops 1000 | bytes 1000 | tf_op jit(solution)/shard_map/project_add/pallas_call | solution.py:405
  82.9 2.0 %pad_maximum_fusion.mine = bf16[4,512,512]{2,1,0:T(8,128)(2,1)S(1)} fusion(bf16[1,512,512]{2,1,0:T(8,128)(2,1)} %bitcast.8, bf16[1,512,512]{2,1,0:T(8,128)(2,1)S(1)} %bitcast.19, bf16[1,512,512]{2,1,0:T(8,128)(2,1)S(1)} %bitcast.18, bf16[1,512,512]{2,1,0:T(8,128)(2,1)} %bitcast.5), kind=kLoop, calls=%fused_computation | loop fusion | flops 3145728 | bytes 4194304 | tf_op jit(solution)/shard_map/stack | solution.py:586
  85.1 8.2 %all-to-all-start.2 = ((bf16[8,512,128]{2,1,0:T(8,128)(2,1)}), bf16[8,512,128]{2,1,0:T(8,128)(2,1)}, u32[]{:S(2)}, u32[]{:S(2)}) async-start(bf16[8,512,128]{2,1,0:T(8,128)(2,1)} %outer.1.refs_0_), calls=%async_computation.2 | async-start | bytes 2097152 | tf_op jit(solution)/shard_map/all_to_all | solution.py:525
  98.0 2.2 %copy-done.2 = bf16[512,4096]{1,0:T(8,128)(2,1)S(1)} copy-done((bf16[512,4096]{1,0:T(8,128)(2,1)S(1)}, bf16[512,4096]{1,0:T(8,128)(2,1)}, u32[]{:S(2)}) %copy-start.2) | copy-done | bytes 4194328
  102.3 4.1 %d_mix.1 = (bf16[512,512]{1,0:T(8,128)(2,1)S(1)}, bf16[512,512]{1,0:T(8,128)(2,1)S(1)}, bf16[192,512]{1,0:T(8,128)(2,1)S(1)}) custom-call(s32[4]{0:T(128)S(1)} %copy-done.23, bf16[512,4096]{1,0:T(8,128)(2,1)S(1)} %copy-done.2, bf16[4,512,512]{2,1,0:T(8,128)(2,1)S(1)} %pad_maximum_fusion.mine, bf16[4,512,512]{2,1,0:T(8,128)(2,1)} %collective-permute-done.9.theirs, ...), custom_call_target="tpu_custom_call" | custom-call | flops 1000 | bytes 1000 | tf_op jit(solution)/shard_map/d_mix/pallas_call | solution.py:505
  108.0 3.0 %collective-permute-start.10 = (bf16[192,512]{1,0:T(8,128)(2,1)S(1)}, bf16[192,512]{1,0:T(8,128)(2,1)S(1)}, u32[]{:S(2)}, u32[]{:S(2)}) collective-permute-start(bf16[192,512]{1,0:T(8,128)(2,1)S(1)} %get-tuple-element.58), channel_id=1, source_target_pairs={{8,0},{16,8},{24,16},{32,24},{40,32},{48,40},{56,48},{64,56},{72,6... | collective-permute-start | bytes 589832 | tf_op jit(solution)/shard_map/ppermute | solution.py:554
  111.2 1.8 %collective-permute-start.14 = (bf16[256,512]{1,0:T(8,128)(2,1)S(1)}, bf16[256,512]{1,0:T(8,128)(2,1)S(1)}, u32[]{:S(2)}, u32[]{:S(2)}) collective-permute-start(bf16[256,512]{1,0:T(8,128)(2,1)S(1)} %add_convert_fusion.2.refs_2_), channel_id=1, source_target_pairs={{0,6},{1,7},{2,0},{3,1},{4,2},{5,3},{6,4},{7,5},{8,14},{9,15},{10,... | collective-permute-start | bytes 786440 | tf_op jit(solution)/shard_map/ppermute | solution.py:541
  113.4 6.6 %backward.1.refs_0_ = bf16[3,512,512]{2,1,0:T(8,128)(2,1)} custom-call(s32[4]{0:T(128)} %pad_add_fusion.info_ref.valid_ref.order_ref, bf16[512,512]{1,0:T(8,128)(2,1)} %copy-done.6, bf16[512,512]{1,0:T(8,128)(2,1)} %copy-done.7, bf16[512,512]{1,0:T(8,128)(2,1)} %get-tuple-element.54.k_ref, bf16[512,512]{1,0:T(8,128)(2,1)} %get-tuple-element.55.v_ref, ...), custom_call_target="tpu_custom_call" | custom-call | flops 1000 | bytes 1000 | tf_op jit(solution)/shard_map/backward/pallas_call | solution.py:303
  120.1 6.3 %collective-permute-done.10.msg_ref = bf16[192,512]{1,0:T(8,128)(2,1)S(1)} collective-permute-done((bf16[192,512]{1,0:T(8,128)(2,1)S(1)}, bf16[192,512]{1,0:T(8,128)(2,1)S(1)}, u32[]{:S(2)}, u32[]{:S(2)}) %collective-permute-start.10) | collective-permute-done | bytes 196640 | tf_op jit(solution)/shard_map/ppermute | solution.py:554
  127.1 6.5 %backward_end.1 = bf16[3,512,512]{2,1,0:T(8,128)(2,1)} custom-call(s32[4]{0:T(128)} %pad_add_fusion.info_ref.valid_ref.order_ref, bf16[512,512]{1,0:T(8,128)(2,1)} %copy-done.6, bf16[192,512]{1,0:T(8,128)(2,1)} %copy-done.32, bf16[512,512]{1,0:T(8,128)(2,1)} %copy-done.7, bf16[512,512]{1,0:T(8,128)(2,1)} %get-tuple-element.54.k_ref, ...), custom_call_target="tpu_custom_call", output_to_operand_aliasing={{}: (10, {})} | custom-call | flops 1000 | bytes 1000 | tf_op jit(solution)/shard_map/backward_end/pallas_call | solution.py:322
  133.6 2.1 %convert_reduce_fusion = f32[512,128]{1,0:T(8,128)} fusion(bf16[8,512,128]{2,1,0:T(8,128)(2,1)} %all-to-all-done.2), kind=kLoop, calls=%fused_computation.1 | loop fusion | flops 983040 | bytes 1310720 | tf_op jit(solution)/shard_map/reduce_sum | solution.py:603
  (97 shorter events, 27.7 us)
Async XLA Ops:
  4.2 18.3 %all-to-all-start = ((bf16[4,512,128]{2,1,0:T(8,128)(2,1)}), bf16[4,512,128]{2,1,0:T(8,128)(2,1)S(1)}, u32[]{:S(2)}, u32[]{:S(2)}) async-start(bf16[4,512,128]{2,1,0:T(8,128)(2,1)} %get-tuple-element.35), calls=%async_computation | async-start | bytes 1048576 | tf_op jit(solution)/shard_map/all_to_all | solution.py:525
  8.9 13.5 %collective-permute-start = (bf16[304,512]{1,0:T(8,128)(2,1)}, bf16[304,512]{1,0:T(8,128)(2,1)S(1)}, u32[]{:S(2)}, u32[]{:S(2)}) collective-permute-start(bf16[304,512]{1,0:T(8,128)(2,1)} %get-tuple-element.36.refs_0_), channel_id=1, source_target_pairs={{0,8},{8,16},{16,24},{24,32},{32,40},{40,48},{48,56},{56,64},{64,7... | collective-permute-start | bytes 933896 | tf_op jit(solution)/shard_map/ppermute | solution.py:554
  24.2 40.9 %all-to-all-start.1 = ((bf16[4,4,512,128]{3,2,1,0:T(8,128)(2,1)}), bf16[4,4,512,128]{3,2,1,0:T(8,128)(2,1)S(1)}, u32[]{:S(2)}, u32[]{:S(2)}) async-start(bf16[4,4,512,128]{3,2,1,0:T(8,128)(2,1)} %broadcast_in_dim.2.refs_3_), calls=%async_computation.1 | async-start | bytes 4194304 | tf_op jit(solution)/shard_map/all_to_all | solution.py:525
  28.6 28.9 %copy-start = (bf16[512,4096]{1,0:T(8,128)(2,1)S(1)}, bf16[512,4096]{1,0:T(8,128)(2,1)}, u32[]{:S(2)}) copy-start(bf16[512,4096]{1,0:T(8,128)(2,1)} %weight_ref.5) | copy-start | bytes 12582916
  28.6 28.9 %copy-start.23 = (s32[4]{0:T(128)S(1)}, s32[4]{0:T(128)}, u32[]{:S(2)}) copy-start(s32[4]{0:T(128)} %pad_add_fusion.info_ref.valid_ref.order_ref) | copy-start | bytes 52
  34.4 23.2 %collective-permute-start.2 = (bf16[512,512]{1,0:T(8,128)(2,1)}, bf16[512,512]{1,0:T(8,128)(2,1)S(1)}, u32[]{:S(2)}, u32[]{:S(2)}) collective-permute-start(bf16[512,512]{1,0:T(8,128)(2,1)} %get-tuple-element.47.refs_0_), channel_id=1, source_target_pairs={{0,8},{8,16},{16,24},{24,0},{32,40},{40,48},{48,56},{56,32},{64,72... | collective-permute-start | bytes 1572872 | tf_op jit(solution)/shard_map/ppermute | solution.py:536
  36.8 26.5 %collective-permute-start.3 = (bf16[512,512]{1,0:T(8,128)(2,1)}, bf16[512,512]{1,0:T(8,128)(2,1)S(1)}, u32[]{:S(2)}, u32[]{:S(2)}) collective-permute-start(bf16[512,512]{1,0:T(8,128)(2,1)} %get-tuple-element.47.refs_0_), channel_id=1, source_target_pairs={{0,16},{8,24},{16,0},{24,8},{32,48},{40,56},{48,32},{56,40},{64,80... | collective-permute-start | bytes 1572872 | tf_op jit(solution)/shard_map/ppermute | solution.py:536
  37.1 27.1 %collective-permute-start.4 = (bf16[512,512]{1,0:T(8,128)(2,1)}, bf16[512,512]{1,0:T(8,128)(2,1)S(1)}, u32[]{:S(2)}, u32[]{:S(2)}) collective-permute-start(bf16[512,512]{1,0:T(8,128)(2,1)} %get-tuple-element.47.refs_0_), channel_id=1, source_target_pairs={{0,24},{8,0},{16,8},{24,16},{32,56},{40,32},{48,40},{56,48},{64,88... | collective-permute-start | bytes 1572872 | tf_op jit(solution)/shard_map/ppermute | solution.py:536
  37.8 27.4 %collective-permute-start.1 = (bf16[512,512]{1,0:T(8,128)(2,1)}, bf16[512,512]{1,0:T(8,128)(2,1)}, u32[]{:S(2)}, u32[]{:S(2)}) collective-permute-start(bf16[512,512]{1,0:T(8,128)(2,1)} %cot_ref.1), channel_id=1, source_target_pairs={{0,4},{1,5},{2,6},{3,7},{4,0},{5,1},{6,2},{7,3},{8,12},{9,13},{10,... | collective-permute-start | bytes 1572872 | tf_op jit(solution)/shard_map/ppermute | solution.py:541
  63.4 15.1 %copy-start.4 = (bf16[512,512]{1,0:T(8,128)(2,1)S(1)}, bf16[512,512]{1,0:T(8,128)(2,1)}, u32[]{:S(2)}) copy-start(bf16[512,512]{1,0:T(8,128)(2,1)} %get-tuple-element.46.mix_ref) | copy-start | bytes 1572868
  65.1 6.2 %collective-permute-start.5 = (bf16[4,4,512,128]{3,2,1,0:T(8,128)(2,1)S(1)}, bf16[4,4,512,128]{3,2,1,0:T(8,128)(2,1)S(1)}, u32[]{:S(2)}, u32[]{:S(2)}) collective-permute-start(bf16[4,4,512,128]{3,2,1,0:T(8,128)(2,1)S(1)} %all-to-all-done.1.mine), channel_id=1, source_target_pairs={{0,1},{1,0},{2,3},{3,2},{4,5},{5,4},{6,7},{7,6},{8,9},{9,8},{10,11... | collective-permute-start | bytes 6291464 | tf_op jit(solution)/shard_map/ppermute | solution.py:549
  65.1 13.3 %collective-permute-start.6 = (bf16[4,512,512]{2,1,0:T(8,128)(2,1)}, bf16[4,512,512]{2,1,0:T(8,128)(2,1)S(1)}, u32[]{:S(2)}, u32[]{:S(2)}) collective-permute-start(bf16[4,512,512]{2,1,0:T(8,128)(2,1)} %copy-done.8), channel_id=1, source_target_pairs={{0,1},{1,0},{2,3},{3,2},{4,5},{5,4},{6,7},{7,6},{8,9},{9,8},{10,11... | collective-permute-start | bytes 6291464 | tf_op jit(solution)/shard_map/ppermute | solution.py:549
  65.6 17.2 %collective-permute-start.7 = (bf16[512,512]{1,0:T(8,128)(2,1)}, bf16[512,512]{1,0:T(8,128)(2,1)S(1)}, u32[]{:S(2)}, u32[]{:S(2)}) collective-permute-start(bf16[512,512]{1,0:T(8,128)(2,1)} %cot_ref.1), channel_id=1, source_target_pairs={{0,2},{1,3},{2,4},{3,5},{4,6},{5,7},{6,0},{7,1},{8,10},{9,11},{10,... | collective-permute-start | bytes 1572872 | tf_op jit(solution)/shard_map/ppermute | solution.py:541
  67.4 15.5 %collective-permute-start.8 = (bf16[512,512]{1,0:T(8,128)(2,1)}, bf16[512,512]{1,0:T(8,128)(2,1)S(1)}, u32[]{:S(2)}, u32[]{:S(2)}) collective-permute-start(bf16[512,512]{1,0:T(8,128)(2,1)} %cot_ref.1), channel_id=1, source_target_pairs={{0,6},{1,7},{2,0},{3,1},{4,2},{5,3},{6,4},{7,5},{8,14},{9,15},{10,... | collective-permute-start | bytes 1572872 | tf_op jit(solution)/shard_map/ppermute | solution.py:541
  84.9 13.1 %collective-permute-start.9 = (bf16[4,512,512]{2,1,0:T(8,128)(2,1)S(1)}, bf16[4,512,512]{2,1,0:T(8,128)(2,1)}, u32[]{:S(2)}, u32[]{:S(2)}) collective-permute-start(bf16[4,512,512]{2,1,0:T(8,128)(2,1)S(1)} %pad_maximum_fusion.mine), channel_id=1, source_target_pairs={{0,1},{1,0},{2,3},{3,2},{4,5},{5,4},{6,7},{7,6},{8,9},{9,8},{10,11... | collective-permute-start | bytes 6291464 | tf_op jit(solution)/shard_map/ppermute | solution.py:549
  85.1 48.4 %all-to-all-start.2 = ((bf16[8,512,128]{2,1,0:T(8,128)(2,1)}), bf16[8,512,128]{2,1,0:T(8,128)(2,1)}, u32[]{:S(2)}, u32[]{:S(2)}) async-start(bf16[8,512,128]{2,1,0:T(8,128)(2,1)} %outer.1.refs_0_), calls=%async_computation.2 | async-start | bytes 2097152 | tf_op jit(solution)/shard_map/all_to_all | solution.py:525
  93.3 17.7 %collective-permute-start.11 = (bf16[512,512]{1,0:T(8,128)(2,1)}, bf16[512,512]{1,0:T(8,128)(2,1)S(1)}, u32[]{:S(2)}, u32[]{:S(2)}) collective-permute-start(bf16[512,512]{1,0:T(8,128)(2,1)} %copy-done.19), channel_id=1, source_target_pairs={{0,2},{1,3},{2,4},{3,5},{4,6},{5,7},{6,0},{7,1},{8,10},{9,11},{10,... | collective-permute-start | bytes 1572872 | tf_op jit(solution)/shard_map/ppermute | solution.py:541
  95.0 16.0 %collective-permute-start.12 = (bf16[512,512]{1,0:T(8,128)(2,1)}, bf16[512,512]{1,0:T(8,128)(2,1)S(1)}, u32[]{:S(2)}, u32[]{:S(2)}) collective-permute-start(bf16[512,512]{1,0:T(8,128)(2,1)} %copy-done.24), channel_id=1, source_target_pairs={{0,6},{1,7},{2,0},{3,1},{4,2},{5,3},{6,4},{7,5},{8,14},{9,15},{10,... | collective-permute-start | bytes 1572872 | tf_op jit(solution)/shard_map/ppermute | solution.py:541
  108.0 18.4 %collective-permute-start.10 = (bf16[192,512]{1,0:T(8,128)(2,1)S(1)}, bf16[192,512]{1,0:T(8,128)(2,1)S(1)}, u32[]{:S(2)}, u32[]{:S(2)}) collective-permute-start(bf16[192,512]{1,0:T(8,128)(2,1)S(1)} %get-tuple-element.58), channel_id=1, source_target_pairs={{8,0},{16,8},{24,16},{32,24},{40,32},{48,40},{56,48},{64,56},{72,6... | collective-permute-start | bytes 589832 | tf_op jit(solution)/shard_map/ppermute | solution.py:554
  111.2 24.5 %collective-permute-start.14 = (bf16[256,512]{1,0:T(8,128)(2,1)S(1)}, bf16[256,512]{1,0:T(8,128)(2,1)S(1)}, u32[]{:S(2)}, u32[]{:S(2)}) collective-permute-start(bf16[256,512]{1,0:T(8,128)(2,1)S(1)} %add_convert_fusion.2.refs_2_), channel_id=1, source_target_pairs={{0,6},{1,7},{2,0},{3,1},{4,2},{5,3},{6,4},{7,5},{8,14},{9,15},{10,... | collective-permute-start | bytes 786440 | tf_op jit(solution)/shard_map/ppermute | solution.py:541
  113.0 22.7 %collective-permute-start.13 = (bf16[256,512]{1,0:T(8,128)(2,1)S(1)}, bf16[256,512]{1,0:T(8,128)(2,1)S(1)}, u32[]{:S(2)}, u32[]{:S(2)}) collective-permute-start(bf16[256,512]{1,0:T(8,128)(2,1)S(1)} %add_convert_fusion.3.refs_1_), channel_id=1, source_target_pairs={{0,2},{1,3},{2,4},{3,5},{4,6},{5,7},{6,0},{7,1},{8,10},{9,11},{10,... | collective-permute-start | bytes 786440 | tf_op jit(solution)/shard_map/ppermute | solution.py:541
  120.0 15.6 %copy-start.14 = (f32[512,512]{1,0:T(8,128)S(1)}, f32[512,512]{1,0:T(8,128)}, u32[]{:S(2)}) copy-start(f32[512,512]{1,0:T(8,128)} %copy-done.13) | copy-start | bytes 3145732
  120.0 15.6 %copy-start.28 = (bf16[512,512]{1,0:T(8,128)(2,1)S(1)}, bf16[512,512]{1,0:T(8,128)(2,1)}, u32[]{:S(2)}) copy-start(bf16[512,512]{1,0:T(8,128)(2,1)} %copy-done.27) | copy-start | bytes 1572868
  120.1 15.6 %copy-start.30 = (bf16[512,512]{1,0:T(8,128)(2,1)S(1)}, bf16[512,512]{1,0:T(8,128)(2,1)}, u32[]{:S(2)}) copy-start(bf16[512,512]{1,0:T(8,128)(2,1)} %copy-done.29) | copy-start | bytes 1572868
  (27 other events, 96.6 us)
